TPU v7x, 32 devices: a whole 2x2x4 slice. The times are simulated.
32 devices in a mesh: dp: 8 (over z, x), ffn: 4 (over y, core).
Axes of the slice: x: 2, y: 2, z: 4, core: 2. Of those that a mesh axis runs over, the one named last changes fastest.
Arguments:
- inputs: bfloat16 [4, 32, 512, 768], P(None, ('dp', 'ffn')), may hold values from -6 to 6
- doc_ids: int32 [4, 32, 512], P(None, ('dp', 'ffn')), may hold values from 0 to 3, never falling along the last dimension, each value on 1 to 192 neighbouring positions
- cotangent: bfloat16 [4, 32, 512, 768], P(None, ('dp', 'ffn')), may hold values from -6 to 6
- query_weight: bfloat16 [4, 192, 192], replicated, may hold values from -0.875 to 0.875
- query_bias: bfloat16 [768], replicated, may hold values from -3 to 3
- key_weight: bfloat16 [4, 192, 192], replicated, may hold values from -0.4375 to 0.4375
- value_weight: bfloat16 [4, 192, 192], replicated, may hold values from -0.4375 to 0.4375
- value_bias: bfloat16 [768], replicated, may hold values from -3 to 3
- out_weight: bfloat16 [768, 768], replicated, may hold values from -0.875 to 0.875
- out_bias: bfloat16 [768], replicated, may hold values from -3 to 3
- mixed_gain: float32 [768], replicated, may hold values from 0.5 to 1.5
- mixed_bias: float32 [768], replicated, may hold values from -2 to 2
- expand_weight: bfloat16 [4, 192, 768], P(None, None, 'ffn'), may hold values from -0.4375 to 0.4375
- expand_bias: bfloat16 [4, 768], P(None, 'ffn'), may hold values from -3 to 3
- shrink_weight: bfloat16 [4, 768, 192], P(None, 'ffn'), may hold values from -0.21875 to 0.21875
- shrink_bias: bfloat16 [768], replicated, may hold values from -3 to 3
- final_gain: float32 [768], replicated, may hold values from 0.5 to 1.5
- final_bias: float32 [768], replicated, may hold values from -2 to 2
Outputs:
- result: bfloat16 [4, 32, 512, 768], P(None, ('dp', 'ffn'))
- input_grad: bfloat16 [4, 32, 512, 768], P(None, ('dp', 'ffn'))
- grad_query_weight: float32 [4, 192, 192], replicated
- grad_query_bias: float32 [768], replicated
- grad_key_weight: float32 [4, 192, 192], replicated
- grad_value_weight: float32 [4, 192, 192], replicated
- grad_value_bias: float32 [768], replicated
- grad_out_weight: float32 [768, 768], replicated
- grad_out_bias: float32 [768], replicated
- grad_mixed_gain: float32 [768], replicated
- grad_mixed_bias: float32 [768], replicated
- grad_expand_weight: float32 [4, 192, 768], P(None, None, 'ffn')
- grad_expand_bias: float32 [4, 768], P(None, 'ffn')
- grad_shrink_weight: float32 [4, 768, 192], P(None, 'ffn')
- grad_shrink_bias: float32 [768], replicated
- grad_final_gain: float32 [768], replicated
- grad_final_bias: float32 [768], replicated
Inputs may be any that keep to these rules, and one draw needn't show every extreme that they name: `doc_ids`: within each batch row the document numbers never fall; each row has 4 documents, each of 1 to 192 tokens, one of exactly that many.
All inputs are finite; a program needn't handle non-finite values.
Results may differ from a plain program's by a relative error of at most 0.015.
The roundings to bfloat16 on the way count: a program that leaves them out, or rounds other values in their place, can miss the bound.
Values may be sent and summed in bfloat16 or wider, within the bound.
No kernel may reach another device: no remote copies, remote signals or barrier semaphores. Data moves between devices by JAX's collectives and lax.ppermute only.
A program may use at most 384 MiB of HBM per device.

v0:
```python
import jax
import jax.numpy as jnp
from jax import lax
from jax.sharding import PartitionSpec as P

HEADS = 12


epsilon = 1e-05
masked_score = -1e30


def layer_norm(value, gain, offset):
    centered = value - jnp.mean(value, axis=-1, keepdims=True)
    variance = jnp.mean(centered * centered, axis=-1, keepdims=True)
    return centered * lax.rsqrt(variance + epsilon) * gain + offset


def exact_gelu(value):
    return jax.nn.gelu(value, approximate=False)


def grouped(inputs, weight):
    groups, width_in, width_out = weight.shape
    parted = inputs.reshape(inputs.shape[0], groups, width_in)
    result = jnp.einsum("tgi,gio->tgo", parted, weight, preferred_element_type=jnp.float32)
    return result.reshape(inputs.shape[0], groups * width_out)


def grouped_back(upstream, weight):
    groups, width_in, width_out = weight.shape
    parted = upstream.reshape(upstream.shape[0], groups, width_out)
    result = jnp.einsum("tgo,gio->tgi", parted, weight, preferred_element_type=jnp.float32)
    return result.reshape(upstream.shape[0], groups * width_in)


def grouped_grad(inputs, upstream, groups):
    count = inputs.shape[0]
    return jnp.einsum(
        "tgi,tgo->gio",
        inputs.reshape(count, groups, -1),
        upstream.reshape(count, groups, -1),
        preferred_element_type=jnp.float32,
    )


def row_scores(query, keys, docs):
    scale = query.shape[-1] ** (-0.5)
    scores = jnp.einsum("qhd,khd->hqk", query, keys, preferred_element_type=jnp.float32) * scale
    same = docs[:, None] == docs[None, :]
    return jnp.where(same[None], scores, masked_score)


def attend_row(inputs):
    query, keys, values, docs = inputs
    scores = row_scores(query, keys, docs)
    top = jnp.max(scores, axis=-1, keepdims=True)
    totals = jnp.sum(jnp.exp(scores - top), axis=-1, keepdims=True)
    log_total = top + jnp.log(totals)
    probs = jnp.exp(scores - log_total).astype(jnp.bfloat16)
    context = jnp.einsum("hqk,khd->qhd", probs, values, preferred_element_type=jnp.float32)
    return (context, log_total)


def attend_back(inputs):
    query, keys, values, docs, log_total, upstream = inputs
    scale = query.shape[-1] ** (-0.5)
    probs = jnp.exp(row_scores(query, keys, docs) - log_total)
    grad_values = jnp.einsum(
        "hqk,qhd->khd", probs.astype(jnp.bfloat16), upstream, preferred_element_type=jnp.float32
    )
    grad_probs = jnp.einsum("qhd,khd->hqk", upstream, values, preferred_element_type=jnp.float32)
    grad_scores = probs * (grad_probs - jnp.sum(probs * grad_probs, axis=-1, keepdims=True))
    grad_scores = grad_scores.astype(jnp.bfloat16)
    grad_query = (
        jnp.einsum("hqk,khd->qhd", grad_scores, keys, preferred_element_type=jnp.float32) * scale
    )
    grad_keys = (
        jnp.einsum("hqk,qhd->khd", grad_scores, query, preferred_element_type=jnp.float32) * scale
    )
    return (grad_query, grad_keys, grad_values)


def zeros_like_float(value):
    return jnp.zeros(value.shape, jnp.float32)


def on_device(
    inputs,
    doc_ids,
    cotangent,
    query_weight,
    query_bias,
    key_weight,
    value_weight,
    value_bias,
    out_weight,
    out_bias,
    mixed_gain,
    mixed_bias,
    expand_weight,
    expand_bias,
    shrink_weight,
    shrink_bias,
    final_gain,
    final_bias,
):
    micro, rows_dev, length, width = inputs.shape
    heads = HEADS
    head_size = width // heads
    tokens_dev = rows_dev * length
    groups = query_weight.shape[0]
    shape = (rows_dev, length, heads, head_size)
    expand_full, expand_row, shrink_full = (expand_weight, expand_bias, shrink_weight)
    acc_query = zeros_like_float(query_weight)
    acc_query_bias = zeros_like_float(query_bias)
    acc_key = zeros_like_float(key_weight)
    acc_value = zeros_like_float(value_weight)
    acc_value_bias = zeros_like_float(value_bias)
    acc_out = zeros_like_float(out_weight)
    acc_out_bias = zeros_like_float(out_bias)
    acc_mixed_gain = zeros_like_float(mixed_gain)
    acc_mixed_bias = zeros_like_float(mixed_bias)
    acc_expand = zeros_like_float(expand_full)
    acc_expand_bias = zeros_like_float(expand_row)
    acc_shrink = zeros_like_float(shrink_full)
    acc_shrink_bias = zeros_like_float(shrink_bias)
    acc_final_gain = zeros_like_float(final_gain)
    acc_final_bias = zeros_like_float(final_bias)
    results = []
    input_grads = []
    for index in range(micro):
        tokens = inputs[index].reshape(tokens_dev, width)
        docs = doc_ids[index]
        query = (grouped(tokens, query_weight) + query_bias).astype(jnp.bfloat16)
        keys = grouped(tokens, key_weight).astype(jnp.bfloat16)
        values = (grouped(tokens, value_weight) + value_bias).astype(jnp.bfloat16)
        query_rows = query.reshape(shape)
        key_rows = keys.reshape(shape)
        value_rows = values.reshape(shape)
        context, log_total = lax.map(attend_row, (query_rows, key_rows, value_rows, docs))
        context_low = context.reshape(tokens_dev, width).astype(jnp.bfloat16)
        hidden_one = (
            tokens.astype(jnp.float32)
            + jnp.dot(context_low, out_weight, preferred_element_type=jnp.float32)
            + out_bias
        )
        normed, mixed_back = jax.vjp(layer_norm, hidden_one, mixed_gain, mixed_bias)
        normed_low = normed.astype(jnp.bfloat16)
        gathered = lax.all_gather(normed_low, "ffn", axis=0, tiled=True)
        pre_active = grouped(gathered, expand_full) + expand_row.reshape(-1)
        active, gelu_back = jax.vjp(exact_gelu, pre_active)
        active = active.astype(jnp.bfloat16)
        ffn_out = lax.psum_scatter(
            grouped(active, shrink_full), "ffn", scatter_dimension=0, tiled=True
        )
        hidden_two = normed + ffn_out + shrink_bias
        result, final_back = jax.vjp(layer_norm, hidden_two, final_gain, final_bias)
        results.append(result.astype(jnp.bfloat16).reshape(rows_dev, length, width))
        upstream = cotangent[index].reshape(tokens_dev, width).astype(jnp.float32)
        grad_two, grad_fgain, grad_fbias = final_back(upstream)
        acc_final_gain = acc_final_gain + grad_fgain
        acc_final_bias = acc_final_bias + grad_fbias
        acc_shrink_bias = acc_shrink_bias + jnp.sum(grad_two, axis=0)
        grad_two_low = grad_two.astype(jnp.bfloat16)
        grad_gathered = lax.all_gather(grad_two_low, "ffn", axis=0, tiled=True)
        grad_active = grouped_back(grad_gathered, shrink_full)
        (grad_pre,) = gelu_back(grad_active)
        grad_pre_low = grad_pre.astype(jnp.bfloat16)
        acc_shrink = acc_shrink + grouped_grad(active, grad_gathered, groups)
        acc_expand = acc_expand + grouped_grad(gathered, grad_pre_low, groups)
        acc_expand_bias = acc_expand_bias + jnp.sum(
            grad_pre_low.astype(jnp.float32), axis=0
        ).reshape(expand_row.shape)
        grad_normed_ffn = lax.psum_scatter(
            grouped_back(grad_pre_low, expand_full), "ffn", scatter_dimension=0, tiled=True
        )
        grad_one, grad_mgain, grad_mbias = mixed_back(grad_two + grad_normed_ffn)
        acc_mixed_gain = acc_mixed_gain + grad_mgain
        acc_mixed_bias = acc_mixed_bias + grad_mbias
        acc_out_bias = acc_out_bias + jnp.sum(grad_one, axis=0)
        grad_one_low = grad_one.astype(jnp.bfloat16)
        acc_out = acc_out + jnp.einsum(
            "td,te->de", context_low, grad_one_low, preferred_element_type=jnp.float32
        )
        grad_context = jnp.einsum(
            "te,de->td", grad_one_low, out_weight, preferred_element_type=jnp.float32
        )
        grad_context = grad_context.astype(jnp.bfloat16).reshape(shape)
        grad_query, grad_keys, grad_values = lax.map(
            attend_back, (query_rows, key_rows, value_rows, docs, log_total, grad_context)
        )
        grad_query = grad_query.reshape(tokens_dev, width).astype(jnp.bfloat16)
        grad_keys = grad_keys.reshape(tokens_dev, width).astype(jnp.bfloat16)
        grad_values = grad_values.reshape(tokens_dev, width).astype(jnp.bfloat16)
        acc_query = acc_query + grouped_grad(tokens, grad_query, groups)
        acc_key = acc_key + grouped_grad(tokens, grad_keys, groups)
        acc_value = acc_value + grouped_grad(tokens, grad_values, groups)
        acc_query_bias = acc_query_bias + jnp.sum(grad_query.astype(jnp.float32), axis=0)
        acc_value_bias = acc_value_bias + jnp.sum(grad_values.astype(jnp.float32), axis=0)
        grad_tokens = (
            grad_one
            + grouped_back(grad_query, query_weight)
            + grouped_back(grad_keys, key_weight)
            + grouped_back(grad_values, value_weight)
        )
        input_grads.append(grad_tokens.astype(jnp.bfloat16).reshape(rows_dev, length, width))
    (
        acc_query,
        acc_query_bias,
        acc_key,
        acc_value,
        acc_value_bias,
        acc_out,
        acc_out_bias,
        acc_mixed_gain,
        acc_mixed_bias,
        acc_shrink_bias,
        acc_final_gain,
        acc_final_bias,
    ) = lax.psum(
        (
            acc_query,
            acc_query_bias,
            acc_key,
            acc_value,
            acc_value_bias,
            acc_out,
            acc_out_bias,
            acc_mixed_gain,
            acc_mixed_bias,
            acc_shrink_bias,
            acc_final_gain,
            acc_final_bias,
        ),
        ("dp", "ffn"),
    )
    acc_expand, acc_expand_bias, acc_shrink = (
        lax.psum(acc_expand.astype(jnp.bfloat16), "dp").astype(jnp.float32),
        lax.psum(acc_expand_bias.astype(jnp.bfloat16), "dp").astype(jnp.float32),
        lax.psum(acc_shrink.astype(jnp.bfloat16), "dp").astype(jnp.float32),
    )
    return (
        jnp.stack(results),
        jnp.stack(input_grads),
        acc_query,
        acc_query_bias,
        acc_key,
        acc_value,
        acc_value_bias,
        acc_out,
        acc_out_bias,
        acc_mixed_gain,
        acc_mixed_bias,
        acc_expand,
        acc_expand_bias,
        acc_shrink,
        acc_shrink_bias,
        acc_final_gain,
        acc_final_bias,
    )


def solution(mesh):
    in_specs = (
        P(None, ("dp", "ffn"), None, None),
        P(None, ("dp", "ffn"), None),
        P(None, ("dp", "ffn"), None, None),
        P(),
        P(),
        P(),
        P(),
        P(),
        P(),
        P(),
        P(),
        P(),
        P(None, None, "ffn"),
        P(None, "ffn"),
        P(None, "ffn", None),
        P(),
        P(),
        P(),
    )
    out_specs = (
        P(None, ("dp", "ffn"), None, None),
        P(None, ("dp", "ffn"), None, None),
        P(),
        P(),
        P(),
        P(),
        P(),
        P(),
        P(),
        P(),
        P(),
        P(None, None, "ffn"),
        P(None, "ffn"),
        P(None, "ffn", None),
        P(),
        P(),
        P(),
    )
    return jax.shard_map(
        on_device, mesh=mesh, in_specs=in_specs, out_specs=out_specs, check_vma=False
    )
```

profile of v0, /device:TPU:0, one launch (start us, length us, event | category | flops | bytes accessed | tf_op | source)
XLA Modules:
  0.0 1439.7 jit_solution(15943469173032978848)
XLA Ops:
  38.1 7.8 convolution_convert_fusion.12
  56.6 12.8 convolution_convert_fusion.14
  78.9 4.9 convolution_convert_fusion.10
  91.3 29.8 %all-gather.11.cloned.1.call-done = bf16[2048,768]{1,0:T(8,128)(2,1)} async-done(((bf16[512,768]{1,0:T(8,128)(2,1)}), bf16[2048,768]{1,0:T(8,128)(2,1)}) %all-gather.11.cloned.1.call-update) | async-done | bytes 3145744 | tf_op jit(solution)/shard_map/all_gather | solution.py:150
  121.2 5.0 copy.151
  126.2 25.1 %all-gather.13.cloned.1.call-done = bf16[2048,768]{1,0:T(8,128)(2,1)} async-done(((bf16[512,768]{1,0:T(8,128)(2,1)}), bf16[2048,768]{1,0:T(8,128)(2,1)}) %all-gather.13.cloned.1.call-update) | async-done | bytes 3145744 | tf_op jit(solution)/shard_map/all_gather | solution.py:150
  155.9 5.9 fusion.211
  165.6 16.4 %all-gather.9.cloned.1.call-done = bf16[2048,768]{1,0:T(8,128)(2,1)} async-done(((bf16[512,768]{1,0:T(8,128)(2,1)}), bf16[2048,768]{1,0:T(8,128)(2,1)}) %all-gather.9.cloned.1.call-update) | async-done | bytes 3145744 | tf_op jit(solution)/shard_map/all_gather | solution.py:150
  186.7 48.0 %fusion.47 = (bf16[2048,4,192]{0,2,1:T(8,128)(2,1)}, f32[2048,4,192]{0,2,1:T(8,128)}, bf16[2048,4,192]{0,2,1:T(8,128)(2,1)}, f32[2048,4,192]{0,2,1:T(8,128)}, bf...) fusion(f32[4,192]{1,0:T(4,128)S(1)} %convert_element_type.557, ...), kind=kOutput, calls=%fused_computation.99 | convolution fusion | flops 915406848 | bytes 50629632 | tf_op jit(solution)/shard_map/tgi,gio->tgo/dot_general | solution.py:26
  238.3 6.6 copy.154
  244.9 5.6 fusion.216
  250.5 7.6 copy.163
  258.4 5.6 fusion.208
  264.0 6.7 copy.145
  288.1 15.3 %reduce-scatter.11.cloned.1.call-done = f32[512,768]{1,0:T(8,128)} async-done(((f32[2048,768]{1,0:T(8,128)}), f32[512,768]{1,0:T(8,128)}) %reduce-scatter.11.cloned.1.call-update) | async-done | bytes 1572880 | tf_op jit(solution)/shard_map/reduce_scatter | solution.py:154
  303.4 61.0 %reduce-scatter.13.cloned.1.call-done = f32[512,768]{1,0:T(8,128)} async-done(((f32[2048,768]{1,0:T(8,128)}), f32[512,768]{1,0:T(8,128)}) %reduce-scatter.13.cloned.1.call-update) | async-done | bytes 1572880 | tf_op jit(solution)/shard_map/reduce_scatter | solution.py:154
  364.4 60.8 %reduce-scatter.9.cloned.1.call-done = f32[512,768]{1,0:T(8,128)} async-done(((f32[2048,768]{1,0:T(8,128)}), f32[512,768]{1,0:T(8,128)}) %reduce-scatter.9.cloned.1.call-update) | async-done | bytes 1572880 | tf_op jit(solution)/shard_map/reduce_scatter | solution.py:154
  425.2 6.7 fusion.192
  432.2 28.4 %all-gather.15.cloned.1.call-done = bf16[2048,768]{1,0:T(8,128)(2,1)} async-done(((bf16[512,768]{1,0:T(8,128)(2,1)}), bf16[2048,768]{1,0:T(8,128)(2,1)}) %all-gather.15.cloned.1.call-update) | async-done | bytes 3145744 | tf_op jit(solution)/shard_map/all_gather | solution.py:150
  460.6 4.7 copy.169
  465.3 17.4 %fusion.41 = (bf16[2048,4,192]{0,2,1:T(8,128)(2,1)S(1)}, f32[2048,4,192]{0,2,1:T(8,128)}, f32[4,2048,192]{1,2,0:T(8,128)}) fusion(f32[4,192]{1,0:T(4,128)S(1)} %copy-done.249, bf16[2048,4,192]{0,2,1:T(8,128)(2,1)} %bitcast.860, bf16[4,192,192]{2,1,0:T(8,128)(2,1)S(1)} %copy-done.42), kind=kOutput, calls=%fused_computation.78 | convolution fusion | flops 707788800 | bytes 19172352 | tf_op jit(solution)/shard_map/tgi,gio->tgo/dot_general | solution.py:26
  486.5 6.6 copy.172
  500.4 51.3 %reduce-scatter.15.cloned.1.call-done = f32[512,768]{1,0:T(8,128)} async-done(((f32[2048,768]{1,0:T(8,128)}), f32[512,768]{1,0:T(8,128)}) %reduce-scatter.15.cloned.1.call-update) | async-done | bytes 1572880 | tf_op jit(solution)/shard_map/reduce_scatter | solution.py:154
  555.4 6.2 fusion.118
  582.6 14.3 all-gather.17.cloned.1.call-done
  601.5 12.2 convert_reduce_fusion.3
  613.7 13.1 all-gather.21.cloned.1.call-done
  626.8 4.8 copy.191
  631.6 25.4 %all-gather.19.cloned.1.call-done = bf16[2048,768]{1,0:T(8,128)(2,1)} async-done(((bf16[512,768]{1,0:T(8,128)(2,1)}), bf16[2048,768]{1,0:T(8,128)(2,1)}) %all-gather.19.cloned.1.call-update) | async-done | bytes 3145744 | tf_op jit(solution)/shard_map/all_gather | solution.py:166
  657.0 4.8 copy.182
  674.5 7.9 convert_reduce_fusion.1
  682.5 5.5 convert_reduce_fusion.2
  688.0 4.8 copy.200
  692.8 4.7 fusion.132
  697.6 7.3 convert_reduce_fusion
  712.6 5.5 fusion.237
  718.0 6.6 copy.201
  724.7 5.5 fusion.229
  730.2 6.6 copy.183
  736.8 5.5 fusion.233
  742.3 6.6 copy.192
  749.0 5.5 fusion.225
  754.5 6.6 copy.174
  767.6 21.7 %psum.115 = bf16[4,192]{1,0:T(4,128)(2,1)S(1)} all-reduce(bf16[4,192]{1,0:T(4,128)(2,1)S(1)} %add_convert_fusion.40), channel_id=1, replica_groups=mesh['dp'=8,'ffn'=4] {'dp'}, use_global_device_ids=true, to_apply=%region_86.87 | all-reduce | flops 768 | bytes 3072 | tf_op jit(solution)/shard_map/psum | solution.py:240
  793.8 53.6 %reduce-scatter.23.cloned.1.call-done = f32[512,768]{1,0:T(8,128)} async-done(((f32[2048,768]{1,0:T(8,128)}), f32[512,768]{1,0:T(8,128)}) %reduce-scatter.23.cloned.1.call-update) | async-done | bytes 1572880 | tf_op jit(solution)/shard_map/reduce_scatter | solution.py:175
  847.4 60.8 %reduce-scatter.19.cloned.1.call-done = f32[512,768]{1,0:T(8,128)} async-done(((f32[2048,768]{1,0:T(8,128)}), f32[512,768]{1,0:T(8,128)}) %reduce-scatter.19.cloned.1.call-update) | async-done | bytes 1572880 | tf_op jit(solution)/shard_map/reduce_scatter | solution.py:175
  908.2 6.2 multiply_reduce_fusion.6
  914.4 54.7 %reduce-scatter.21.cloned.1.call-done = f32[512,768]{1,0:T(8,128)} async-done(((f32[2048,768]{1,0:T(8,128)}), f32[512,768]{1,0:T(8,128)}) %reduce-scatter.21.cloned.1.call-update) | async-done | bytes 1572880 | tf_op jit(solution)/shard_map/reduce_scatter | solution.py:175
  969.2 60.7 %reduce-scatter.17.cloned.1.call-done = f32[512,768]{1,0:T(8,128)} async-done(((f32[2048,768]{1,0:T(8,128)}), f32[512,768]{1,0:T(8,128)}) %reduce-scatter.17.cloned.1.call-update) | async-done | bytes 1572880 | tf_op jit(solution)/shard_map/reduce_scatter | solution.py:175
  1030.0 7.7 multiply_reduce_fusion.7
  1046.8 11.5 multiply_reduce_fusion.3
  1059.6 7.0 multiply_convert_fusion.3
  1072.2 5.0 convert_reduce_fusion.11
  1081.3 14.0 multiply_reduce_fusion.2
  1095.3 7.1 multiply_convert_fusion.2
  1107.0 4.8 convert_reduce_fusion.10
  1116.5 14.0 multiply_reduce_fusion.1
  1130.6 7.1 multiply_convert_fusion.1
  1143.2 4.8 convert_reduce_fusion.9
  1152.6 14.1 multiply_reduce_fusion
  1166.7 7.1 multiply_convert_fusion
  1179.4 5.0 convert_reduce_fusion.8
  1290.6 41.6 %all-reduce = (f32[768]{0:T(1024)}, f32[768]{0:T(1024)}, f32[768]{0:T(1024)}, f32[768]{0:T(1024)}, f32[768]{0:T(1024)}, /*index=5*/f32[768]{0:T(1024)}, f32[768]{0:T(1024)}, f32[768]{0:T(1024)}) all-reduce(f32[768]{0:T(1024)} %add.706, f32[768]{0:T(1024)} %add.718, ...), channel_id=1, replica_groups=mesh['dp'=8,'ffn'=4] {'dp','ffn'}, use_global_device_ids=true, to_apply=%region_57.58 | all-reduce | flops 6144 | bytes 49152 | tf_op jit(solution)/shard_map/psum | solution.py:221
  1335.1 89.1 %all-reduce.6.cloned.1.call-done = (f32[4,192,192]{1,2,0:T(8,128)}, f32[4,192,192]{1,2,0:T(8,128)}, f32[4,192,192]{1,2,0:T(8,128)}, f32[768,768]{1,0:T(8,128)}) async-done(((f32[4,192,192]{1,2,0:T(8,128)}, f32[4,192,192]{1,2,0:T(8,128)}, f32[4,192,192]{1,2,0:T(8,128)}, f32[768,768]{1,0:T(8,128)}), (f32[4,192,192]{1,2,0:T(8,128)}, f32[4,192,192]{1,2,0:T(8,128)}, f32[4,192,192]{1,2,0:T(8,128)}, ...) | async-done | bytes 4128784 | tf_op jit(solution)/shard_map/psum | solution.py:221
  (793 shorter events, 325.4 us)
Async XLA Ops:
  7.2 38.8 %copy-start = (bf16[768,768]{1,0:T(8,128)(2,1)S(1)}, bf16[768,768]{1,0:T(8,128)(2,1)}, u32[]{:S(2)}) copy-start(bf16[768,768]{1,0:T(8,128)(2,1)} %param.26) | copy-start | bytes 3538948
  7.2 113.9 %all-gather.11.cloned.1.call-start = ((), (), s32[]{:S(2)}) async-start(), calls=%async_computation.10 | async-start | bytes 3932160 | tf_op jit(solution)/shard_map/all_gather | solution.py:150
  29.1 43.0 %copy-start.140 = (f32[12,64]{1,0:T(8,128)}, f32[12,64]{1,0:T(8,128)S(1)}, u32[]{:S(2)}) copy-start(f32[12,64]{1,0:T(8,128)S(1)} %reshape.926) | copy-start | bytes 9220
  38.1 38.8 %copy-start.152 = (f32[12,64]{1,0:T(8,128)}, f32[12,64]{1,0:T(8,128)S(1)}, u32[]{:S(2)}) copy-start(f32[12,64]{1,0:T(8,128)S(1)} %reshape.925) | copy-start | bytes 9220
  38.1 45.7 %copy-start.252 = (f32[768]{0:T(1024)}, f32[768]{0:T(1024)S(1)}, u32[]{:S(2)}) copy-start(f32[768]{0:T(1024)S(1)} %convert_element_type.555) | copy-start | bytes 9220
  49.5 38.2 %copy-start.157 = (f32[512]{0:T(512)}, f32[512]{0:T(512)S(1)}, u32[]{:S(2)}) copy-start(f32[512]{0:T(512)S(1)} %broadcast_multiply_fusion.5) | copy-start | bytes 6148
  54.5 14.9 %copy-start.148 = (f32[12,512]{1,0:T(8,128)}, f32[12,512]{1,0:T(8,128)S(1)}, u32[]{:S(2)}) copy-start(f32[12,512]{1,0:T(8,128)S(1)} %log_add_fusion.3) | copy-start | bytes 73732
  71.8 15.8 %copy-start.5 = (f32[512,768]{1,0:T(8,128)}, f32[512,768]{1,0:T(8,128)S(1)}, u32[]{:S(2)}) copy-start(f32[512,768]{1,0:T(8,128)S(1)} %get-tuple-element.400) | copy-start | bytes 4718596
  71.9 15.8 %copy-start.160 = (f32[512]{0:T(512)}, f32[512]{0:T(512)S(1)}, u32[]{:S(2)}) copy-start(f32[512]{0:T(512)S(1)} %broadcast_multiply_fusion.7) | copy-start | bytes 6148
  89.8 61.5 %all-gather.13.cloned.1.call-start = ((), (), s32[]{:S(2)}) async-start(), calls=%async_computation.12 | async-start | bytes 3932160 | tf_op jit(solution)/shard_map/all_gather | solution.py:150
  90.5 91.5 %all-gather.9.cloned.1.call-start = ((), (), s32[]{:S(2)}) async-start(), calls=%async_computation.8 | async-start | bytes 3932160 | tf_op jit(solution)/shard_map/all_gather | solution.py:150
  91.2 212.2 %reduce-scatter.11.cloned.1.call-start = ((), (), s32[]{:S(2)}) async-start(), calls=%async_computation.11 | async-start | bytes 7864320 | tf_op jit(solution)/shard_map/reduce_scatter | solution.py:154
  91.3 95.3 %copy-start.248 = (f32[4,192]{1,0:T(4,128)}, f32[4,192]{1,0:T(4,128)S(1)}, u32[]{:S(2)}) copy-start(f32[4,192]{1,0:T(4,128)S(1)} %convert_element_type.557) | copy-start | bytes 9220
  126.2 29.7 %copy-start.42 = (bf16[4,192,192]{2,1,0:T(8,128)(2,1)S(1)}, bf16[4,192,192]{2,1,0:T(8,128)(2,1)}, u32[]{:S(2)}) copy-start(bf16[4,192,192]{2,1,0:T(8,128)(2,1)} %param.30) | copy-start | bytes 884740
  186.7 48.0 %copy-start.97 = (bf16[4,192,192]{2,1,0:T(8,128)(2,1)S(1)}, bf16[4,192,192]{2,1,0:T(8,128)(2,1)}, u32[]{:S(2)}) copy-start(bf16[4,192,192]{2,1,0:T(8,128)(2,1)} %param.32) | copy-start | bytes 884740
  244.9 119.5 %reduce-scatter.13.cloned.1.call-start = ((), (), s32[]{:S(2)}) async-start(), calls=%async_computation.13 | async-start | bytes 7864320 | tf_op jit(solution)/shard_map/reduce_scatter | solution.py:154
  258.2 167.0 %reduce-scatter.9.cloned.1.call-start = ((), (), s32[]{:S(2)}) async-start(), calls=%async_computation.9 | async-start | bytes 7864320 | tf_op jit(solution)/shard_map/reduce_scatter | solution.py:154
  270.7 189.9 %all-gather.15.cloned.1.call-start = ((), (), s32[]{:S(2)}) async-start(), calls=%async_computation.14 | async-start | bytes 3932160 | tf_op jit(solution)/shard_map/all_gather | solution.py:150
  272.3 152.8 %copy-start.178 = (f32[768]{0:T(1024)}, f32[768]{0:T(1024)S(1)}, u32[]{:S(2)}) copy-start(f32[768]{0:T(1024)S(1)} %convert_element_type.559) | copy-start | bytes 9220
  284.1 141.0 %copy-start.6 = (f32[512,768]{1,0:T(8,128)S(1)}, f32[512,768]{1,0:T(8,128)}, u32[]{:S(2)}) copy-start(f32[512,768]{1,0:T(8,128)} %copy-done.5) | copy-start | bytes 4718596
  284.1 141.0 %copy-start.156 = (f32[768]{0:T(1024)S(1)}, f32[768]{0:T(1024)}, u32[]{:S(2)}) copy-start(f32[768]{0:T(1024)} %param.28) | copy-start | bytes 9220
  284.2 141.0 %copy-start.158 = (f32[512]{0:T(512)S(1)}, f32[512]{0:T(512)}, u32[]{:S(2)}) copy-start(f32[512]{0:T(512)} %copy-done.157) | copy-start | bytes 6148
  284.2 141.0 %copy-start.161 = (f32[512]{0:T(512)S(1)}, f32[512]{0:T(512)}, u32[]{:S(2)}) copy-start(f32[512]{0:T(512)} %copy-done.160) | copy-start | bytes 6148
  284.2 141.0 %copy-start.164 = (f32[512]{0:T(512)S(1)}, f32[512]{0:T(512)}, u32[]{:S(2)}) copy-start(f32[512]{0:T(512)} %copy-done.163) | copy-start | bytes 6148
  284.2 141.0 %copy-start.167 = (f32[512]{0:T(512)S(1)}, f32[512]{0:T(512)}, u32[]{:S(2)}) copy-start(f32[512]{0:T(512)} %copy-done.166) | copy-start | bytes 6148
  284.2 141.0 %copy-start.170 = (f32[512]{0:T(512)S(1)}, f32[512]{0:T(512)}, u32[]{:S(2)}) copy-start(f32[512]{0:T(512)} %copy-done.169) | copy-start | bytes 6148
  284.2 141.0 %copy-start.173 = (f32[512]{0:T(512)S(1)}, f32[512]{0:T(512)}, u32[]{:S(2)}) copy-start(f32[512]{0:T(512)} %copy-done.172) | copy-start | bytes 6148
  284.2 141.0 %copy-start.177 = (f32[768]{0:T(1024)S(1)}, f32[768]{0:T(1024)}, u32[]{:S(2)}) copy-start(f32[768]{0:T(1024)} %param.29) | copy-start | bytes 9220
  288.1 143.8 %copy-start.206 = (f32[512]{0:T(512)}, f32[512]{0:T(512)S(1)}, u32[]{:S(2)}) copy-start(f32[512]{0:T(512)S(1)} %multiply_reduce_fusion.13) | copy-start | bytes 6148
  431.9 33.4 %copy-start.249 = (f32[4,192]{1,0:T(4,128)S(1)}, f32[4,192]{1,0:T(4,128)}, u32[]{:S(2)}) copy-start(f32[4,192]{1,0:T(4,128)} %copy-done.248) | copy-start | bytes 9220
  432.0 119.7 %reduce-scatter.15.cloned.1.call-start = ((), (), s32[]{:S(2)}) async-start(), calls=%async_computation.15 | async-start | bytes 7864320 | tf_op jit(solution)/shard_map/reduce_scatter | solution.py:154
  465.3 17.5 %copy-start.98 = (bf16[4,192,192]{2,1,0:T(8,128)(2,1)S(1)}, bf16[4,192,192]{2,1,0:T(8,128)(2,1)}, u32[]{:S(2)}) copy-start(bf16[4,192,192]{2,1,0:T(8,128)(2,1)} %param.32) | copy-start | bytes 884740
  493.2 58.5 %copy-start.11 = (f32[512,768]{1,0:T(8,128)S(1)}, f32[512,768]{1,0:T(8,128)}, u32[]{:S(2)}) copy-start(f32[512,768]{1,0:T(8,128)} %copy-done.10) | copy-start | bytes 4718596
  493.2 103.7 %all-gather.17.cloned.1.call-start = ((), (), s32[]{:S(2)}) async-start(), calls=%async_computation.16 | async-start | bytes 3932160 | tf_op jit(solution)/shard_map/all_gather | solution.py:166
  500.4 54.5 %copy-start.175 = (f32[768]{0:T(1024)S(1)}, f32[768]{0:T(1024)}, u32[]{:S(2)}) copy-start(f32[768]{0:T(1024)} %param.34) | copy-start | bytes 9220
  568.1 58.7 %all-gather.21.cloned.1.call-start = ((), (), s32[]{:S(2)}) async-start(), calls=%async_computation.20 | async-start | bytes 3932160 | tf_op jit(solution)/shard_map/all_gather | solution.py:166
  572.0 84.9 %all-gather.19.cloned.1.call-start = ((), (), s32[]{:S(2)}) async-start(), calls=%async_computation.18 | async-start | bytes 3932160 | tf_op jit(solution)/shard_map/all_gather | solution.py:166
  576.6 111.4 %all-gather.23.cloned.1.call-start = ((), (), s32[]{:S(2)}) async-start(), calls=%async_computation.22 | async-start | bytes 3932160 | tf_op jit(solution)/shard_map/all_gather | solution.py:166
  579.2 22.4 %copy-start.224 = (f32[512]{0:T(512)}, f32[512]{0:T(512)S(1)}, u32[]{:S(2)}) copy-start(f32[512]{0:T(512)S(1)} %negate_multiply_fusion.5) | copy-start | bytes 6148
  582.1 19.4 %copy-start.250 = (f32[4,192]{1,0:T(4,128)S(1)}, f32[4,192]{1,0:T(4,128)}, u32[]{:S(2)}) copy-start(f32[4,192]{1,0:T(4,128)} %copy-done.248) | copy-start | bytes 9220
  582.1 207.8 %all-reduce.8.cloned.1.call-start = ((), (), s32[]{:S(2)}) async-start(), calls=%async_computation.25 | async-start | bytes 1572864 | tf_op jit(solution)/shard_map/psum | solution.py:239
  712.5 134.9 %reduce-scatter.23.cloned.1.call-start = ((), (), s32[]{:S(2)}) async-start(), calls=%async_computation.23 | async-start | bytes 7864320 | tf_op jit(solution)/shard_map/reduce_scatter | solution.py:175
  724.7 183.5 %reduce-scatter.19.cloned.1.call-start = ((), (), s32[]{:S(2)}) async-start(), calls=%async_computation.19 | async-start | bytes 7864320 | tf_op jit(solution)/shard_map/reduce_scatter | solution.py:175
  736.8 232.4 %reduce-scatter.21.cloned.1.call-start = ((), (), s32[]{:S(2)}) async-start(), calls=%async_computation.21 | async-start | bytes 7864320 | tf_op jit(solution)/shard_map/reduce_scatter | solution.py:175
  748.9 281.0 %reduce-scatter.17.cloned.1.call-start = ((), (), s32[]{:S(2)}) async-start(), calls=%async_computation.17 | async-start | bytes 7864320 | tf_op jit(solution)/shard_map/reduce_scatter | solution.py:175
  761.2 663.0 %all-reduce.6.cloned.1.call-start = ((), (), s32[]{:S(2)}) async-start(), calls=%async_computation.24 | async-start | bytes 9437184 | tf_op jit(solution)/shard_map/psum | solution.py:221
  765.6 142.6 %copy-start.159 = (f32[512]{0:T(512)S(1)}, f32[512]{0:T(512)}, u32[]{:S(2)}) copy-start(f32[512]{0:T(512)} %copy-done.157) | copy-start | bytes 6148
  793.8 120.6 %copy-start.207 = (f32[512]{0:T(512)S(1)}, f32[512]{0:T(512)}, u32[]{:S(2)}) copy-start(f32[512]{0:T(512)} %copy-done.206) | copy-start | bytes 6148
  793.8 236.1 %copy-start.7 = (f32[512,768]{1,0:T(8,128)S(1)}, f32[512,768]{1,0:T(8,128)}, u32[]{:S(2)}) copy-start(f32[512,768]{1,0:T(8,128)} %copy-done.5) | copy-start | bytes 4718596
  793.8 236.1 %copy-start.162 = (f32[512]{0:T(512)S(1)}, f32[512]{0:T(512)}, u32[]{:S(2)}) copy-start(f32[512]{0:T(512)} %copy-done.160) | copy-start | bytes 6148
  793.8 236.1 %copy-start.165 = (f32[512]{0:T(512)S(1)}, f32[512]{0:T(512)}, u32[]{:S(2)}) copy-start(f32[512]{0:T(512)} %copy-done.163) | copy-start | bytes 6148
  793.8 236.1 %copy-start.168 = (f32[512]{0:T(512)S(1)}, f32[512]{0:T(512)}, u32[]{:S(2)}) copy-start(f32[512]{0:T(512)} %copy-done.166) | copy-start | bytes 6148
  793.8 236.1 %copy-start.171 = (f32[512]{0:T(512)S(1)}, f32[512]{0:T(512)}, u32[]{:S(2)}) copy-start(f32[512]{0:T(512)} %copy-done.169) | copy-start | bytes 6148
  793.8 236.1 %copy-start.220 = (f32[512]{0:T(512)S(1)}, f32[512]{0:T(512)}, u32[]{:S(2)}) copy-start(f32[512]{0:T(512)} %copy-done.219) | copy-start | bytes 6148
  793.8 236.1 %copy-start.222 = (f32[512]{0:T(512)S(1)}, f32[512]{0:T(512)}, u32[]{:S(2)}) copy-start(f32[512]{0:T(512)} %copy-done.221) | copy-start | bytes 6148
  1116.4 14.1 slice-start.4
  1116.4 14.1 slice-start.5
  1116.4 14.1 copy-start.92
  1116.4 14.1 copy-start.147
  1152.6 14.1 slice-start.9
  1152.6 14.1 slice-start.10
  1152.6 14.1 slice-start.11
  1152.6 14.1 copy-start.96
  1152.6 14.1 copy-start.151
  (235 other events, 973.7 us)
Sparse Core Ops, SparseCore 0:
  89.9 31.2 all-gather.10
  122.7 28.5 all-gather.12
  153.4 28.5 all-gather.8
  245.0 58.3 reduce-scatter.10
  306.0 58.3 reduce-scatter.12
  366.7 58.3 reduce-scatter.8
  432.1 28.5 all-gather.14
  493.3 58.3 reduce-scatter.14
  568.3 28.5 all-gather.16
  598.3 28.5 all-gather.20
  628.4 28.5 all-gather.18
  658.4 28.5 all-gather.22
  712.6 74.7 all-reduce.7
  790.0 57.3 reduce-scatter.22
  849.8 58.3 reduce-scatter.18
  910.8 58.3 reduce-scatter.20
  971.5 58.3 reduce-scatter.16
  1278.2 145.8 all-reduce.5
where the time goes:
time: 1440 us
  waiting for transfers between devices  661 us (46%)
  matrix products  383 us (27%)
  local copies, waits for them, and re-layouts  192 us (13%)
  other arithmetic  121 us (8%)
  blocking collectives  63.3 us (4%)
  between operations  17.4 us (1%)
    reduce_scatter x4, waiting for transfers between devices, on_device(): lax.psum_scatter(grouped_back(grad_pre_low, expand_full), 'ffn', scatter_...  230 us
    reduce_scatter x4, waiting for transfers between devices, on_device(): lax.psum_scatter(grouped(active, shrink_full), 'ffn', scatter_dimension=0...  188 us
    dot_general x20, matrix products, grouped(): jnp.einsum('tgi,gio->tgo', parted, weight, preferred_element_type=jnp.flo...  109 us
    all_gather x4, waiting for transfers between devices, on_device(): gathered = lax.all_gather(normed_low, 'ffn', axis=0, tiled=True)  99.7 us
    psum x1, waiting for transfers between devices, on_device(): lax.psum((acc_query, acc_query_bias, acc_key, acc_value, acc_value_bias,...  89.1 us
    dot_general x20, matrix products, grouped_back(): jnp.einsum('tgo,gio->tgi', parted, weight, preferred_element_type=jnp.flo...  82.4 us
    reshape x16, local copies, waits for them, and re-layouts, grouped_back(): return result.reshape(upstream.shape[0], groups * width_in)  63.1 us
    dot_general x4, matrix products, attend_back(): jnp.einsum('qhd,khd->hqk', upstream, values, preferred_element_type=jnp.f...  53.6 us
  transfers between devices with their start and end apart: 18, of which 16 were waited for; matrix products, arithmetic and copies ran while one was open for 14% of the time, Pallas kernels for 0%

commit v1 on v0

v1 whole, which is shorter than its diff:
```python
import functools

import jax
import jax.numpy as jnp
from jax import lax
from jax.experimental import pallas as pl
from jax.experimental.pallas import tpu as pltpu
from jax.sharding import PartitionSpec as P

HEADS = 12
HEAD = 64
epsilon = 1e-05
masked_score = -1e30
bf16 = jnp.bfloat16
f32 = jnp.float32
VMEM_LIMIT = 60 * 1024 * 1024

NN = (((1,), (0,)), ((), ()))
NT = (((1,), (1,)), ((), ()))
TN = (((0,), (0,)), ((), ()))


def dot(a, b, dims=NN):
    return lax.dot_general(a, b, dims, preferred_element_type=f32)


def window(group, width):
    start = group * width
    base = start // 128 * 128
    return base, start - base


def shift_matrix(rows, cols, offset):
    r = lax.broadcasted_iota(jnp.int32, (rows, cols), 0)
    c = lax.broadcasted_iota(jnp.int32, (rows, cols), 1)
    return jnp.where(c == r + offset, 1.0, 0.0).astype(bf16)


def pad_cols(w, offset):
    return dot(w, shift_matrix(w.shape[1], 256, offset)).astype(bf16)


def pad_rows(w, offset):
    rows = w.shape[0]
    parts = []
    if offset:
        parts.append(jnp.zeros((offset, w.shape[1]), bf16))
    parts.append(w)
    if 256 - offset - rows:
        parts.append(jnp.zeros((256 - offset - rows, w.shape[1]), bf16))
    return jnp.concatenate(parts, axis=0)


def join_windows(parts):
    out = []
    for i in range(0, len(parts), 2):
        a, b = parts[i], parts[i + 1]
        out += [a[:, :128], a[:, 128:] + b[:, :128], b[:, 128:]]
    return out


def attend_kernel(x_ref, docs_ref, wq_ref, qb_ref, wk_ref, wv_ref, vb_ref,
                  q_ref, k_ref, v_ref, c_ref, p_ref, wpad, bias_ref):
    length = x_ref.shape[1]
    width = x_ref.shape[2]
    groups = wq_ref.shape[0]
    per = width // groups

    @pl.when(pl.program_id(0) == 0)
    def _():
        for j, w_ref in enumerate((wq_ref, wk_ref, wv_ref)):
            for g in range(groups):
                _, off = window(g, per)
                wpad[j, g] = pad_rows(pad_cols(w_ref[g], off), off)

    for j, (out, b_ref) in enumerate(((q_ref, qb_ref), (k_ref, None), (v_ref, vb_ref))):
        parts = []
        for g in range(groups):
            base, _ = window(g, per)
            parts.append(dot(x_ref[0, :, base:base + 256], wpad[j, g]))
        for n, col in enumerate(join_windows(parts)):
            if b_ref is not None:
                col = col + b_ref[:, 128 * n:128 * n + 128].astype(f32)
            out[0, :, 128 * n:128 * n + 128] = col.astype(bf16)

    docs = docs_ref[0].astype(f32)
    down = jnp.transpose(jnp.broadcast_to(docs, (128, length)))[:, :1]
    bias_ref[...] = jnp.where(down == docs, 0.0, masked_score)
    low = lax.broadcasted_iota(jnp.int32, (1, 128), 1) < HEAD
    for pair in range(HEADS // 2):
        lanes = slice(128 * pair, 128 * pair + 128)
        q2 = q_ref[0, :, lanes] * bf16(HEAD ** -0.5)
        k2 = k_ref[0, :, lanes]
        v2 = v_ref[0, :, lanes]
        acc = None
        for h in range(2):
            half = low if h == 0 else jnp.logical_not(low)
            km = jnp.where(half, k2, bf16(0))
            vm = jnp.where(half, v2, bf16(0))
            s = dot(q2, km, NT) + bias_ref[...]
            top = jnp.max(s, axis=-1, keepdims=True)
            e = jnp.exp(s - top)
            total = jnp.sum(e, axis=-1, keepdims=True)
            pr = (e * (1.0 / total)).astype(bf16)
            p_ref[0, 2 * pair + h] = pr
            c = dot(pr, vm)
            acc = c if acc is None else acc + c
        c_ref[0, :, lanes] = acc.astype(bf16)


def full(shape):
    return pl.BlockSpec(shape, lambda *_: (0,) * len(shape))


def row_spec(shape):
    return pl.BlockSpec((1,) + shape, lambda r: (r,) + (0,) * len(shape))


def attend(x, docs, wq, qb, wk, wv, vb):
    rows, length, width = x.shape
    wide = row_spec((length, width))
    low = jax.ShapeDtypeStruct((rows, length, width), bf16)
    return pl.pallas_call(
        attend_kernel,
        grid=(rows,),
        in_specs=[wide, row_spec((1, length)), full(wq.shape), full(qb.shape), full(wk.shape),
                  full(wv.shape), full(vb.shape)],
        out_specs=[wide, wide, wide, wide, row_spec((HEADS, length, length))],
        out_shape=[low, low, low, low, jax.ShapeDtypeStruct((rows, HEADS, length, length), bf16)],
        scratch_shapes=[pltpu.VMEM((3, wq.shape[0], 256, 256), bf16), pltpu.VMEM((length, length), f32)],
        compiler_params=pltpu.CompilerParams(vmem_limit_bytes=VMEM_LIMIT),
        cost_estimate=pl.CostEstimate(flops=int(2e10), bytes_accessed=int(5e7), transcendentals=0),
        name="attend",
    )(x, docs, wq, qb, wk, wv, vb)


def gelu_both(u):
    cdf = 0.5 * (1.0 + lax.erf(u * 0.7071067811865476))
    pdf = jnp.exp(-0.5 * u * u) * 0.3989422804014327
    return u * cdf, cdf + u * pdf


def feed_kernel(x_ref, c_ref, e_ref, wo_ref, we_ref, be_ref, ws_ref, vec_ref,
                result_ref, dh1_ref, dc_ref, gwo_ref, gwe_ref, gws_ref, gbe_ref, gvec_ref,
                wepad, wspad, act, slope, pre_low, df_low, wo_t):
    step = pl.program_id(0)
    shards = we_ref.shape[0]
    groups = we_ref.shape[1]
    part = we_ref.shape[3]
    per = we_ref.shape[2]
    hidden = shards * part
    width = x_ref.shape[2]

    @pl.when(step == 0)
    def _():
        gwo_ref[...] = jnp.zeros(gwo_ref.shape, f32)
        gwe_ref[...] = jnp.zeros(gwe_ref.shape, f32)
        gws_ref[...] = jnp.zeros(gws_ref.shape, f32)
        gbe_ref[...] = jnp.zeros(gbe_ref.shape, f32)
        gvec_ref[...] = jnp.zeros(gvec_ref.shape, f32)
        for g in range(groups):
            _, off = window(g, per)
            w = jnp.concatenate([we_ref[s, g].astype(f32) for s in range(shards)], axis=1).astype(bf16)
            wepad[g] = pad_rows(w, off)
            wspad[g] = jnp.concatenate([pad_cols(ws_ref[s, g], off) for s in range(shards)], axis=0)

    out_bias, mixed_gain, mixed_bias = vec_ref[0:1], vec_ref[1:2], vec_ref[2:3]
    shrink_bias, final_gain, final_bias = vec_ref[3:4], vec_ref[4:5], vec_ref[5:6]
    h1 = x_ref[0].astype(f32) + dot(c_ref[0], wo_ref[...]) + out_bias
    cen = h1 - jnp.mean(h1, axis=-1, keepdims=True)
    rstd1 = lax.rsqrt(jnp.mean(cen * cen, axis=-1, keepdims=True) + epsilon)
    xhat1 = cen * rstd1
    a = xhat1 * mixed_gain + mixed_bias
    a_low = a.astype(bf16)
    pre_low[...] = a_low

    parts = []
    for g in range(groups):
        base, _ = window(g, per)
        for n in range(hidden // 256):
            cols = slice(256 * n, 256 * n + 256)
            u = dot(pre_low[:, base:base + 256], wepad[g, :, cols]) + be_ref[g:g + 1, cols]
            val, slp = gelu_both(u)
            act[g, :, cols] = val.astype(bf16)
            slope[g, :, cols] = slp
        parts.append(dot(act[g], wspad[g]))
    f = jnp.concatenate(join_windows(parts), axis=1)
    h2 = a + f + shrink_bias
    cen = h2 - jnp.mean(h2, axis=-1, keepdims=True)
    rstd2 = lax.rsqrt(jnp.mean(cen * cen, axis=-1, keepdims=True) + epsilon)
    xhat2 = cen * rstd2
    result_ref[0] = (xhat2 * final_gain + final_bias).astype(bf16)

    up = e_ref[0].astype(f32)
    gvec_ref[4:5] += jnp.sum(up * xhat2, axis=0, keepdims=True)
    gvec_ref[5:6] += jnp.sum(up, axis=0, keepdims=True)
    dx = up * final_gain
    dh2 = rstd2 * (dx - jnp.mean(dx, axis=-1, keepdims=True) - xhat2 * jnp.mean(dx * xhat2, axis=-1, keepdims=True))
    gvec_ref[3:4] += jnp.sum(dh2, axis=0, keepdims=True)
    df_low[...] = dh2.astype(bf16)
    a_t = jnp.transpose(a_low)
    df_t = jnp.transpose(df_low[...])
    parts = []
    for g in range(groups):
        base, _ = window(g, per)
        rows = slice(per * g, per * g + per)
        gws_ref[g] += dot(df_t[rows], act[g])
        acc = None
        for n in range(hidden // 256):
            cols = slice(256 * n, 256 * n + 256)
            dg = dot(df_low[:, base:base + 256], wspad[g, cols, :], NT)
            du = (dg * slope[g, :, cols]).astype(bf16)
            gbe_ref[g:g + 1, cols] += jnp.sum(du.astype(f32), axis=0, keepdims=True)
            gwe_ref[g, :, cols] += dot(a_t[rows], du)
            da = dot(du, wepad[g, :, cols], NT)
            acc = da if acc is None else acc + da
        parts.append(acc)
    da = dh2 + jnp.concatenate(join_windows(parts), axis=1)
    gvec_ref[1:2] += jnp.sum(da * xhat1, axis=0, keepdims=True)
    gvec_ref[2:3] += jnp.sum(da, axis=0, keepdims=True)
    dx = da * mixed_gain
    dh1 = rstd1 * (dx - jnp.mean(dx, axis=-1, keepdims=True) - xhat1 * jnp.mean(dx * xhat1, axis=-1, keepdims=True))
    gvec_ref[0:1] += jnp.sum(dh1, axis=0, keepdims=True)
    dh1_ref[0] = dh1
    dy = dh1.astype(bf16)
    gwo_ref[...] += dot(jnp.transpose(c_ref[0]), dy)
    dc_ref[0] = dot(dy, wo_ref[...], NT).astype(bf16)


def feed(x, c, e, wo, we, be, ws, vec):
    rows, length, width = x.shape
    shards, groups, per, part = we.shape
    hidden = shards * part
    wide = row_spec((length, width))
    low = jax.ShapeDtypeStruct((rows, length, width), bf16)
    grads = [(width, width), (groups, per, hidden), (groups, per, hidden), (groups, hidden), (8, width)]
    return pl.pallas_call(
        feed_kernel,
        grid=(rows,),
        in_specs=[wide, wide, wide] + [full(t.shape) for t in (wo, we, be, ws, vec)],
        out_specs=[wide, wide, wide] + [full(s) for s in grads],
        out_shape=[low, jax.ShapeDtypeStruct((rows, length, width), f32), low]
        + [jax.ShapeDtypeStruct(s, f32) for s in grads],
        scratch_shapes=[
            pltpu.VMEM((groups, 256, hidden), bf16),
            pltpu.VMEM((groups, hidden, 256), bf16),
            pltpu.VMEM((groups, length, hidden), bf16),
            pltpu.VMEM((groups, length, hidden), f32),
            pltpu.VMEM((length, width), bf16),
            pltpu.VMEM((length, width), bf16),
            pltpu.VMEM((8, 128), bf16),
        ],
        compiler_params=pltpu.CompilerParams(vmem_limit_bytes=VMEM_LIMIT),
        cost_estimate=pl.CostEstimate(flops=int(4e10), bytes_accessed=int(5e7), transcendentals=0),
        name="feed",
    )(x, c, e, wo, we, be, ws, vec)


def attend_back_kernel(x_ref, q_ref, k_ref, v_ref, c_ref, dc_ref, p_ref, dh1_ref, wq_ref, wk_ref, wv_ref,
                       dx_ref, gw_ref, gvec_ref, wpad, dqkv, gacc):
    step = pl.program_id(0)
    groups, per = wq_ref.shape[0], wq_ref.shape[1]
    lanes_in = x_ref.shape[2]

    @pl.when(step == 0)
    def _():
        gacc[...] = jnp.zeros(gacc.shape, f32)
        gvec_ref[...] = jnp.zeros(gvec_ref.shape, f32)
        for j, w_ref in enumerate((wq_ref, wk_ref, wv_ref)):
            for g in range(groups):
                _, off = window(g, per)
                wpad[j, g] = pad_rows(pad_cols(w_ref[g], off), off)

    low = lax.broadcasted_iota(jnp.int32, (1, 128), 1) < HEAD
    for pair in range(lanes_in // 128):
        lanes = slice(128 * pair, 128 * pair + 128)
        q2 = q_ref[0, :, lanes] * bf16(HEAD ** -0.5)
        k2 = k_ref[0, :, lanes]
        v2 = v_ref[0, :, lanes]
        dc2 = dc_ref[0, :, lanes]
        prod = dc2.astype(f32) * c_ref[0, :, lanes].astype(f32)
        dq = dk = dv = None
        for h in range(2):
            half = low if h == 0 else jnp.logical_not(low)
            km = jnp.where(half, k2, bf16(0))
            qm = jnp.where(half, q2, bf16(0))
            dcm = jnp.where(half, dc2, bf16(0))
            delta = jnp.sum(jnp.where(half, prod, 0.0), axis=-1, keepdims=True)
            pr = p_ref[0, 2 * pair + h]
            dp = dot(dcm, v2, NT)
            ds = (pr.astype(f32) * (dp - delta)).astype(bf16)
            a = dot(ds, km)
            b = dot(ds, qm, TN)
            c = dot(pr, dcm, TN)
            dq = a if dq is None else dq + a
            dk = b if dk is None else dk + b
            dv = c if dv is None else dv + c
        dq = (dq * (HEAD ** -0.5)).astype(bf16)
        dk = dk.astype(bf16)
        dv = dv.astype(bf16)
        dqkv[0, :, lanes] = dq
        dqkv[1, :, lanes] = dk
        dqkv[2, :, lanes] = dv
        gvec_ref[0:1, lanes] += jnp.sum(dq.astype(f32), axis=0, keepdims=True)
        gvec_ref[1:2, lanes] += jnp.sum(dv.astype(f32), axis=0, keepdims=True)

    x_t = jnp.transpose(x_ref[0])
    parts = []
    for g in range(groups):
        base, off = window(g, per)
        acc = None
        for j in range(3):
            d = dqkv[j, :, base:base + 256]
            gacc[j, g] += dot(x_t[per * g:per * g + per], d)
            t = dot(d, wpad[j, g], NT)
            acc = t if acc is None else acc + t
        parts.append(acc)
    for n, col in enumerate(join_windows(parts)):
        lanes = slice(128 * n, 128 * n + 128)
        dx_ref[0, :, lanes] = (col + dh1_ref[0, :, lanes]).astype(bf16)

    @pl.when(step == pl.num_programs(0) - 1)
    def _():
        gw_ref[...] = gacc[...]


def attend_back(x, q, k, v, c, dc, p, dh1, wq, wk, wv, part, parts, prev=None):
    rows, length, width = x.shape
    groups, per, _ = wq.shape
    mine = groups // parts
    lanes = width // parts
    heads = HEADS // parts
    wide = pl.BlockSpec((1, length, lanes), lambda r: (r, 0, part))
    wspec = pl.BlockSpec((mine, per, per), lambda r: (part, 0, 0))
    args = [x, q, k, v, c, dc, p, dh1, wq, wk, wv]
    specs = [wide] * 6 + [pl.BlockSpec((1, heads, length, length), lambda r: (r, part, 0, 0)), wide] + [wspec] * 3
    kernel = attend_back_kernel
    aliases = {}
    if prev is not None:
        args.append(prev)
        specs.append(pl.BlockSpec(memory_space=pl.ANY))
        aliases = {len(args) - 1: 0}
        kernel = lambda *refs: attend_back_kernel(*refs[:11], *refs[12:])
    return pl.pallas_call(
        kernel,
        grid=(rows,),
        in_specs=specs,
        out_specs=[wide, full((3, mine, per, 256)), full((8, lanes))],
        out_shape=[jax.ShapeDtypeStruct((rows, length, width), bf16),
                   jax.ShapeDtypeStruct((3, mine, per, 256), f32), jax.ShapeDtypeStruct((8, lanes), f32)],
        input_output_aliases=aliases,
        scratch_shapes=[
            pltpu.VMEM((3, mine, 256, 256), bf16),
            pltpu.VMEM((3, length, lanes), bf16),
            pltpu.VMEM((3, mine, per, 256), f32),
        ],
        compiler_params=pltpu.CompilerParams(vmem_limit_bytes=VMEM_LIMIT),
        cost_estimate=pl.CostEstimate(flops=int(2e10), bytes_accessed=int(3e7), transcendentals=0),
        name="attend_back",
    )(*args)


def gather_shards(shard):
    count = lax.axis_size("ffn")
    return [shard] + [
        lax.ppermute(shard, "ffn", [(i, (i + d) % count) for i in range(count)]) for d in range(1, count)
    ]


def order_shards(got):
    count = len(got)
    me = lax.axis_index("ffn")
    stacked = jnp.stack(got)
    return stacked[(me - jnp.arange(count)) % count]


def reduce_all(x, axes, count):
    got = lax.all_to_all(x, axes, 0, 0, tiled=True)
    return jnp.sum(got.astype(f32), axis=0)


def spread(x, axes, count):
    return lax.all_to_all(jnp.broadcast_to(x[None], (count,) + x.shape), axes, 0, 0, tiled=True)


def on_device(
    inputs,
    doc_ids,
    cotangent,
    query_weight,
    query_bias,
    key_weight,
    value_weight,
    value_bias,
    out_weight,
    out_bias,
    mixed_gain,
    mixed_bias,
    expand_weight,
    expand_bias,
    shrink_weight,
    shrink_bias,
    final_gain,
    final_bias,
):
    micro, rows_dev, length, width = inputs.shape
    rows = micro * rows_dev
    groups, per, part = expand_weight.shape
    x = inputs.reshape(rows, length, width)
    docs = doc_ids.reshape(rows, 1, length)
    cot = cotangent.reshape(rows, length, width)
    ffn = lax.axis_size("ffn")
    devices = ffn * lax.axis_size("dp")
    hidden = part * ffn

    expand_got = gather_shards(expand_weight)
    shrink_got = gather_shards(shrink_weight)
    bias_all = lax.all_gather(expand_bias, "ffn", axis=1, tiled=True).astype(f32)
    q, k, v, c, p = attend(
        x, docs, query_weight, query_bias[None], key_weight, value_weight, value_bias[None]
    )
    expand_all = order_shards(expand_got)
    shrink_all = order_shards(shrink_got)
    vec = jnp.stack(
        [out_bias.astype(f32), mixed_gain, mixed_bias, shrink_bias.astype(f32), final_gain, final_bias]
        + [jnp.zeros(width, f32)] * 2
    )
    result, dh1, dc, gwo, gwe, gws, gbe, gvec = feed(
        x, c, cot, out_weight, expand_all, bias_all, shrink_all, vec
    )
    dx, gw0, gv0 = attend_back(x, q, k, v, c, dc, p, dh1, query_weight, key_weight, value_weight, 0, 2)
    dx, gw1, gv1 = attend_back(x, q, k, v, c, dc, p, dh1, query_weight, key_weight, value_weight, 1, 2, dx)

    everything = ("dp", "ffn")
    dp = devices // ffn
    shard = jnp.stack([gwe.reshape(groups, per, ffn, part).transpose(2, 0, 1, 3),
                       gws.reshape(groups, per, ffn, part).transpose(2, 0, 1, 3)], axis=1).astype(bf16)
    n = 2 * groups * per * part
    shard = shard.reshape(ffn, dp, n // dp // 128, 128).transpose(1, 0, 2, 3).reshape(devices, n // dp // 128, 128)
    mine = reduce_all(shard, everything, devices)
    ffn_grads = spread(mine.astype(bf16), "dp", dp).reshape(2, groups, per, part).astype(f32)
    grad_expand = ffn_grads[0]
    grad_shrink = ffn_grads[1].transpose(0, 2, 1)

    gw = jnp.concatenate([gw0, gw1], axis=1)
    gw = jnp.stack([gw[:, g, :, window(g, per)[1]:window(g, per)[1] + per] for g in range(groups)], axis=1)
    flat = jnp.concatenate([gwo.reshape(-1), gw.reshape(-1)]).astype(bf16)
    mine = reduce_all(flat.reshape(devices, -1), everything, devices)
    flat = spread(mine.astype(bf16), everything, devices).reshape(-1).astype(f32)
    grad_out = flat[: width * width].reshape(width, width)
    gqkv = flat[width * width :].reshape(3, groups, per, per)

    gvec2 = jnp.concatenate([gv0[:2], gv1[:2]], axis=1)
    vecs = lax.psum((gvec[:6], gvec2), everything)
    gbe = lax.psum(gbe.reshape(groups, ffn, part), "dp")
    gbe = lax.psum_scatter(gbe.transpose(1, 0, 2), "ffn", scatter_dimension=0, tiled=False)
    v6, v2 = vecs
    return (
        result.reshape(inputs.shape),
        dx.reshape(inputs.shape),
        gqkv[0],
        v2[0],
        gqkv[1],
        gqkv[2],
        v2[1],
        grad_out,
        v6[0],
        v6[1],
        v6[2],
        grad_expand,
        gbe,
        grad_shrink,
        v6[3],
        v6[4],
        v6[5],
    )


def solution(mesh):
    in_specs = (
        P(None, ("dp", "ffn"), None, None),
        P(None, ("dp", "ffn"), None),
        P(None, ("dp", "ffn"), None, None),
        P(),
        P(),
        P(),
        P(),
        P(),
        P(),
        P(),
        P(),
        P(),
        P(None, None, "ffn"),
        P(None, "ffn"),
        P(None, "ffn", None),
        P(),
        P(),
        P(),
    )
    out_specs = (
        P(None, ("dp", "ffn"), None, None),
        P(None, ("dp", "ffn"), None, None),
        P(),
        P(),
        P(),
        P(),
        P(),
        P(),
        P(),
        P(),
        P(),
        P(None, None, "ffn"),
        P(None, "ffn"),
        P(None, "ffn", None),
        P(),
        P(),
        P(),
    )
    return jax.shard_map(
        on_device, mesh=mesh, in_specs=in_specs, out_specs=out_specs, check_vma=False
    )
```

time: 1440 us -> 481 us (0.33)
  waiting for transfers between devices: 661 us -> 47.7 us
  matrix products: 383 us -> 0 us
  Pallas kernels: 0 us -> 128 us
  local copies, waits for them, and re-layouts: 192 us -> 84.2 us
  other arithmetic: 121 us -> 77.3 us
  blocking collectives: 63.3 us -> 105 us
  starting transfers between devices: 1.53 us -> 28.9 us
  between operations: 17.4 us -> 1.49 us
    reduce_scatter x8 -> x0, waiting for transfers between devices: 418 us -> none  [the longest x4 230 us: on_device(): lax.psum_scatter(grouped_back(grad_pre_low, expand_full), 'ffn', scatter_...]
    dot_general x96 -> x0, matrix products: 383 us -> none  [the longest x20 109 us: grouped(): jnp.einsum('tgi,gio->tgo', parted, weight, preferred_element_type=jnp.flo...]
    all_gather x8 -> x0, waiting for transfers between devices: 152 us -> none  [the longest x4 99.7 us: on_device(): gathered = lax.all_gather(normed_low, 'ffn', axis=0, tiled=True)]
    pallas_call x0 -> x4, Pallas kernels: none -> 128 us  [the longest x2 48.5 us: attend_back(): pl.pallas_call(kernel, grid=(rows,), in_specs=specs, out_specs=[wide, ful...]
    psum x2 -> x0, waiting for transfers between devices: 89.1 us -> none  [the longest x1 89.1 us: on_device(): lax.psum((acc_query, acc_query_bias, acc_key, acc_value, acc_value_bias,...]
    reshape x20 -> x6, local copies, waits for them, and re-layouts: 90.7 us -> 9.39 us  [the longest x2 4.41 us: on_device(): flat = jnp.concatenate([gwo.reshape(-1), gw.reshape(-1)]).astype(bf16)]
    reduce_sum x29 -> x2, other arithmetic: 70.4 us -> 5.9 us  [reduce_all(): return jnp.sum(got.astype(f32), axis=0)]
    all_to_all x0 -> x4, waiting for transfers between devices: none -> 47.7 us  [the longest x2 47.7 us: reduce_all(): got = lax.all_to_all(x, axes, 0, 0, tiled=True)]
  transfers between devices with their start and end apart: 18 -> 10, of which waited for: 16 -> 1; matrix products, arithmetic and copies ran while one was open for 14% -> 18% of each run, Pallas kernels for 0% -> 17%
where the time goes in v1:
time: 481 us; the launch traced here: 473 us
  Pallas kernels  128 us (27%)
  blocking collectives  105 us (22%)
  local copies, waits for them, and re-layouts  84.2 us (18%)
  other arithmetic  77.3 us (16%)
  waiting for transfers between devices  47.7 us (10%)
  starting transfers between devices  28.9 us (6%)
    pallas_call x2, Pallas kernels, attend_back(): pl.pallas_call(kernel, grid=(rows,), in_specs=specs, out_specs=[wide, ful...  48.5 us
    pallas_call x1, Pallas kernels, feed(): pl.pallas_call(feed_kernel, grid=(rows,), in_specs=[wide, wide, wide] + [...  48 us
    psum x1, blocking collectives, on_device(): vecs = lax.psum((gvec[:6], gvec2), everything)  47.7 us
    all_to_all x2, waiting for transfers between devices, reduce_all(): got = lax.all_to_all(x, axes, 0, 0, tiled=True)  47.7 us
    pallas_call x1, Pallas kernels, attend(): pl.pallas_call(attend_kernel, grid=(rows,), in_specs=[wide, row_spec((1,...  31.3 us
    psum x1, blocking collectives, on_device(): gbe = lax.psum(gbe.reshape(groups, ffn, part), 'dp')  30 us
    unnamed x37, local copies, waits for them, and re-layouts  24.8 us
    unnamed x1, blocking collectives  17 us
  transfers between devices with their start and end apart: 10, of which 1 were waited for; matrix products, arithmetic and copies ran while one was open for 18% of the time, Pallas kernels for 17%

profile of v1, /device:TPU:0, one launch (start us, length us, event | category | flops | bytes accessed | tf_op | source)
XLA Modules:
  0.0 472.8 jit_solution(7265799115046315757)
XLA Ops:
  1.2 2.0 collective-permute-start.2
  3.2 2.2 collective-permute-start.1
  5.4 1.7 collective-permute-start.5
  7.2 1.3 broadcast_in_dim.8.qb_ref
  8.4 1.3 broadcast_in_dim.9.vb_ref
  9.8 31.3 %attend.1 = (bf16[4,512,768]{2,1,0:T(8,128)(2,1)}, bf16[4,512,768]{2,1,0:T(8,128)(2,1)}, bf16[4,512,768]{2,1,0:T(8,128)(2,1)}, bf16[4,512,768]{2,1,0:T(8,128)(2,1)}, bf16[4,12,512,512]{3,2,1,0:T(8,128)(2,1)}) custom-call(bf16[4,512,768]{2,1,0:T(8,128)(2,1)} %bitcast.61, s32[4,1,512]{2,1,0:T(1,128)} %docs_ref.1, bf16[4,192,192]{2,1,0:T(8,128)(2,1)} %refs_8_.1, ...), custom_call_target="tpu_custom_call" | custom-call | flops 20000000000 | bytes 50000000 | tf_op jit(solution)/shard_map/attend/pallas_call | solution.py:123
  41.4 10.6 %all-gather = bf16[4,192,4]{1,2,0:T(4,128)(2,1)S(1)} all-gather(bf16[1,192,4]{1,2,0:T(4,128)(2,1)S(1)} %bitcast.59), channel_id=1, replica_groups=mesh['dp'=8,'ffn'=4] {'ffn'}, dimensions={0}, use_global_device_ids=true | all-gather | bytes 7680 | tf_op jit(solution)/shard_map/all_gather | solution.py:418
  52.0 0.7 reshape.214
  52.7 0.6 stack.95.vec_ref
  53.3 0.7 copy-done.3
  54.2 1.5 pad_maximum_fusion.2
  55.7 1.9 gather_fusion
  57.6 1.4 pad_maximum_fusion.3
  59.0 1.8 gather_fusion.1
  60.8 48.0 %feed.1 = (bf16[4,512,768]{2,1,0:T(8,128)(2,1)}, f32[4,512,768]{2,1,0:T(8,128)}, bf16[4,512,768]{2,1,0:T(8,128)(2,1)}, f32[768,768]{1,0:T(8,128)}, f32[4,192,768...) custom-call(bf16[4,512,768]{2,1,0:T(8,128)(2,1)} %bitcast.62, ...), custom_call_target="tpu_custom_call" | custom-call | flops 40000000000 | bytes 50000000 | tf_op jit(solution)/shard_map/feed/pallas_call | solution.py:237
  108.8 1.8 convert.37
  110.6 2.1 reshape.187
  112.6 1.8 convert.40
  114.4 1.4 reshape.189
  115.9 2.8 convert.41
  118.6 3.5 reshape.190
  122.1 0.6 copy_bitcast_fusion
  122.7 0.6 pad_maximum_fusion
  123.3 4.7 convert_element_type.48
  128.0 3.2 copy.61
  131.2 6.1 %all-to-all-start.2 = ((bf16[32,288,128]{2,1,0:T(8,128)(2,1)}), bf16[32,288,128]{2,1,0:T(8,128)(2,1)S(1)}, u32[]{:S(2)}, u32[]{:S(2)}) async-start(bf16[32,288,128]{2,1,0:T(8,128)(2,1)} %bitcast.45), calls=%async_computation.2 | async-start | bytes 4718592 | tf_op jit(solution)/shard_map/all_to_all | solution.py:378
  137.4 24.1 %attend_back.2 = (bf16[4,512,768]{2,1,0:T(8,128)(2,1)}, f32[3,2,192,256]{3,2,1,0:T(8,128)}, f32[8,384]{1,0:T(8,128)}) custom-call(bf16[4,512,768]{2,1,0:T(8,128)(2,1)} %bitcast.63, bf16[4,512,768]{2,1,0:T(8,128)(2,1)} %get-tuple-element.38.q_ref.refs_1_, bf16[4,512,768]{2,1,0:T(8,128)(2,1)} %get-tuple-element.39.k_ref.refs_2_, ...), custom_call_target="tpu_custom_call" | custom-call | flops 20000000000 | bytes 30000000 | tf_op jit(solution)/shard_map/attend_back/pallas_call | solution.py:344
  161.5 24.4 %attend_back.3 = (bf16[4,512,768]{2,1,0:T(8,128)(2,1)}, f32[3,2,192,256]{3,2,1,0:T(8,128)}, f32[8,384]{1,0:T(8,128)}) custom-call(bf16[4,512,768]{2,1,0:T(8,128)(2,1)} %bitcast.64, bf16[4,512,768]{2,1,0:T(8,128)(2,1)} %get-tuple-element.38.q_ref.refs_1_, bf16[4,512,768]{2,1,0:T(8,128)(2,1)} %get-tuple-element.39.k_ref.refs_2_, ...), custom_call_target="tpu_custom_call", output_to_operand_aliasing={{0}: (11, {})} | custom-call | flops 20000000000 | bytes 30000000 | tf_op jit(solution)/shard_map/attend_back/pallas_call | solution.py:344
  185.9 1.4 convert.39
  188.1 2.4 reshape.188
  190.5 3.0 pad_maximum_fusion.1
  193.4 10.0 %convert_element_type.53 = bf16[32,1,32256]{2,1,0:T(2,128)(2,1)} reshape(bf16[1032192]{0:T(1024)(128)(2,1)} %pad_maximum_fusion.1) | data formatting | bytes 4128768 | tf_op jit(solution)/shard_map/convert_element_type | solution.py:447
  203.5 0.5 broadcast.86
  204.0 14.2 %reduce.22 = bf16[32,32256]{1,0:T(8,128)(2,1)} reduce(bf16[32,1,32256]{2,1,0:T(2,128)(2,1)} %convert_element_type.53, bf16[]{:T(256)} %broadcast.86), dimensions={1}, to_apply=%convert_element_type.53.reduce_sub_computation | reduce | bytes 4128770 | tf_op jit(solution)/shard_map/convert_element_type | solution.py:447
  218.2 2.8 reshape.226
  221.0 6.1 %all-to-all-start = ((bf16[32,2,16128]{2,1,0:T(2,128)(2,1)}), bf16[32,2,16128]{2,1,0:T(2,128)(2,1)}, u32[]{:S(2)}, u32[]{:S(2)}) async-start(bf16[32,2,16128]{2,1,0:T(2,128)(2,1)} %reshape.226), calls=%async_computation | async-start | bytes 4128768 | tf_op jit(solution)/shard_map/all_to_all | solution.py:378
  227.4 47.7 %all-to-all-done = bf16[32,2,16128]{2,1,0:T(2,128)(2,1)} async-done(((bf16[32,2,16128]{2,1,0:T(2,128)(2,1)}), bf16[32,2,16128]{2,1,0:T(2,128)(2,1)}, u32[]{:S(2)}, u32[]{:S(2)}) %all-to-all-start) | async-done | bytes 2064416 | tf_op jit(solution)/shard_map/all_to_all | solution.py:378
  275.1 0.9 broadcast_in_dim.11
  276.0 3.6 all-to-all-start.3
  279.6 10.3 %reshape.227 = bf16[32,1,32256]{2,1,0:T(2,128)(2,1)} reshape(bf16[32,2,16128]{2,1,0:T(2,128)(2,1)} %all-to-all-done) | data formatting | bytes 4128768
  289.9 5.6 %reduce_sum.24 = bf16[32256]{0:T(1024)(128)(2,1)S(1)} reduce(bf16[32,1,32256]{2,1,0:T(2,128)(2,1)} %reshape.227, bf16[]{:T(256)} %constant.29.clone.1), dimensions={0,1}, to_apply=%region_0.1 | reduce | flops 999936 | bytes 2128898 | tf_op jit(solution)/shard_map/reduce_sum | solution.py:379
  295.5 4.0 broadcast_in_dim.10
  299.5 12.9 %reduce.23 = bf16[32,32256]{1,0:T(8,128)(2,1)S(1)} reduce(bf16[32,1,32256]{2,1,0:T(2,128)(2,1)} %broadcast_in_dim.10, bf16[]{:T(256)} %broadcast.86), dimensions={1}, to_apply=%broadcast_in_dim.10.reduce_sub_computation | reduce | bytes 4128770 | tf_op jit(solution)/shard_map/broadcast_in_dim | solution.py:383
  312.4 1.6 reshape.228
  314.0 6.5 %all-to-all-start.1 = ((bf16[32,2,16128]{2,1,0:T(2,128)(2,1)}), bf16[32,2,16128]{2,1,0:T(2,128)(2,1)S(1)}, u32[]{:S(2)}, u32[]{:S(2)}) async-start(bf16[32,2,16128]{2,1,0:T(2,128)(2,1)} %reshape.228), calls=%async_computation.1 | async-start | bytes 4128768 | tf_op jit(solution)/shard_map/all_to_all | solution.py:383
  320.5 0.6 dynamic-slice
  321.2 0.7 slice.101
  321.9 0.7 slice.100
  322.6 17.0 %all-reduce = f32[4,4,192]{2,1,0:T(4,128)S(1)} all-reduce(f32[4,4,192]{2,1,0:T(4,128)S(1)} %bitcast.55), channel_id=2, replica_groups=mesh['dp'=8,'ffn'=4] {'ffn'}, use_global_device_ids=true, to_apply=%region_5.6.clone | all-reduce | flops 3072 | bytes 24576
  339.6 0.6 constant_dynamic-slice_fusion
  340.3 30.0 %psum.24 = f32[1,4,192]{2,1,0:T(4,128)} all-reduce(f32[1,4,192]{2,1,0:T(4,128)S(1)} %constant_dynamic-slice_fusion), channel_id=1, replica_groups=mesh['dp'=8,'ffn'=4] {'dp'}, use_global_device_ids=true, to_apply=%region_4.5 | all-reduce | flops 768 | bytes 6144 | tf_op jit(solution)/shard_map/psum | solution.py:455
  370.3 47.7 %all-reduce.1 = (f32[2,768]{1,0:T(2,128)S(1)}, f32[6,768]{1,0:T(8,128)S(1)}) all-reduce(f32[2,768]{1,0:T(2,128)S(1)} %pad_maximum_fusion.5, f32[6,768]{1,0:T(8,128)S(1)} %bitcast.56), channel_id=1, replica_groups=mesh['dp'=8,'ffn'=4] {'dp','ffn'}, use_global_device_ids=true, to_apply=%region_1.2 | all-reduce | flops 6144 | bytes 49152 | tf_op jit(solution)/shard_map/psum | solution.py:454
  418.0 0.7 slice_reduce_fusion
  418.7 0.9 fusion.3
  419.6 1.2 squeeze.39
  420.8 1.2 copy.65
  422.0 1.1 squeeze.38
  423.1 6.6 %reshape.229 = bf16[32,1,32256]{2,1,0:T(2,128)(2,1)} reshape(bf16[32,2,16128]{2,1,0:T(2,128)(2,1)S(1)} %all-to-all-done.1) | data formatting | bytes 4128768
  429.7 12.2 %reduce.6 = bf16[32,32256]{1,0:T(8,128)(2,1)S(1)} reduce(bf16[32,1,32256]{2,1,0:T(2,128)(2,1)} %reshape.229, bf16[]{:T(256)} %constant.40), dimensions={1}, to_apply=%all_to_all.15.reduce_sub_computation | reduce | bytes 4128770 | tf_op jit(solution)/shard_map/all_to_all | solution.py:383
  441.9 14.7 %convert_reduce_fusion = f32[32,32256]{1,0:T(8,128)} fusion(bf16[32,1,32256]{2,1,0:T(2,128)(2,1)} %reshape.229), kind=kLoop, calls=%fused_computation.2 | loop fusion | flops 1032192 | bytes 6193152 | tf_op jit(solution)/shard_map/convert_element_type | solution.py:449
  456.6 4.1 convert_element_type.47
  460.8 2.8 slice_convert_fusion
  463.6 5.7 %reshape.195 = f32[28,192,192]{2,1,0:T(8,128)} reshape(f32[32,32256]{1,0:T(8,128)} %convert_reduce_fusion) | data formatting | bytes 8257536 | tf_op jit(solution)/shard_map/convert_element_type | solution.py:449
  469.3 3.1 fusion.2
  (58 shorter events, 2.1 us)
Async XLA Ops:
  0.7 40.5 %collective-permute-start = (bf16[4,192,192]{2,1,0:T(8,128)(2,1)}, bf16[4,192,192]{2,1,0:T(8,128)(2,1)S(1)}, u32[]{:S(2)}, u32[]{:S(2)}) collective-permute-start(bf16[4,192,192]{2,1,0:T(8,128)(2,1)} %param.30), channel_id=1, source_target_pairs={{0,1},{1,2},{2,3},{3,0},{4,5},{5,6},{6,7},{7,4},{8,9},{9,10},{10,1... | collective-permute-start | bytes 884744 | tf_op jit(solution)/shard_map/ppermute | solution.py:366
  1.2 52.1 %collective-permute-start.2 = (bf16[4,192,192]{2,1,0:T(8,128)(2,1)}, bf16[4,192,192]{2,1,0:T(8,128)(2,1)S(1)}, u32[]{:S(2)}, u32[]{:S(2)}) collective-permute-start(bf16[4,192,192]{2,1,0:T(8,128)(2,1)} %param.30), channel_id=1, source_target_pairs={{0,3},{1,0},{2,1},{3,2},{4,7},{5,4},{6,5},{7,6},{8,11},{9,8},{10,9... | collective-permute-start | bytes 884744 | tf_op jit(solution)/shard_map/ppermute | solution.py:366
  3.2 50.1 %collective-permute-start.1 = (bf16[4,192,192]{2,1,0:T(8,128)(2,1)}, bf16[4,192,192]{2,1,0:T(8,128)(2,1)S(1)}, u32[]{:S(2)}, u32[]{:S(2)}) collective-permute-start(bf16[4,192,192]{2,1,0:T(8,128)(2,1)} %param.30), channel_id=1, source_target_pairs={{0,2},{1,3},{2,0},{3,1},{4,6},{5,7},{6,4},{7,5},{8,10},{9,11},{10,... | collective-permute-start | bytes 884744 | tf_op jit(solution)/shard_map/ppermute | solution.py:366
  5.4 52.1 %collective-permute-start.3 = (bf16[4,192,192]{2,1,0:T(8,128)(2,1)}, bf16[4,192,192]{2,1,0:T(8,128)(2,1)S(1)}, u32[]{:S(2)}, u32[]{:S(2)}) collective-permute-start(bf16[4,192,192]{2,1,0:T(8,128)(2,1)} %param.32), channel_id=1, source_target_pairs={{0,1},{1,2},{2,3},{3,0},{4,5},{5,6},{6,7},{7,4},{8,9},{9,10},{10,1... | collective-permute-start | bytes 884744 | tf_op jit(solution)/shard_map/ppermute | solution.py:366
  5.4 52.1 %collective-permute-start.5 = (bf16[4,192,192]{2,1,0:T(8,128)(2,1)}, bf16[4,192,192]{2,1,0:T(8,128)(2,1)S(1)}, u32[]{:S(2)}, u32[]{:S(2)}) collective-permute-start(bf16[4,192,192]{2,1,0:T(8,128)(2,1)} %param.32), channel_id=1, source_target_pairs={{0,3},{1,0},{2,1},{3,2},{4,7},{5,4},{6,5},{7,6},{8,11},{9,8},{10,9... | collective-permute-start | bytes 884744 | tf_op jit(solution)/shard_map/ppermute | solution.py:366
  9.7 31.4 %copy-start.2 = (bf16[4,192,192]{2,1,0:T(8,128)(2,1)S(1)}, bf16[4,192,192]{2,1,0:T(8,128)(2,1)}, u32[]{:S(2)}) copy-start(bf16[4,192,192]{2,1,0:T(8,128)(2,1)} %param.32) | copy-start | bytes 884740
  9.7 31.6 %copy-start.12 = (bf16[768]{0:T(1024)(128)(2,1)S(1)}, bf16[768]{0:T(1024)(128)(2,1)}, u32[]{:S(2)}) copy-start(bf16[768]{0:T(1024)(128)(2,1)} %param.27) | copy-start | bytes 4612
  9.7 31.6 %copy-start.7 = (f32[768]{0:T(1024)S(1)}, f32[768]{0:T(1024)}, u32[]{:S(2)}) copy-start(f32[768]{0:T(1024)} %param.28) | copy-start | bytes 9220
  9.7 31.6 %copy-start.8 = (f32[768]{0:T(1024)S(1)}, f32[768]{0:T(1024)}, u32[]{:S(2)}) copy-start(f32[768]{0:T(1024)} %param.29) | copy-start | bytes 9220
  9.7 31.6 %copy-start.13 = (bf16[768]{0:T(1024)(128)(2,1)S(1)}, bf16[768]{0:T(1024)(128)(2,1)}, u32[]{:S(2)}) copy-start(bf16[768]{0:T(1024)(128)(2,1)} %param.33) | copy-start | bytes 4612
  9.7 31.6 %copy-start.9 = (f32[768]{0:T(1024)S(1)}, f32[768]{0:T(1024)}, u32[]{:S(2)}) copy-start(f32[768]{0:T(1024)} %param.34) | copy-start | bytes 9220
  9.7 31.6 %copy-start.10 = (f32[768]{0:T(1024)S(1)}, f32[768]{0:T(1024)}, u32[]{:S(2)}) copy-start(f32[768]{0:T(1024)} %param.35) | copy-start | bytes 9220
  9.7 31.6 %copy-start.11 = (bf16[4,192]{1,0:T(4,128)(2,1)S(1)}, bf16[4,192]{1,0:T(4,128)(2,1)}, u32[]{:S(2)}) copy-start(bf16[4,192]{1,0:T(4,128)(2,1)} %param.31) | copy-start | bytes 4612
  9.8 44.4 %copy-start.1 = (bf16[4,192,192]{2,1,0:T(8,128)(2,1)S(1)}, bf16[4,192,192]{2,1,0:T(8,128)(2,1)}, u32[]{:S(2)}) copy-start(bf16[4,192,192]{2,1,0:T(8,128)(2,1)} %param.30) | copy-start | bytes 884740
  41.1 16.4 %collective-permute-start.4 = (bf16[4,192,192]{2,1,0:T(8,128)(2,1)S(1)}, bf16[4,192,192]{2,1,0:T(8,128)(2,1)}, u32[]{:S(2)}, u32[]{:S(2)}) collective-permute-start(bf16[4,192,192]{2,1,0:T(8,128)(2,1)S(1)} %copy-done.2), channel_id=1, source_target_pairs={{0,2},{1,3},{2,0},{3,1},{4,6},{5,7},{6,4},{7,5},{8,10},{9,11},{10,... | collective-permute-start | bytes 884744 | tf_op jit(solution)/shard_map/ppermute | solution.py:366
  53.3 0.7 copy-start.3
  53.3 0.9 copy-start.4
  131.2 89.8 %all-to-all-start.2 = ((bf16[32,288,128]{2,1,0:T(8,128)(2,1)}), bf16[32,288,128]{2,1,0:T(8,128)(2,1)S(1)}, u32[]{:S(2)}, u32[]{:S(2)}) async-start(bf16[32,288,128]{2,1,0:T(8,128)(2,1)} %bitcast.45), calls=%async_computation.2 | async-start | bytes 4718592 | tf_op jit(solution)/shard_map/all_to_all | solution.py:378
  185.9 1.6 copy-start
  221.0 54.1 %all-to-all-start = ((bf16[32,2,16128]{2,1,0:T(2,128)(2,1)}), bf16[32,2,16128]{2,1,0:T(2,128)(2,1)}, u32[]{:S(2)}, u32[]{:S(2)}) async-start(bf16[32,2,16128]{2,1,0:T(2,128)(2,1)} %reshape.226), calls=%async_computation | async-start | bytes 4128768 | tf_op jit(solution)/shard_map/all_to_all | solution.py:378
  276.0 38.0 %all-to-all-start.3 = ((bf16[8,288,128]{2,1,0:T(8,128)(2,1)}), bf16[8,288,128]{2,1,0:T(8,128)(2,1)S(1)}, u32[]{:S(2)}, u32[]{:S(2)}) async-start(bf16[8,288,128]{2,1,0:T(8,128)(2,1)} %broadcast_in_dim.11), calls=%async_computation.3 | async-start | bytes 1179648 | tf_op jit(solution)/shard_map/all_to_all | solution.py:383
  314.0 6.5 %copy-start.14 = (u32[32]{0:T(128)S(1)}, u32[32]{0:T(128)}, u32[]{:S(2)}) copy-start(u32[32]{0:T(128)} %constant.35) | copy-start | bytes 388
  314.0 7.1 %copy-start.6 = (f32[4,768]{1,0:T(4,128)S(1)}, f32[4,768]{1,0:T(4,128)}, u32[]{:S(2)}) copy-start(f32[4,768]{1,0:T(4,128)} %get-tuple-element.54) | copy-start | bytes 36868
  314.0 56.3 %copy-start.5 = (f32[8,768]{1,0:T(8,128)S(1)}, f32[8,768]{1,0:T(8,128)}, u32[]{:S(2)}) copy-start(f32[8,768]{1,0:T(8,128)} %get-tuple-element.51) | copy-start | bytes 73732
  314.0 109.1 %all-to-all-start.1 = ((bf16[32,2,16128]{2,1,0:T(2,128)(2,1)}), bf16[32,2,16128]{2,1,0:T(2,128)(2,1)S(1)}, u32[]{:S(2)}, u32[]{:S(2)}) async-start(bf16[32,2,16128]{2,1,0:T(2,128)(2,1)} %reshape.228), calls=%async_computation.1 | async-start | bytes 4128768 | tf_op jit(solution)/shard_map/all_to_all | solution.py:383

commit v2 on v1

v2 whole, which is shorter than its diff:
```python
import functools

import jax
import jax.numpy as jnp
from jax import lax
from jax.experimental import pallas as pl
from jax.experimental.pallas import tpu as pltpu
from jax.sharding import PartitionSpec as P

HEADS = 12
HEAD = 64
epsilon = 1e-05
masked_score = -1e30
bf16 = jnp.bfloat16
f32 = jnp.float32
VMEM_LIMIT = 60 * 1024 * 1024

OUT_BIAS, MIXED_GAIN, MIXED_BIAS, SHRINK_BIAS, FINAL_GAIN, FINAL_BIAS, QUERY_BIAS, VALUE_BIAS = range(8)

NN = (((1,), (0,)), ((), ()))
NT = (((1,), (1,)), ((), ()))
TN = (((0,), (0,)), ((), ()))


def dot(a, b, dims=NN):
    return lax.dot_general(a, b, dims, preferred_element_type=f32)


def window(group, width):
    start = group * width
    base = start // 128 * 128
    return base, start - base


def shift_matrix(rows, cols, offset, low=0):
    r = lax.broadcasted_iota(jnp.int32, (rows, cols), 0) + offset
    c = lax.broadcasted_iota(jnp.int32, (rows, cols), 1)
    return jnp.where((c == r) & (c >= low), 1.0, 0.0).astype(bf16)


def as_row(ref):
    return ref[...].astype(f32).reshape(1, ref.shape[0])


def pad_cols(w, offset):
    return dot(w, shift_matrix(w.shape[1], 256, offset)).astype(bf16)


def pad_rows(w, offset):
    rows = w.shape[0]
    parts = []
    if offset:
        parts.append(jnp.zeros((offset, w.shape[1]), bf16))
    parts.append(w)
    if 256 - offset - rows:
        parts.append(jnp.zeros((256 - offset - rows, w.shape[1]), bf16))
    return jnp.concatenate(parts, axis=0)


def join_windows(parts):
    out = []
    for i in range(0, len(parts), 2):
        a, b = parts[i], parts[i + 1]
        out += [a[:, :128], a[:, 128:] + b[:, :128], b[:, 128:]]
    return out


def attend_kernel(x_ref, docs_ref, wq_ref, wk_ref, wv_ref, qb_ref, vb_ref,
                  q_ref, k_ref, v_ref, c_ref, p_ref, wpad, bias_ref):
    length = x_ref.shape[1]
    width = x_ref.shape[2]
    groups = wq_ref.shape[0]
    per = width // groups

    @pl.when(pl.program_id(0) == 0)
    def _():
        for j, w_ref in enumerate((wq_ref, wk_ref, wv_ref)):
            for g in range(groups):
                _, off = window(g, per)
                wpad[j, g] = pad_rows(pad_cols(w_ref[g], off), off)

    for j, (out, b_ref) in enumerate(((q_ref, qb_ref), (k_ref, None), (v_ref, vb_ref))):
        bias = None if b_ref is None else as_row(b_ref)
        parts = []
        for g in range(groups):
            base, _ = window(g, per)
            parts.append(dot(x_ref[0, :, base:base + 256], wpad[j, g]))
        for n, col in enumerate(join_windows(parts)):
            if bias is not None:
                col = col + bias[:, 128 * n:128 * n + 128]
            out[0, :, 128 * n:128 * n + 128] = col.astype(bf16)

    docs = docs_ref[0].astype(f32)
    down = jnp.transpose(jnp.broadcast_to(docs, (128, length)))[:, :1]
    bias_ref[...] = jnp.where(down == docs, 0.0, masked_score)
    low = lax.broadcasted_iota(jnp.int32, (1, 128), 1) < HEAD
    for pair in range(HEADS // 2):
        lanes = slice(128 * pair, 128 * pair + 128)
        q2 = q_ref[0, :, lanes] * bf16(HEAD ** -0.5)
        k2 = k_ref[0, :, lanes]
        v2 = v_ref[0, :, lanes]
        acc = None
        for h in range(2):
            half = low if h == 0 else jnp.logical_not(low)
            km = jnp.where(half, k2, bf16(0))
            vm = jnp.where(half, v2, bf16(0))
            s = dot(q2, km, NT) + bias_ref[...]
            top = jnp.max(s, axis=-1, keepdims=True)
            e = jnp.exp(s - top)
            total = jnp.sum(e, axis=-1, keepdims=True)
            pr = (e * (1.0 / total)).astype(bf16)
            p_ref[0, 2 * pair + h] = pr
            c = dot(pr, vm)
            acc = c if acc is None else acc + c
        c_ref[0, :, lanes] = acc.astype(bf16)


def full(shape):
    return pl.BlockSpec(shape, lambda *_: (0,) * len(shape))


def row_spec(shape):
    return pl.BlockSpec((1,) + shape, lambda r: (r,) + (0,) * len(shape))


def attend(x, docs, wq, wk, wv, qb, vb):
    rows, length, width = x.shape
    wide = row_spec((length, width))
    low = jax.ShapeDtypeStruct((rows, length, width), bf16)
    return pl.pallas_call(
        attend_kernel,
        grid=(rows,),
        in_specs=[wide, row_spec((1, length)), full(wq.shape), full(wk.shape), full(wv.shape),
                  whole(), whole()],
        out_specs=[wide, wide, wide, wide, row_spec((HEADS, length, length))],
        out_shape=[low, low, low, low, jax.ShapeDtypeStruct((rows, HEADS, length, length), bf16)],
        scratch_shapes=[pltpu.VMEM((3, wq.shape[0], 256, 256), bf16), pltpu.VMEM((length, length), f32)],
        compiler_params=pltpu.CompilerParams(vmem_limit_bytes=VMEM_LIMIT),
        cost_estimate=pl.CostEstimate(flops=int(2e10), bytes_accessed=int(5e7), transcendentals=0),
        name="attend",
    )(x, docs, wq, wk, wv, qb, vb)


def gelu_both(u):
    cdf = 0.5 * (1.0 + lax.erf(u * 0.7071067811865476))
    pdf = jnp.exp(-0.5 * u * u) * 0.3989422804014327
    return u * cdf, cdf + u * pdf


def low_half():
    return lax.broadcasted_iota(jnp.int32, (1, 128), 1) < 64


def shard_lanes(pos, part):
    start = pos * part
    if start % 128 == 0:
        return start, start + 128
    return start + 64, start - 64


def both_halves(a, b, odd):
    if odd:
        return jnp.where(low_half(), pltpu.roll(a, 64, 1), b)
    return jnp.where(low_half(), a, pltpu.roll(b, 64, 1))


def feed_kernel(me_ref, x_ref, c_ref, e_ref, wo_ref, w0_ref, w1_ref, w2_ref, w3_ref, ob_ref, mg_ref, mb_ref, sb_ref, fg_ref, fb_ref,
                result_ref, dh1_ref, dc_ref, near_e, far_e, send_e, keep_w, send_w, gvec_ref, gbe_ref,
                wepad, wspad, be_s, act, slope, pre_low, df_low, gwo_ref, gwe_ref, gws_ref):
    step = pl.program_id(0)
    groups, width = w0_ref.shape[0], x_ref.shape[2]
    per = width // groups
    part = w0_ref.shape[2] // 2
    hidden = 4 * part
    mine_y = me_ref[0] // 2
    mine_c = me_ref[0] % 2

    @pl.when(step == 0)
    def _():
        gwo_ref[...] = jnp.zeros(gwo_ref.shape, f32)
        gwe_ref[...] = jnp.zeros(gwe_ref.shape, f32)
        gws_ref[...] = jnp.zeros(gws_ref.shape, f32)
        gbe_ref[...] = jnp.zeros(gbe_ref.shape, f32)
        gvec_ref[...] = jnp.zeros(gvec_ref.shape, f32)
        for g in range(groups):
            _, off = window(g, per)
            wide, tall, bias = [], [], []
            for pos in range(4):
                y, dc = pos % 2, pos // 2
                near, far = ((w0_ref, w2_ref), (w1_ref, w3_ref))[dc]
                own = mine_y == y
                blk = jnp.where(own, near[g], far[g])
                e = blk[:per, :256].astype(f32)[:, :part]
                s_ = dot(blk[:part, 128:], shift_matrix(256, 256, off - 64, off)).astype(bf16)
                b = blk[per:, :256].astype(f32)[:1, :part]
                if pos % 2:
                    wide += [e[:, 128:], e[:, :128]]
                    tall += [s_[128:], s_[:128]]
                    bias += [b[:, 128:], b[:, :128]]
                else:
                    wide.append(e)
                    tall.append(s_)
                    bias.append(b)
            wepad[g] = pad_rows(jnp.concatenate(wide, axis=1).astype(bf16), off)
            wspad[g] = jnp.concatenate(tall, axis=0)
            be_s[g:g + 1] = jnp.concatenate(bias, axis=1)

    out_bias, mixed_gain, mixed_bias = as_row(ob_ref), as_row(mg_ref), as_row(mb_ref)
    shrink_bias, final_gain, final_bias = as_row(sb_ref), as_row(fg_ref), as_row(fb_ref)
    h1 = x_ref[0].astype(f32) + dot(c_ref[0], wo_ref[...]) + out_bias
    cen = h1 - jnp.mean(h1, axis=-1, keepdims=True)
    rstd1 = lax.rsqrt(jnp.mean(cen * cen, axis=-1, keepdims=True) + epsilon)
    xhat1 = cen * rstd1
    a = xhat1 * mixed_gain + mixed_bias
    a_low = a.astype(bf16)
    pre_low[...] = a_low

    parts = []
    for g in range(groups):
        base, _ = window(g, per)
        for n in range(hidden // 256):
            cols = slice(256 * n, 256 * n + 256)
            u = dot(pre_low[:, base:base + 256], wepad[g, :, cols]) + be_s[g:g + 1, cols]
            val, slp = gelu_both(u)
            act[g, :, cols] = val.astype(bf16)
            slope[g, :, cols] = slp
        parts.append(dot(act[g], wspad[g]))
    f = jnp.concatenate(join_windows(parts), axis=1)
    h2 = a + f + shrink_bias
    cen = h2 - jnp.mean(h2, axis=-1, keepdims=True)
    rstd2 = lax.rsqrt(jnp.mean(cen * cen, axis=-1, keepdims=True) + epsilon)
    xhat2 = cen * rstd2
    result_ref[0] = (xhat2 * final_gain + final_bias).astype(bf16)

    up = e_ref[0].astype(f32)
    gvec_ref[4:5] += jnp.sum(up * xhat2, axis=0, keepdims=True)
    gvec_ref[5:6] += jnp.sum(up, axis=0, keepdims=True)
    dx = up * final_gain
    dh2 = rstd2 * (dx - jnp.mean(dx, axis=-1, keepdims=True) - xhat2 * jnp.mean(dx * xhat2, axis=-1, keepdims=True))
    gvec_ref[3:4] += jnp.sum(dh2, axis=0, keepdims=True)
    df_low[...] = dh2.astype(bf16)
    a_t = jnp.transpose(a_low)
    df_t = jnp.transpose(df_low[...])
    parts = []
    for g in range(groups):
        base, _ = window(g, per)
        rows = slice(per * g, per * g + per)
        gws_ref[g] += dot(df_t[rows], act[g])
        acc = None
        for n in range(hidden // 256):
            cols = slice(256 * n, 256 * n + 256)
            dg = dot(df_low[:, base:base + 256], wspad[g, cols, :], NT)
            du = (dg * slope[g, :, cols]).astype(bf16)
            gbe_ref[g:g + 1, cols] += jnp.sum(du.astype(f32), axis=0, keepdims=True)
            gwe_ref[g, :, cols] += dot(a_t[rows], du)
            da = dot(du, wepad[g, :, cols], NT)
            acc = da if acc is None else acc + da
        parts.append(acc)
    da = dh2 + jnp.concatenate(join_windows(parts), axis=1)
    gvec_ref[1:2] += jnp.sum(da * xhat1, axis=0, keepdims=True)
    gvec_ref[2:3] += jnp.sum(da, axis=0, keepdims=True)
    dx = da * mixed_gain
    dh1 = rstd1 * (dx - jnp.mean(dx, axis=-1, keepdims=True) - xhat1 * jnp.mean(dx * xhat1, axis=-1, keepdims=True))
    gvec_ref[0:1] += jnp.sum(dh1, axis=0, keepdims=True)
    dh1_ref[0] = dh1
    dy = dh1.astype(bf16)
    gwo_ref[...] += dot(jnp.transpose(c_ref[0]), dy)
    dc_ref[0] = dot(dy, wo_ref[...], NT).astype(bf16)

    @pl.when(step == pl.num_programs(0) - 1)
    def _():
        half = width // 2
        for n in range(3):
            a = gwo_ref[:, 128 * n:128 * n + 128].astype(bf16)
            b = gwo_ref[:, half + 128 * n:half + 128 * n + 128].astype(bf16)
            first = mine_c == 0
            keep_w[width * n:width * n + width] = jnp.where(first, a, b)
            send_w[width * n:width * n + width] = jnp.where(first, b, a)
        for pos in range(4):
            near = mine_y == pos % 2
            base = jnp.where(near, 0, send_e.shape[0] // 2)
            most, rest = shard_lanes(pos, part)
            for i in range(groups):
                acc, g = ((gwe_ref, 2 * i) if 2 * i < groups else (gws_ref, 2 * i - groups))
                tiles = (acc[g, :, most:most + 128], acc[g + 1, :, most:most + 128], both_halves(
                    acc[g, :, rest:rest + 128], acc[g + 1, :, rest:rest + 128], pos % 2))
                for n, tile in enumerate(tiles):
                    first = per * (3 * i + n)
                    tile = tile.astype(bf16)
                    if pos // 2:
                        send_e[pl.ds(pl.multiple_of(base + first, 16), per)] = tile
                    else:
                        @pl.when(near)
                        def _():
                            near_e[first:first + per] = tile

                        @pl.when(jnp.logical_not(near))
                        def _():
                            far_e[first:first + per] = tile


def whole():
    return pl.BlockSpec(memory_space=pltpu.VMEM)


def feed(me, x, c, e, wo, shards, vectors):
    rows, length, width = x.shape
    groups = shards[0].shape[0]
    part = shards[0].shape[2] // 2
    hidden = 4 * part
    per = width // groups
    wide = row_spec((length, width))
    low = jax.ShapeDtypeStruct((rows, length, width), bf16)
    half_e = jax.ShapeDtypeStruct((groups * 3 * per, 128), bf16)
    flat_e = jax.ShapeDtypeStruct((2 * groups * 3 * per, 128), bf16)
    flat_w = jax.ShapeDtypeStruct((3 * width, 128), bf16)
    return pl.pallas_call(
        feed_kernel,
        grid=(rows,),
        in_specs=[pl.BlockSpec(memory_space=pltpu.SMEM), wide, wide, wide] + [whole()] * 11,
        out_specs=[wide, wide, wide] + [whole()] * 7,
        out_shape=[low, jax.ShapeDtypeStruct((rows, length, width), f32), low, half_e, half_e, flat_e, flat_w, flat_w,
                   jax.ShapeDtypeStruct((8, width), f32), jax.ShapeDtypeStruct((8, hidden), f32)],
        scratch_shapes=[
            pltpu.VMEM((groups, 256, hidden), bf16),
            pltpu.VMEM((groups, hidden, 256), bf16),
            pltpu.VMEM((8, hidden), f32),
            pltpu.VMEM((groups, length, hidden), bf16),
            pltpu.VMEM((groups, length, hidden), f32),
            pltpu.VMEM((length, width), bf16),
            pltpu.VMEM((length, width), bf16),
            pltpu.VMEM((width, width), f32),
            pltpu.VMEM((groups, per, hidden), f32),
            pltpu.VMEM((groups, per, hidden), f32),
        ],
        compiler_params=pltpu.CompilerParams(vmem_limit_bytes=VMEM_LIMIT),
        cost_estimate=pl.CostEstimate(flops=int(4e10), bytes_accessed=int(5e7), transcendentals=0),
        name="feed",
    )(me, x, c, e, wo, *shards, *vectors)


def attend_back_kernel(lanes_in, per, x_ref, q_ref, k_ref, v_ref, c_ref, dc_ref, p_ref, me_ref, vec_ref, gbe_ref,
                       prev_ref, dqkv_ref, out_ref, send_ref, gacc, gvec_ref, flat_ref):
    step = pl.program_id(0)
    groups = lanes_in // per

    @pl.when(step == 0)
    def _():
        gacc[...] = jnp.zeros(gacc.shape, f32)
        gvec_ref[...] = jnp.zeros(gvec_ref.shape, f32)

    low = lax.broadcasted_iota(jnp.int32, (1, 128), 1) < HEAD
    for pair in range(lanes_in // 128):
        lanes = slice(128 * pair, 128 * pair + 128)
        q2 = q_ref[0, :, lanes] * bf16(HEAD ** -0.5)
        k2 = k_ref[0, :, lanes]
        v2 = v_ref[0, :, lanes]
        dc2 = dc_ref[0, :, lanes]
        prod = dc2.astype(f32) * c_ref[0, :, lanes].astype(f32)
        dq = dk = dv = None
        for h in range(2):
            half = low if h == 0 else jnp.logical_not(low)
            km = jnp.where(half, k2, bf16(0))
            qm = jnp.where(half, q2, bf16(0))
            dcm = jnp.where(half, dc2, bf16(0))
            delta = jnp.sum(jnp.where(half, prod, 0.0), axis=-1, keepdims=True)
            pr = p_ref[0, 2 * pair + h]
            dp = dot(dcm, v2, NT)
            ds = (pr.astype(f32) * (dp - delta)).astype(bf16)
            a = dot(ds, km)
            b = dot(ds, qm, TN)
            c = dot(pr, dcm, TN)
            dq = a if dq is None else dq + a
            dk = b if dk is None else dk + b
            dv = c if dv is None else dv + c
        dq = (dq * (HEAD ** -0.5)).astype(bf16)
        dk = dk.astype(bf16)
        dv = dv.astype(bf16)
        dqkv_ref[0, 0, :, lanes] = dq
        dqkv_ref[0, 1, :, lanes] = dk
        dqkv_ref[0, 2, :, lanes] = dv
        gvec_ref[0:1, lanes] += jnp.sum(dq.astype(f32), axis=0, keepdims=True)
        gvec_ref[1:2, lanes] += jnp.sum(dv.astype(f32), axis=0, keepdims=True)

    x_t = jnp.transpose(x_ref[0])
    for g in range(groups):
        base, _ = window(g, per)
        for j in range(3):
            gacc[j, g] += dot(x_t[per * g:per * g + per], dqkv_ref[0, j, :, base:base + 256])

    @pl.when(step == pl.num_programs(0) - 1)
    def _():
        base = 0
        if prev_ref is not None:
            base = prev_ref.shape[0]
            flat_ref[:base] = prev_ref[...]
        for j in range(3):
            a, b = gacc[j, 0], gacc[j, 1]
            cols = (a[:, :128], jnp.where(low, a[:, 128:], b[:, :128]), b[:, 128:])
            for n, col in enumerate(cols):
                first = base + per * (3 * j + n)
                flat_ref[first:first + per] = col.astype(bf16)
        first = base + 9 * per
        bits = [gvec_ref[:, 128 * n:128 * n + 128] for n in range(3)] + [jnp.zeros((8, 128), f32)]
        if vec_ref is not None:
            bits += [vec_ref[:, 128 * n:128 * n + 128] for n in range(vec_ref.shape[1] // 128)]
            part = gbe_ref.shape[1] // 4
            same = me_ref[0] % 2 == 0
            for f in range(4):
                y, core = f // 2, f % 2
                near = [gbe_ref[:, lane:lane + 128] for lane in shard_lanes(y + 2 * core, part)]
                far = [gbe_ref[:, lane:lane + 128] for lane in shard_lanes(y + 2 * (1 - core), part)]
                most, rest = (jnp.where(same, a, b) for a, b in zip(near, far))
                bits += [most, pltpu.roll(rest, 64, 1) if y else rest]
        left = flat_ref.shape[0] - first - 8 * len(bits)
        if left:
            bits.append(jnp.zeros((left, 128), f32))
        flat_ref[first:] = jnp.concatenate(bits, axis=0).astype(bf16)
        if send_ref is None:
            out_ref[...] = flat_ref[...]
        else:
            half = out_ref.shape[0]
            core = me_ref[0] % 2
            out_ref[...] = flat_ref[pl.ds(pl.multiple_of(core * half, 16), half)]
            send_ref[...] = flat_ref[pl.ds(pl.multiple_of((1 - core) * half, 16), half)]


def unused():
    return pl.BlockSpec(memory_space=pl.ANY)


def call_sum(kernel, args, shape, after):
    count = len(args)
    return pl.pallas_call(
        lambda *refs: kernel(*refs[:count], *refs[count + len(after):]),
        in_specs=[whole()] * count + [unused()] * len(after),
        out_specs=whole(),
        out_shape=jax.ShapeDtypeStruct(shape, bf16),
        compiler_params=pltpu.CompilerParams(vmem_limit_bytes=VMEM_LIMIT),
        name="add_up",
    )(*args, *after)


def add(arrays, halves=None, after=()):
    shape = arrays[0].shape
    starts = [(n or 0) * shape[0] for n in halves or [0] * len(arrays)]

    def kernel(*refs):
        acc = None
        for first, ref in zip(starts, refs):
            term = ref[first:first + shape[0]].astype(f32)
            acc = term if acc is None else acc + term
        refs[-1][...] = acc.astype(bf16)

    return call_sum(kernel, arrays, shape, after)


def total(x, after=(), copies=0):
    shape = x.shape[1:]

    def kernel(x_ref, o_ref):
        acc = x_ref[0].astype(f32)
        for n in range(1, x_ref.shape[0]):
            acc = acc + x_ref[n].astype(f32)
        acc = acc.astype(bf16)
        if copies:
            for n in range(copies):
                o_ref[n] = acc
        else:
            o_ref[...] = acc

    return call_sum(kernel, (x,), (copies,) + shape if copies else shape, after)


def attend_back(x, q, k, v, c, dc, p, part, me, per, vec=None, gbe=None, prev=None, devices=1, after=()):
    rows, length, width = x.shape
    lanes = width // 2
    heads = HEADS // 2
    wide = pl.BlockSpec((1, length, lanes), lambda r: (r, 0, part))
    args = [x, q, k, v, c, dc, p, me]
    specs = [wide] * 6 + [pl.BlockSpec((1, heads, length, length), lambda r: (r, part, 0, 0)),
                          pl.BlockSpec(memory_space=pltpu.SMEM)]
    flat = 9 * per + 32
    dqkv = jax.ShapeDtypeStruct((rows, 3, length, lanes), bf16)
    if prev is None:
        args += [vec, gbe]
        specs += [whole(), whole()]
        flat += 8 * (width // 128) + 64
        outs = [jax.ShapeDtypeStruct((flat, 128), bf16)]
        pick = lambda refs: (refs[8], refs[9], None) + refs[10:12] + (None,) + refs[12:]
    else:
        args.append(prev)
        specs.append(whole())
        flat = -(-(prev.shape[0] + flat) // (8 * devices)) * 8 * devices
        outs = [jax.ShapeDtypeStruct((flat // 2, 128), bf16)] * 2
        pick = lambda refs: (None, None, refs[8]) + refs[9:]
    return pl.pallas_call(
        lambda *refs: attend_back_kernel(lanes, per, *refs[:8], *pick(refs[:len(args)] + refs[len(args) + len(after):])),
        grid=(rows,),
        in_specs=specs + [unused()] * len(after),
        out_specs=[pl.BlockSpec((1, 3, length, lanes), lambda r: (r, 0, 0, 0))] + [whole()] * len(outs),
        out_shape=[dqkv] + outs,
        scratch_shapes=[
            pltpu.VMEM((3, lanes // per, per, 256), f32),
            pltpu.VMEM((8, lanes), f32),
            pltpu.VMEM((flat, 128), bf16),
        ],
        compiler_params=pltpu.CompilerParams(vmem_limit_bytes=VMEM_LIMIT),
        cost_estimate=pl.CostEstimate(flops=int(2e10), bytes_accessed=int(3e7), transcendentals=0),
        name="attend_back",
    )(*args, *after)


def input_grad_kernel(dh1_ref, d0_ref, d1_ref, wq_ref, wk_ref, wv_ref, dx_ref, wpad):
    groups, per = wq_ref.shape[0], wq_ref.shape[1]

    @pl.when(pl.program_id(0) == 0)
    def _():
        for j, w_ref in enumerate((wq_ref, wk_ref, wv_ref)):
            for g in range(groups):
                _, off = window(g, per)
                wpad[j, g] = pad_rows(pad_cols(w_ref[g], off), off)

    half = d0_ref.shape[3]
    parts = []
    for g in range(groups):
        base, _ = window(g, per)
        d_ref = (d0_ref, d1_ref)[base // half]
        acc = None
        for j in range(3):
            t = dot(d_ref[0, j, :, base % half:base % half + 256], wpad[j, g], NT)
            acc = t if acc is None else acc + t
        parts.append(acc)
    for n, col in enumerate(join_windows(parts)):
        lanes = slice(128 * n, 128 * n + 128)
        dx_ref[0, :, lanes] = (col + dh1_ref[0, :, lanes]).astype(bf16)


def input_grad(dh1, d0, d1, wq, wk, wv, after=()):
    rows, length, width = dh1.shape
    wide = row_spec((length, width))
    back = pl.BlockSpec((1, 3, length, width // 2), lambda r: (r, 0, 0, 0))
    count = 6
    return pl.pallas_call(
        lambda *refs: input_grad_kernel(*refs[:count], *refs[count + len(after):]),
        grid=(rows,),
        in_specs=[wide, back, back] + [full(wq.shape)] * 3 + [unused()] * len(after),
        out_specs=wide,
        out_shape=jax.ShapeDtypeStruct((rows, length, width), bf16),
        scratch_shapes=[pltpu.VMEM((3, wq.shape[0], 256, 256), bf16)],
        compiler_params=pltpu.CompilerParams(vmem_limit_bytes=VMEM_LIMIT),
        cost_estimate=pl.CostEstimate(flops=int(1e10), bytes_accessed=int(2e7), transcendentals=0),
        name="input_grad",
    )(dh1, d0, d1, wq, wk, wv, *after)


def unpack_kernel(order, me_ref, *refs):
    count = len(order)
    pieces, w_ref, own_ref, other_ref = refs[:count], *refs[count:count + 3]
    refs = refs[1:]
    gexp_ref, gshr_ref, gout_ref, gq_ref, gk_ref, gv_ref, gbe_ref = refs[count + 2:count + 9]
    vecs, (e_ref, flat_w, q_ref) = refs[count + 9:count + 17], refs[count + 17:]
    groups, per = gq_ref.shape[0], gq_ref.shape[1]
    width = gout_ref.shape[0]
    part = gexp_ref.shape[2]
    size = pieces[0].shape[0]
    for bit, piece in zip(order, pieces):
        place = pl.multiple_of((me_ref[1] ^ bit) * size, 8)
        e_ref[pl.ds(place, size)] = piece[...].astype(f32)
    size = w_ref.shape[1]
    for i in range(w_ref.shape[0]):
        place = i % 2 * (flat_w.shape[0] // 2) + i // 2 * size
        flat_w[place:place + size] = w_ref[i].astype(f32)
    for i in range(groups):
        first = 3 * per * i
        a = e_ref[first:first + per]
        b = e_ref[first + per:first + 2 * per]
        mix = e_ref[first + 2 * per:first + 3 * per]
        one = jnp.concatenate([a, mix], axis=1)
        two = jnp.concatenate([b, pltpu.roll(mix, 64, 1)], axis=1)
        if 2 * i < groups:
            gexp_ref[2 * i] = one[:, :part]
            gexp_ref[2 * i + 1] = two[:, :part]
        else:
            gshr_ref[2 * i - groups] = jnp.transpose(one)[:part]
            gshr_ref[2 * i - groups + 1] = jnp.transpose(two)[:part]
    half = own_ref.shape[0]
    core = me_ref[0] % 2
    q_ref[pl.ds(pl.multiple_of(core * half, 16), half)] = own_ref[...]
    q_ref[pl.ds(pl.multiple_of((1 - core) * half, 16), half)] = other_ref[...]
    for n in range(width // 128):
        gout_ref[:, 128 * n:128 * n + 128] = flat_w[width * n:width * n + width]
    tiles = width // 128
    used = 9 * per + 32
    start = used + 8 * tiles + 64
    got = {n: [] for n in range(8)}
    for half, flat in enumerate((q_ref[:start], q_ref[start:start + used])):
        for j, out in enumerate((gq_ref, gk_ref, gv_ref)):
            cols = [flat[per * (3 * j + n):per * (3 * j + n) + per].astype(f32) for n in range(3)]
            out[2 * half] = jnp.concatenate(cols[:2], axis=1)[:, :per]
            out[2 * half + 1] = pltpu.roll(jnp.concatenate(cols[1:], axis=1), 192, 1)[:, :per]
        ends = flat[9 * per:9 * per + 32].astype(f32)
        for m, bias in enumerate((QUERY_BIAS, VALUE_BIAS)):
            got[bias] += [ends[8 * n + m:8 * n + m + 1] for n in range(3)]
    rows = q_ref[used:used + 8 * tiles].astype(f32)
    for m in range(6):
        got[m] = [rows[8 * n + m:8 * n + m + 1] for n in range(tiles)]
    for m, vec in enumerate(vecs):
        vec[...] = jnp.concatenate(got[m], axis=1).reshape(width)
    blocks = q_ref[used + 8 * tiles:start].astype(f32)
    pick = blocks[:16]
    for f in range(1, 4):
        pick = jnp.where(me_ref[0] == f, blocks[16 * f:16 * f + 16], pick)
    gbe_ref[...] = jnp.concatenate([pick[:8], pick[8:]], axis=1)[:groups, :part]


def unpack(place, order, pieces, w, own, other, groups, per, width, part):
    shapes = [(groups, per, part), (groups, part, per), (width, width)] + [(groups, per, per)] * 3 + [
        (groups, part)] + [(width,)] * 8
    return pl.pallas_call(
        functools.partial(unpack_kernel, order),
        in_specs=[pl.BlockSpec(memory_space=pltpu.SMEM)] + [whole()] * (len(pieces) + 3),
        out_specs=[whole()] * len(shapes),
        out_shape=[jax.ShapeDtypeStruct(t, f32) for t in shapes],
        scratch_shapes=[pltpu.VMEM((len(pieces) * pieces[0].shape[0], 128), f32),
                        pltpu.VMEM((w.shape[0] * w.shape[1], 128), f32),
                        pltpu.VMEM((2 * own.shape[0], 128), bf16)],
        compiler_params=pltpu.CompilerParams(vmem_limit_bytes=VMEM_LIMIT),
        name="unpack",
    )(place, *pieces, w, own, other)


def exchange(x, axes, groups=None):
    return lax.all_to_all(x, axes, 0, 0, axis_index_groups=groups, tiled=True)


def on_device(
    inputs,
    doc_ids,
    cotangent,
    query_weight,
    query_bias,
    key_weight,
    value_weight,
    value_bias,
    out_weight,
    out_bias,
    mixed_gain,
    mixed_bias,
    expand_weight,
    expand_bias,
    shrink_weight,
    shrink_bias,
    final_gain,
    final_bias,
):
    micro, rows_dev, length, width = inputs.shape
    rows = micro * rows_dev
    groups, per, part = expand_weight.shape
    x = inputs.reshape(rows, length, width)
    docs = doc_ids.reshape(rows, 1, length)
    cot = cotangent.reshape(rows, length, width)
    dp = lax.axis_size("dp")
    everyone = ("dp", "ffn")
    count = 4 * dp
    me = lax.axis_index("ffn").astype(jnp.int32).reshape(1)
    like = [[4 * d + 2 * y + core for d in range(dp) for y in range(2)] for core in range(2)]

    def swap(array, bit):
        return lax.ppermute(array, "ffn", [(f, f ^ bit) for f in range(4)])

    bias = jnp.pad(expand_bias[:, None], ((0, 0), (0, 15), (0, part)))
    shard = jnp.concatenate([jnp.concatenate([expand_weight, shrink_weight], axis=2), bias], axis=1)
    shards = [shard] + [swap(shard, bit) for bit in (1, 2, 3)]
    q, k, v, c, p = attend(x, docs, query_weight, key_weight, value_weight, query_bias, value_bias)
    result, dh1, dc, near_e, far_e, send_e, keep_w, send_w, gvec, gbe = feed(
        me, x, c, cot, out_weight, shards, (out_bias, mixed_gain, mixed_bias, shrink_bias, final_gain, final_bias)
    )

    core_w = swap(send_w, 1)
    core_e = swap(send_e, 1)
    sum_w = add((keep_w, core_w))
    far = add((far_e, core_e), (None, 1))
    got_w = exchange(sum_w.reshape(2 * dp, -1, 128), everyone, like)
    far_got = swap(far, 2)
    back = functools.partial(attend_back, x, q, k, v, c, dc, p, me=me, per=per)
    d0, flat0 = back(part=0, vec=gvec, gbe=gbe, after=(far, sum_w))
    piece_w = total(got_w, after=(flat0,))
    sum_e = add((near_e, core_e, far_got), (None, 0, None), after=(flat0,))
    got_e = exchange(sum_e.reshape(dp, -1, 128), "dp")
    all_w = lax.all_gather(piece_w, everyone)
    d1, keep_q, send_q = back(part=1, prev=flat0, devices=count, after=(sum_e, piece_w))
    piece_e = total(got_e, after=(d1,))
    order, pieces = [0], [piece_e]
    bit = dp // 2
    while bit:
        pieces = pieces + [lax.ppermute(t, "dp", [(d, d ^ bit) for d in range(dp)]) for t in pieces]
        order = order + [n ^ bit for n in order]
        bit //= 2
    sum_q = add((keep_q, swap(send_q, 1)), after=(piece_e, pieces[1]))
    got_q = exchange(sum_q.reshape(2 * dp, -1, 128), everyone, like)
    dx = input_grad(dh1, d0, d1, query_weight, key_weight, value_weight, after=(sum_q,))
    piece_q = total(got_q, after=(dx, all_w, *pieces[2:]), copies=2 * dp)
    own_q = exchange(piece_q, everyone, like).reshape(-1, 128)
    other_q = swap(own_q, 1)
    place = jnp.stack([lax.axis_index("ffn"), lax.axis_index("dp")]).astype(jnp.int32)
    gexp, gshr, gout, gq, gk, gv, gbe, *vecs = unpack(
        place, order, pieces, all_w, own_q, other_q, groups, per, width, part
    )
    return (
        result.reshape(inputs.shape),
        dx.reshape(inputs.shape),
        gq,
        vecs[QUERY_BIAS],
        gk,
        gv,
        vecs[VALUE_BIAS],
        gout,
        vecs[OUT_BIAS],
        vecs[MIXED_GAIN],
        vecs[MIXED_BIAS],
        gexp,
        gbe,
        gshr,
        vecs[SHRINK_BIAS],
        vecs[FINAL_GAIN],
        vecs[FINAL_BIAS],
    )


def solution(mesh):
    in_specs = (
        P(None, ("dp", "ffn"), None, None),
        P(None, ("dp", "ffn"), None),
        P(None, ("dp", "ffn"), None, None),
        P(),
        P(),
        P(),
        P(),
        P(),
        P(),
        P(),
        P(),
        P(),
        P(None, None, "ffn"),
        P(None, "ffn"),
        P(None, "ffn", None),
        P(),
        P(),
        P(),
    )
    out_specs = (
        P(None, ("dp", "ffn"), None, None),
        P(None, ("dp", "ffn"), None, None),
        P(),
        P(),
        P(),
        P(),
        P(),
        P(),
        P(),
        P(),
        P(),
        P(None, None, "ffn"),
        P(None, "ffn"),
        P(None, "ffn", None),
        P(),
        P(),
        P(),
    )
    return jax.shard_map(
        on_device, mesh=mesh, in_specs=in_specs, out_specs=out_specs, check_vma=False
    )
```

time: 481 us -> 239 us (0.50); the launches traced: 473 us -> 238 us
  blocking collectives: 105 us -> 18.3 us
  local copies, waits for them, and re-layouts: 84.2 us -> 8.53 us
  other arithmetic: 77.3 us -> 2.03 us
  waiting for transfers between devices: 47.7 us -> 8.19 us
  Pallas kernels: 128 us -> 153 us
  between operations: 1.49 us -> 14.3 us
    psum x2 -> x0, blocking collectives: 77.7 us -> none  [the longest x1 47.7 us: on_device(): vecs = lax.psum((gvec[:6], gvec2), everything)]
    all_to_all x4 -> x3, waiting for transfers between devices: 47.7 us -> 0.06 us  [exchange(): return lax.all_to_all(x, axes, 0, 0, axis_index_groups=groups, tiled=True)]
    convert_element_type x2 -> x0, other arithmetic: 28.9 us -> none  [the longest x1 14.7 us: on_device(): spread(mine.astype(bf16), everything, devices).reshape(-1).astype(f32)]
    convert_element_type x7 -> x0, local copies, waits for them, and re-layouts: 25.8 us -> none  [the longest x2 10.5 us: on_device(): flat = jnp.concatenate([gwo.reshape(-1), gw.reshape(-1)]).astype(bf16)]
    pallas_call x3 -> x12, Pallas kernels: 96.5 us -> 122 us  [the longest x1 50.2 us: feed(): pl.pallas_call(feed_kernel, grid=(rows,), in_specs=[pl.BlockSpec(memory_s...]
    all_to_all x0 -> x1, blocking collectives: none -> 18.3 us  [exchange(): return lax.all_to_all(x, axes, 0, 0, axis_index_groups=groups, tiled=True)]
    unnamed x1 -> x0, blocking collectives: 17 us -> none
    unnamed x37 -> x40, local copies, waits for them, and re-layouts: 24.8 us -> 7.84 us
  transfers between devices with their start and end apart: 10 -> 19, of which waited for: 1 -> 4; matrix products, arithmetic and copies ran while one was open for 18% -> 0% of each run, Pallas kernels for 17% -> 40%
where the time goes in v2:
time: 239 us; the launch traced here: 238 us
  Pallas kernels  153 us (64%)
  starting transfers between devices  33.4 us (14%)
  blocking collectives  18.3 us (8%)
  between operations  14.3 us (6%)
  local copies, waits for them, and re-layouts  8.53 us (4%)
  waiting for transfers between devices  8.19 us (3%)
    pallas_call x1, Pallas kernels, feed(): pl.pallas_call(feed_kernel, grid=(rows,), in_specs=[pl.BlockSpec(memory_s...  50.2 us
    pallas_call x2, Pallas kernels, attend_back(): pl.pallas_call(lambda *refs: attend_back_kernel(lanes, per, *refs[:8], *p...  41.3 us
    pallas_call x1, Pallas kernels, attend(): pl.pallas_call(attend_kernel, grid=(rows,), in_specs=[wide, row_spec((1,...  31.3 us
    all_to_all x1, blocking collectives, exchange(): return lax.all_to_all(x, axes, 0, 0, axis_index_groups=groups, tiled=True)  18.3 us
    all_to_all x3, starting transfers between devices, exchange(): return lax.all_to_all(x, axes, 0, 0, axis_index_groups=groups, tiled=True)  17.2 us
    pallas_call x7, Pallas kernels, call_sum(): pl.pallas_call(lambda *refs: kernel(*refs[:count], *refs[count + len(afte...  14.7 us
    ppermute x7, starting transfers between devices, on_device(): lax.ppermute(t, 'dp', [(d, d ^ bit) for d in range(dp)])  10.4 us
    pallas_call x1, Pallas kernels, input_grad(): pl.pallas_call(lambda *refs: input_grad_kernel(*refs[:count], *refs[count...  10.2 us
  transfers between devices with their start and end apart: 19, of which 4 were waited for; matrix products, arithmetic and copies ran while one was open for 0% of the time, Pallas kernels for 40%

profile of v2, /device:TPU:0, one launch (start us, length us, event | category | flops | bytes accessed | tf_op | source)
XLA Modules:
  0.0 237.8 jit_solution(15837223393155481979)
XLA Ops:
  7.2 0.7 copy.37
  7.9 1.3 fusion.1.w0_ref
  9.2 0.5 collective-permute-start
  9.7 2.6 %collective-permute-start.1 = (bf16[4,208,384]{2,1,0:T(8,128)(2,1)S(1)}, bf16[4,208,384]{2,1,0:T(8,128)(2,1)S(1)}, u32[]{:S(2)}, u32[]{:S(2)}) collective-permute-start(bf16[4,208,384]{2,1,0:T(8,128)(2,1)S(1)} %fusion.1.w0_ref), channel_id=1, source_target_pairs={{0,2},{1,3},{2,0},{3,1},{4,6},{5,7},{6,4},{7,5},{8,10},{9,11},{10,... | collective-permute-start | bytes 1916936 | tf_op jit(solution)/shard_map/ppermute | solution.py:670
  12.3 0.1 collective-permute-start.2
  12.4 31.3 %attend.1 = (bf16[4,512,768]{2,1,0:T(8,128)(2,1)}, bf16[4,512,768]{2,1,0:T(8,128)(2,1)}, bf16[4,512,768]{2,1,0:T(8,128)(2,1)}, bf16[4,512,768]{2,1,0:T(8,128)(2,1)}, bf16[4,12,512,512]{3,2,1,0:T(8,128)(2,1)}) custom-call(bf16[4,512,768]{2,1,0:T(8,128)(2,1)} %bitcast.26, s32[4,1,512]{2,1,0:T(1,128)} %docs_ref.1, bf16[4,192,192]{2,1,0:T(8,128)(2,1)} %refs_3_.1, ...), custom_call_target="tpu_custom_call" | custom-call | flops 20000000000 | bytes 50000000 | tf_op jit(solution)/shard_map/attend/pallas_call | solution.py:130
  43.7 0.0 collective-permute-done.w1_ref
  43.7 0.0 copy-start.17
  43.7 0.0 copy-start.18
  43.7 0.0 collective-permute-done.2.w3_ref
  43.7 0.0 copy-start.19
  43.7 0.8 copy-done.17
  44.5 0.2 copy-done.18
  44.7 0.2 copy-done.19
  44.9 50.2 %feed.1 = (bf16[4,512,768]{2,1,0:T(8,128)(2,1)}, f32[4,512,768]{2,1,0:T(8,128)}, bf16[4,512,768]{2,1,0:T(8,128)(2,1)}, bf16[2304,128]{1,0:T(8,128)(2,1)}, bf16[2...) custom-call(s32[1]{0:T(128)} %bitcast.me_ref.refs_7_, ...), custom_call_target="tpu_custom_call" | custom-call | flops 40000000000 | bytes 50000000 | tf_op jit(solution)/shard_map/feed/pallas_call | solution.py:317
  95.1 0.2 collective-permute-start.3
  95.3 0.4 collective-permute-start.4
  95.7 3.4 %collective-permute-done.4.refs_1_ = bf16[2304,128]{1,0:T(8,128)(2,1)S(1)} collective-permute-done((bf16[2304,128]{1,0:T(8,128)(2,1)}, bf16[2304,128]{1,0:T(8,128)(2,1)S(1)}, u32[]{:S(2)}, u32[]{:S(2)}) %collective-permute-start.4) | collective-permute-done | bytes 589856 | tf_op jit(solution)/shard_map/ppermute | solution.py:670
  99.1 0.8 copy-done.6
  99.9 2.2 add_up.8.refs_11_
  102.1 7.1 %all-to-all-start = ((bf16[16,144,128]{2,1,0:T(8,128)(2,1)}), bf16[16,144,128]{2,1,0:T(8,128)(2,1)S(1)}, u32[]{:S(2)}, u32[]{:S(2)}) async-start(bf16[16,144,128]{2,1,0:T(8,128)(2,1)} %bitcast.19), calls=%async_computation | async-start | bytes 1179648 | tf_op jit(solution)/shard_map/all_to_all | solution.py:634
  109.2 0.0 all-gather.3.cloned.1.call-start
  109.3 0.0 copy-start
  109.3 1.0 copy-done
  110.3 2.4 %add_up.7.refs_10_ = bf16[2304,128]{1,0:T(8,128)(2,1)} custom-call(bf16[2304,128]{1,0:T(8,128)(2,1)} %get-tuple-element.62.refs_0_, bf16[4608,128]{1,0:T(8,128)(2,1)} %copy-done), custom_call_target="tpu_custom_call" | custom-call | tf_op jit(solution)/shard_map/add_up/pallas_call | solution.py:434
  112.7 1.9 collective-permute-start.5
  114.6 20.5 %attend_back.2 = (bf16[4,3,512,384]{3,2,1,0:T(8,128)(2,1)}, bf16[1872,128]{1,0:T(8,128)(2,1)}) custom-call(bf16[4,512,768]{2,1,0:T(8,128)(2,1)} %bitcast.28, bf16[4,512,768]{2,1,0:T(8,128)(2,1)} %get-tuple-element.55.refs_1_, bf16[4,512,768]{2,1,0:T(8,128)(2,1)} %get-tuple-element.56.refs_2_, bf16[4,512,768]{2,1,0:T(8,128)(2,1)} %get-tuple-element.57.refs_3_, ...), custom_call_target="tpu_custom_call" | custom-call | flops 20000000000 | bytes 30000000 | tf_op jit(solution)/shard_map/attend_back/pallas_call | solution.py:497
  135.1 0.0 copy-start.1
  135.1 0.8 copy-done.1
  135.9 1.8 add_up.10.refs_10_
  137.7 0.0 all-gather.3.cloned.1.call-update
  137.7 0.0 copy-start.7
  137.7 0.8 copy-done.7
  138.5 2.6 %add_up.9.refs_9_ = bf16[2304,128]{1,0:T(8,128)(2,1)} custom-call(bf16[2304,128]{1,0:T(8,128)(2,1)} %get-tuple-element.68.refs_0_, bf16[4608,128]{1,0:T(8,128)(2,1)} %copy-done, bf16[2304,128]{1,0:T(8,128)(2,1)} %copy-done.7, bf16[1872,128]{1,0:T(8,128)(2,1)} %get-tuple-element.67.refs_3_.refs_1_.refs_8_), custom_call_target="tpu_custom_call" | custom-call | tf_op jit(solution)/shard_map/add_up/pallas_call | solution.py:434
  141.2 5.4 %all-to-all-start.1 = ((bf16[8,288,128]{2,1,0:T(8,128)(2,1)}), bf16[8,288,128]{2,1,0:T(8,128)(2,1)S(1)}, u32[]{:S(2)}, u32[]{:S(2)}) async-start(bf16[8,288,128]{2,1,0:T(8,128)(2,1)} %bitcast.20), calls=%async_computation.1 | async-start | bytes 1179648 | tf_op jit(solution)/shard_map/all_to_all | solution.py:634
  146.6 20.8 %attend_back.3 = (bf16[4,3,512,384]{3,2,1,0:T(8,128)(2,1)}, bf16[1920,128]{1,0:T(8,128)(2,1)}, bf16[1920,128]{1,0:T(8,128)(2,1)}) custom-call(bf16[4,512,768]{2,1,0:T(8,128)(2,1)} %bitcast.29, bf16[4,512,768]{2,1,0:T(8,128)(2,1)} %get-tuple-element.55.refs_1_, bf16[4,512,768]{2,1,0:T(8,128)(2,1)} %get-tuple-element.56.refs_2_, ...), custom_call_target="tpu_custom_call" | custom-call | flops 20000000000 | bytes 30000000 | tf_op jit(solution)/shard_map/attend_back/pallas_call | solution.py:497
  167.4 0.1 collective-permute-start.6
  167.5 0.0 copy-start.2
  167.5 0.8 copy-done.2
  168.3 1.8 add_up.11.refs_2_.refs_0_
  170.1 2.9 %collective-permute-start.7 = (bf16[288,128]{1,0:T(8,128)(2,1)}, bf16[288,128]{1,0:T(8,128)(2,1)S(1)}, u32[]{:S(2)}, u32[]{:S(2)}) collective-permute-start(bf16[288,128]{1,0:T(8,128)(2,1)} %add_up.11.refs_2_.refs_0_), channel_id=1, source_target_pairs={{0,16},{4,20},{8,24},{12,28},{16,0},{20,4},{24,8},{28,12},{1,17},{... | collective-permute-start | bytes 221192 | tf_op jit(solution)/shard_map/ppermute | solution.py:697
  173.0 1.5 collective-permute-start.8
  174.4 3.5 %collective-permute-done.7.refs_3_.refs_1_ = bf16[288,128]{1,0:T(8,128)(2,1)S(1)} collective-permute-done((bf16[288,128]{1,0:T(8,128)(2,1)}, bf16[288,128]{1,0:T(8,128)(2,1)S(1)}, u32[]{:S(2)}, u32[]{:S(2)}) %collective-permute-start.7) | collective-permute-done | bytes 73760 | tf_op jit(solution)/shard_map/ppermute | solution.py:697
  178.0 0.6 collective-permute-start.9
  178.5 1.5 collective-permute-start.10
  180.0 0.8 copy-done.9
  180.8 2.1 add_up.12.refs_6_
  182.8 4.7 %all-to-all-start.2 = ((bf16[16,120,128]{2,1,0:T(8,128)(2,1)}), bf16[16,120,128]{2,1,0:T(8,128)(2,1)S(1)}, u32[]{:S(2)}, u32[]{:S(2)}) async-start(bf16[16,120,128]{2,1,0:T(8,128)(2,1)} %bitcast.23), calls=%async_computation.2 | async-start | bytes 983040 | tf_op jit(solution)/shard_map/all_to_all | solution.py:634
  187.6 2.0 collective-permute-start.11
  189.5 0.1 collective-permute-start.12
  189.7 1.9 collective-permute-start.13
  191.6 10.2 %input_grad.1.refs_1_ = bf16[4,512,768]{2,1,0:T(8,128)(2,1)} custom-call(f32[4,512,768]{2,1,0:T(8,128)} %get-tuple-element.54.refs_0_, bf16[4,3,512,384]{3,2,1,0:T(8,128)(2,1)} %get-tuple-element.66.refs_1_, bf16[4,3,512,384]{3,2,1,0:T(8,128)(2,1)} %get-tuple-element.69.refs_1_.refs_2_, bf16[4,192,192]{2,1,0:T(8,128)(2,1)} %refs_3_.1, ...), custom_call_target="tpu_custom_call" | custom-call | flops 10000000000 | bytes 20000000 | tf_op jit(solution)/shard_map/input_grad/pallas_call | solution.py:544
  201.9 0.1 all-to-all-done.2.refs_0_
  202.0 0.5 copy-done.13
  202.5 0.0 copy-done.14
  202.5 0.0 copy-done.15
  202.5 0.0 copy-done.16
  202.6 0.2 copy-done.4
  202.7 1.9 add_up.13
  204.6 18.3 %all_to_all.20 = bf16[16,120,128]{2,1,0:T(8,128)(2,1)S(1)} all-to-all(bf16[16,120,128]{2,1,0:T(8,128)(2,1)} %add_up.13), channel_id=1, replica_groups={{0,2,4,6,8,10,12,14,16,18,20,22,24,26,28,30},{1,3,5,7,9,11,13,15,17,19,..., dimensions={0} | all-to-all | bytes 983040 | tf_op jit(solution)/shard_map/all_to_all | solution.py:634
  223.0 0.7 pad_add_fusion.me_ref
  223.7 1.2 collective-permute-done.14.refs_10_
  224.8 0.8 copy-done.8
  225.6 5.3 %unpack.1 = (f32[4,192,192]{2,1,0:T(8,128)}, f32[4,192,192]{2,1,0:T(8,128)}, f32[768,768]{1,0:T(8,128)}, f32[4,192,192]{2,1,0:T(8,128)}, f32[4,192,192]{2,1,0:T(...) custom-call(s32[2]{0:T(128)} %pad_add_fusion.me_ref, ...), custom_call_target="tpu_custom_call" | custom-call | tf_op jit(solution)/shard_map/unpack/pallas_call | solution.py:620
  (32 shorter events, 0.1 us)
Async XLA Ops:
  9.2 34.5 %copy-start.5 = (bf16[4,208,384]{2,1,0:T(8,128)(2,1)}, bf16[4,208,384]{2,1,0:T(8,128)(2,1)S(1)}, u32[]{:S(2)}) copy-start(bf16[4,208,384]{2,1,0:T(8,128)(2,1)S(1)} %fusion.1.w0_ref) | copy-start | bytes 1916932
  9.2 34.5 %collective-permute-start = (bf16[4,208,384]{2,1,0:T(8,128)(2,1)S(1)}, bf16[4,208,384]{2,1,0:T(8,128)(2,1)S(1)}, u32[]{:S(2)}, u32[]{:S(2)}) collective-permute-start(bf16[4,208,384]{2,1,0:T(8,128)(2,1)S(1)} %fusion.1.w0_ref), channel_id=1, source_target_pairs={{0,1},{1,0},{2,3},{3,2},{4,5},{5,4},{6,7},{7,6},{8,9},{9,8},{10,11... | collective-permute-start | bytes 1916936 | tf_op jit(solution)/shard_map/ppermute | solution.py:670
  9.7 34.0 %collective-permute-start.1 = (bf16[4,208,384]{2,1,0:T(8,128)(2,1)S(1)}, bf16[4,208,384]{2,1,0:T(8,128)(2,1)S(1)}, u32[]{:S(2)}, u32[]{:S(2)}) collective-permute-start(bf16[4,208,384]{2,1,0:T(8,128)(2,1)S(1)} %fusion.1.w0_ref), channel_id=1, source_target_pairs={{0,2},{1,3},{2,0},{3,1},{4,6},{5,7},{6,4},{7,5},{8,10},{9,11},{10,... | collective-permute-start | bytes 1916936 | tf_op jit(solution)/shard_map/ppermute | solution.py:670
  12.3 31.4 %collective-permute-start.2 = (bf16[4,208,384]{2,1,0:T(8,128)(2,1)S(1)}, bf16[4,208,384]{2,1,0:T(8,128)(2,1)S(1)}, u32[]{:S(2)}, u32[]{:S(2)}) collective-permute-start(bf16[4,208,384]{2,1,0:T(8,128)(2,1)S(1)} %fusion.1.w0_ref), channel_id=1, source_target_pairs={{0,3},{1,2},{2,1},{3,0},{4,7},{5,6},{6,5},{7,4},{8,11},{9,10},{10,... | collective-permute-start | bytes 1916936 | tf_op jit(solution)/shard_map/ppermute | solution.py:670
  43.7 0.8 copy-start.17
  43.7 1.0 copy-start.18
  43.7 1.2 copy-start.19
  95.1 14.1 %collective-permute-start.3 = (bf16[4608,128]{1,0:T(8,128)(2,1)}, bf16[4608,128]{1,0:T(8,128)(2,1)S(1)}, u32[]{:S(2)}, u32[]{:S(2)}) collective-permute-start(bf16[4608,128]{1,0:T(8,128)(2,1)} %get-tuple-element.63), channel_id=1, source_target_pairs={{0,1},{1,0},{2,3},{3,2},{4,5},{5,4},{6,7},{7,6},{8,9},{9,8},{10,11... | collective-permute-start | bytes 3538952 | tf_op jit(solution)/shard_map/ppermute | solution.py:670
  95.3 3.8 %collective-permute-start.4 = (bf16[2304,128]{1,0:T(8,128)(2,1)}, bf16[2304,128]{1,0:T(8,128)(2,1)S(1)}, u32[]{:S(2)}, u32[]{:S(2)}) collective-permute-start(bf16[2304,128]{1,0:T(8,128)(2,1)} %get-tuple-element.65), channel_id=1, source_target_pairs={{0,1},{1,0},{2,3},{3,2},{4,5},{5,4},{6,7},{7,6},{8,9},{9,8},{10,11... | collective-permute-start | bytes 1769480 | tf_op jit(solution)/shard_map/ppermute | solution.py:670
  99.1 0.8 copy-start.6
  102.1 33.0 %all-to-all-start = ((bf16[16,144,128]{2,1,0:T(8,128)(2,1)}), bf16[16,144,128]{2,1,0:T(8,128)(2,1)S(1)}, u32[]{:S(2)}, u32[]{:S(2)}) async-start(bf16[16,144,128]{2,1,0:T(8,128)(2,1)} %bitcast.19), calls=%async_computation | async-start | bytes 1179648 | tf_op jit(solution)/shard_map/all_to_all | solution.py:634
  109.2 92.8 %all-gather.3.cloned.1.call-start = ((), (), s32[]{:S(2)}) async-start(), calls=%async_computation.4 | async-start | bytes 1216512 | tf_op jit(solution)/shard_map/all_gather | solution.py:691
  109.3 1.0 copy-start
  112.7 25.0 %collective-permute-start.5 = (bf16[2304,128]{1,0:T(8,128)(2,1)}, bf16[2304,128]{1,0:T(8,128)(2,1)S(1)}, u32[]{:S(2)}, u32[]{:S(2)}) collective-permute-start(bf16[2304,128]{1,0:T(8,128)(2,1)} %add_up.7.refs_10_), channel_id=1, source_target_pairs={{0,2},{1,3},{2,0},{3,1},{4,6},{5,7},{6,4},{7,5},{8,10},{9,11},{10,... | collective-permute-start | bytes 1769480 | tf_op jit(solution)/shard_map/ppermute | solution.py:670
  135.1 0.8 copy-start.1
  137.7 0.8 copy-start.7
  141.2 26.3 %all-to-all-start.1 = ((bf16[8,288,128]{2,1,0:T(8,128)(2,1)}), bf16[8,288,128]{2,1,0:T(8,128)(2,1)S(1)}, u32[]{:S(2)}, u32[]{:S(2)}) async-start(bf16[8,288,128]{2,1,0:T(8,128)(2,1)} %bitcast.20), calls=%async_computation.1 | async-start | bytes 1179648 | tf_op jit(solution)/shard_map/all_to_all | solution.py:634
  167.4 12.6 %collective-permute-start.6 = (bf16[1920,128]{1,0:T(8,128)(2,1)}, bf16[1920,128]{1,0:T(8,128)(2,1)S(1)}, u32[]{:S(2)}, u32[]{:S(2)}) collective-permute-start(bf16[1920,128]{1,0:T(8,128)(2,1)} %get-tuple-element.71), channel_id=1, source_target_pairs={{0,1},{1,0},{2,3},{3,2},{4,5},{5,4},{6,7},{7,6},{8,9},{9,8},{10,11... | collective-permute-start | bytes 1474568 | tf_op jit(solution)/shard_map/ppermute | solution.py:670
  167.5 0.8 copy-start.2
  170.1 7.9 %collective-permute-start.7 = (bf16[288,128]{1,0:T(8,128)(2,1)}, bf16[288,128]{1,0:T(8,128)(2,1)S(1)}, u32[]{:S(2)}, u32[]{:S(2)}) collective-permute-start(bf16[288,128]{1,0:T(8,128)(2,1)} %add_up.11.refs_2_.refs_0_), channel_id=1, source_target_pairs={{0,16},{4,20},{8,24},{12,28},{16,0},{20,4},{24,8},{28,12},{1,17},{... | collective-permute-start | bytes 221192 | tf_op jit(solution)/shard_map/ppermute | solution.py:697
  173.0 16.6 %collective-permute-start.8 = (bf16[288,128]{1,0:T(8,128)(2,1)}, bf16[288,128]{1,0:T(8,128)(2,1)S(1)}, u32[]{:S(2)}, u32[]{:S(2)}) collective-permute-start(bf16[288,128]{1,0:T(8,128)(2,1)} %add_up.11.refs_2_.refs_0_), channel_id=1, source_target_pairs={{0,8},{4,12},{8,0},{12,4},{16,24},{20,28},{24,16},{28,20},{1,9},{5... | collective-permute-start | bytes 221192 | tf_op jit(solution)/shard_map/ppermute | solution.py:697
  178.0 2.0 copy-start.10
  178.0 11.7 %collective-permute-start.9 = (bf16[288,128]{1,0:T(8,128)(2,1)S(1)}, bf16[288,128]{1,0:T(8,128)(2,1)S(1)}, u32[]{:S(2)}, u32[]{:S(2)}) collective-permute-start(bf16[288,128]{1,0:T(8,128)(2,1)S(1)} %collective-permute-done.7.refs_3_.refs_1_), channel_id=1, source_target_pairs={{0,8},{4,12},{8,0},{12,4},{16,24},{20,28},{24,16},{28,20},{1,9},{5... | collective-permute-start | bytes 221192 | tf_op jit(solution)/shard_map/ppermute | solution.py:697
  178.5 23.3 %collective-permute-start.10 = (bf16[288,128]{1,0:T(8,128)(2,1)}, bf16[288,128]{1,0:T(8,128)(2,1)S(1)}, u32[]{:S(2)}, u32[]{:S(2)}) collective-permute-start(bf16[288,128]{1,0:T(8,128)(2,1)} %add_up.11.refs_2_.refs_0_), channel_id=1, source_target_pairs={{0,4},{4,0},{8,12},{12,8},{16,20},{20,16},{24,28},{28,24},{1,5},{5... | collective-permute-start | bytes 221192 | tf_op jit(solution)/shard_map/ppermute | solution.py:697
  180.0 0.8 copy-start.9
  182.8 19.1 %all-to-all-start.2 = ((bf16[16,120,128]{2,1,0:T(8,128)(2,1)}), bf16[16,120,128]{2,1,0:T(8,128)(2,1)S(1)}, u32[]{:S(2)}, u32[]{:S(2)}) async-start(bf16[16,120,128]{2,1,0:T(8,128)(2,1)} %bitcast.23), calls=%async_computation.2 | async-start | bytes 983040 | tf_op jit(solution)/shard_map/all_to_all | solution.py:634
  187.6 14.3 %collective-permute-start.11 = (bf16[288,128]{1,0:T(8,128)(2,1)}, bf16[288,128]{1,0:T(8,128)(2,1)S(1)}, u32[]{:S(2)}, u32[]{:S(2)}) collective-permute-start(bf16[288,128]{1,0:T(8,128)(2,1)} %copy-done.10), channel_id=1, source_target_pairs={{0,4},{4,0},{8,12},{12,8},{16,20},{20,16},{24,28},{28,24},{1,5},{5... | collective-permute-start | bytes 221192 | tf_op jit(solution)/shard_map/ppermute | solution.py:697
  189.5 12.3 %copy-start.11 = (bf16[288,128]{1,0:T(8,128)(2,1)}, bf16[288,128]{1,0:T(8,128)(2,1)S(1)}, u32[]{:S(2)}) copy-start(bf16[288,128]{1,0:T(8,128)(2,1)S(1)} %collective-permute-done.8.refs_3_.refs_2_) | copy-start | bytes 221188
  189.5 12.3 %collective-permute-start.12 = (bf16[288,128]{1,0:T(8,128)(2,1)S(1)}, bf16[288,128]{1,0:T(8,128)(2,1)S(1)}, u32[]{:S(2)}, u32[]{:S(2)}) collective-permute-start(bf16[288,128]{1,0:T(8,128)(2,1)S(1)} %collective-permute-done.8.refs_3_.refs_2_), channel_id=1, source_target_pairs={{0,4},{4,0},{8,12},{12,8},{16,20},{20,16},{24,28},{28,24},{1,5},{5... | collective-permute-start | bytes 221192 | tf_op jit(solution)/shard_map/ppermute | solution.py:697
  189.7 12.2 %copy-start.12 = (bf16[288,128]{1,0:T(8,128)(2,1)}, bf16[288,128]{1,0:T(8,128)(2,1)S(1)}, u32[]{:S(2)}) copy-start(bf16[288,128]{1,0:T(8,128)(2,1)S(1)} %collective-permute-done.9.refs_4_.refs_3_) | copy-start | bytes 221188
  189.7 12.2 %collective-permute-start.13 = (bf16[288,128]{1,0:T(8,128)(2,1)S(1)}, bf16[288,128]{1,0:T(8,128)(2,1)S(1)}, u32[]{:S(2)}, u32[]{:S(2)}) collective-permute-start(bf16[288,128]{1,0:T(8,128)(2,1)S(1)} %collective-permute-done.9.refs_4_.refs_3_), channel_id=1, source_target_pairs={{0,4},{4,0},{8,12},{12,8},{16,20},{20,16},{24,28},{28,24},{1,5},{5... | collective-permute-start | bytes 221192 | tf_op jit(solution)/shard_map/ppermute | solution.py:697
  201.8 0.6 copy-start.13
  201.8 0.6 copy-start.14
  201.9 0.7 copy-start.15
  201.9 0.7 copy-start.16
  202.0 0.8 copy-start.4
  223.0 1.9 copy-start.3
  223.0 1.9 collective-permute-start.14
  224.8 0.8 copy-start.8
Sparse Core Ops, SparseCore 0:
  137.8 57.3 all-gather.2

commit v3 on v2

--- a/solution.py
+++ b/solution.py
@@ -9,6 +9,8 @@
 
 HEADS = 12
 HEAD = 64
+DOCS = 4
+CHUNK = 256
 epsilon = 1e-05
 masked_score = -1e30
 bf16 = jnp.bfloat16
@@ -66,7 +68,7 @@
 
 
 def attend_kernel(x_ref, docs_ref, wq_ref, wk_ref, wv_ref, qb_ref, vb_ref,
-                  q_ref, k_ref, v_ref, c_ref, p_ref, wpad, bias_ref):
+                  q_ref, k_ref, v_ref, c_ref, r_ref, p_ref, wpad):
     length = x_ref.shape[1]
     width = x_ref.shape[2]
     groups = wq_ref.shape[0]
@@ -91,28 +93,32 @@
             out[0, :, 128 * n:128 * n + 128] = col.astype(bf16)
 
     docs = docs_ref[0].astype(f32)
-    down = jnp.transpose(jnp.broadcast_to(docs, (128, length)))[:, :1]
-    bias_ref[...] = jnp.where(down == docs, 0.0, masked_score)
-    low = lax.broadcasted_iota(jnp.int32, (1, 128), 1) < HEAD
+    down = jnp.transpose(jnp.broadcast_to(docs, (128, length)))
+    lane = lax.broadcasted_iota(jnp.int32, (1, 128), 1)
+    same = down == lane.astype(f32)
+    doc_q = jnp.where(same & (lane < DOCS), 1.0, 0.0).astype(bf16)
+    doc_k = jnp.where(same | (lane >= DOCS), 0.0, masked_score).astype(bf16)
+    low = lane < HEAD
     for pair in range(HEADS // 2):
         lanes = slice(128 * pair, 128 * pair + 128)
-        q2 = q_ref[0, :, lanes] * bf16(HEAD ** -0.5)
+        q2 = jnp.concatenate([q_ref[0, :, lanes] * bf16(HEAD ** -0.5), doc_q], axis=1)
         k2 = k_ref[0, :, lanes]
         v2 = v_ref[0, :, lanes]
         acc = None
         for h in range(2):
             half = low if h == 0 else jnp.logical_not(low)
-            km = jnp.where(half, k2, bf16(0))
-            vm = jnp.where(half, v2, bf16(0))
-            s = dot(q2, km, NT) + bias_ref[...]
+            km = jnp.concatenate([jnp.where(half, k2, bf16(0)), doc_k], axis=1)
+            ones = jnp.broadcast_to(jnp.where(half, 1.0, 0.0), (length, 128)).astype(bf16)
+            vm = jnp.concatenate([jnp.where(half, v2, bf16(0)), ones], axis=1)
+            s = dot(q2, km, NT)
             top = jnp.max(s, axis=-1, keepdims=True)
-            e = jnp.exp(s - top)
-            total = jnp.sum(e, axis=-1, keepdims=True)
-            pr = (e * (1.0 / total)).astype(bf16)
+            pr = jnp.exp(s - top).astype(bf16)
             p_ref[0, 2 * pair + h] = pr
             c = dot(pr, vm)
             acc = c if acc is None else acc + c
-        c_ref[0, :, lanes] = acc.astype(bf16)
+        inverse = 1.0 / acc[:, 128:]
+        r_ref[0, :, lanes] = inverse
+        c_ref[0, :, lanes] = (acc[:, :128] * inverse).astype(bf16)
 
 
 def full(shape):
@@ -132,9 +138,9 @@
         grid=(rows,),
         in_specs=[wide, row_spec((1, length)), full(wq.shape), full(wk.shape), full(wv.shape),
                   whole(), whole()],
-        out_specs=[wide, wide, wide, wide, row_spec((HEADS, length, length))],
-        out_shape=[low, low, low, low, jax.ShapeDtypeStruct((rows, HEADS, length, length), bf16)],
-        scratch_shapes=[pltpu.VMEM((3, wq.shape[0], 256, 256), bf16), pltpu.VMEM((length, length), f32)],
+        out_specs=[wide, wide, wide, wide, wide, row_spec((HEADS, length, length))],
+        out_shape=[low, low, low, low, jax.ShapeDtypeStruct((rows, length, width), f32), jax.ShapeDtypeStruct((rows, HEADS, length, length), bf16)],
+        scratch_shapes=[pltpu.VMEM((3, wq.shape[0], 256, 256), bf16)],
         compiler_params=pltpu.CompilerParams(vmem_limit_bytes=VMEM_LIMIT),
         cost_estimate=pl.CostEstimate(flops=int(2e10), bytes_accessed=int(5e7), transcendentals=0),
         name="attend",
@@ -164,9 +170,9 @@
     return jnp.where(low_half(), a, pltpu.roll(b, 64, 1))
 
 
-def feed_kernel(me_ref, x_ref, c_ref, e_ref, wo_ref, w0_ref, w1_ref, w2_ref, w3_ref, ob_ref, mg_ref, mb_ref, sb_ref, fg_ref, fb_ref,
+def feed_kernel(me_ref, x_ref, c_ref, r_ref, e_ref, wo_ref, w0_ref, w1_ref, w2_ref, w3_ref, ob_ref, mg_ref, mb_ref, sb_ref, fg_ref, fb_ref,
                 result_ref, dh1_ref, dc_ref, near_e, far_e, send_e, keep_w, send_w, gvec_ref, gbe_ref,
-                wepad, wspad, be_s, act, slope, pre_low, df_low, gwo_ref, gwe_ref, gws_ref):
+                wepad, wspad, be_s, act, slope, back, xhat1, dh2_s, pre_low, df_low, gwo_ref, gwe_ref, gws_ref):
     step = pl.program_id(0)
     groups, width = w0_ref.shape[0], x_ref.shape[2]
     per = width // groups
@@ -207,65 +213,82 @@
 
     out_bias, mixed_gain, mixed_bias = as_row(ob_ref), as_row(mg_ref), as_row(mb_ref)
     shrink_bias, final_gain, final_bias = as_row(sb_ref), as_row(fg_ref), as_row(fb_ref)
-    h1 = x_ref[0].astype(f32) + dot(c_ref[0], wo_ref[...]) + out_bias
-    cen = h1 - jnp.mean(h1, axis=-1, keepdims=True)
-    rstd1 = lax.rsqrt(jnp.mean(cen * cen, axis=-1, keepdims=True) + epsilon)
-    xhat1 = cen * rstd1
-    a = xhat1 * mixed_gain + mixed_bias
-    a_low = a.astype(bf16)
-    pre_low[...] = a_low
-
-    parts = []
+    length = x_ref.shape[1]
+    chunks = [slice(first, first + CHUNK) for first in range(0, length, CHUNK)]
+    keep = {}
+    for t in chunks:
+        h1 = x_ref[0, t].astype(f32) + dot(c_ref[0, t], wo_ref[...]) + out_bias
+        cen = h1 - jnp.mean(h1, axis=-1, keepdims=True)
+        rstd1 = lax.rsqrt(jnp.mean(cen * cen, axis=-1, keepdims=True) + epsilon)
+        xhat = cen * rstd1
+        xhat1[t] = xhat
+        a_low = (xhat * mixed_gain + mixed_bias).astype(bf16)
+        pre_low[t] = a_low
+        keep[t.start] = rstd1
+
+    for t in chunks:
+        parts = []
+        for g in range(groups):
+            base, _ = window(g, per)
+            for n in range(hidden // 256):
+                cols = slice(256 * n, 256 * n + 256)
+                u = dot(pre_low[t, base:base + 256], wepad[g, :, cols]) + be_s[g:g + 1, cols]
+                val, slp = gelu_both(u)
+                act[g, t, cols] = val.astype(bf16)
+                slope[g, t, cols] = slp
+            parts.append(dot(act[g, t], wspad[g]))
+        f = jnp.concatenate(join_windows(parts), axis=1)
+        h2 = (xhat1[t] * mixed_gain + mixed_bias) + f + shrink_bias
+        cen = h2 - jnp.mean(h2, axis=-1, keepdims=True)
+        rstd2 = lax.rsqrt(jnp.mean(cen * cen, axis=-1, keepdims=True) + epsilon)
+        xhat2 = cen * rstd2
+        result_ref[0, t] = (xhat2 * final_gain + final_bias).astype(bf16)
+
+        up = e_ref[0, t].astype(f32)
+        gvec_ref[4:5] += jnp.sum(up * xhat2, axis=0, keepdims=True)
+        gvec_ref[5:6] += jnp.sum(up, axis=0, keepdims=True)
+        dx = up * final_gain
+        dh2 = rstd2 * (dx - jnp.mean(dx, axis=-1, keepdims=True) - xhat2 * jnp.mean(dx * xhat2, axis=-1, keepdims=True))
+        gvec_ref[3:4] += jnp.sum(dh2, axis=0, keepdims=True)
+        dh2_s[t] = dh2
+        df_low[t] = dh2.astype(bf16)
+
+    for t in chunks:
+        parts = []
+        for g in range(groups):
+            base, _ = window(g, per)
+            acc = None
+            for n in range(hidden // 256):
+                cols = slice(256 * n, 256 * n + 256)
+                dg = dot(df_low[t, base:base + 256], wspad[g, cols, :], NT)
+                du = (dg * slope[g, t, cols]).astype(bf16)
+                back[g, t, cols] = du
+                gbe_ref[g:g + 1, cols] += jnp.sum(du.astype(f32), axis=0, keepdims=True)
+                da = dot(du, wepad[g, :, cols], NT)
+                acc = da if acc is None else acc + da
+            parts.append(acc)
+        dh2_s[t] += jnp.concatenate(join_windows(parts), axis=1)
+
+    a_t = jnp.transpose(pre_low[...])
+    df_t = jnp.transpose(df_low[...])
     for g in range(groups):
-        base, _ = window(g, per)
-        for n in range(hidden // 256):
-            cols = slice(256 * n, 256 * n + 256)
-            u = dot(pre_low[:, base:base + 256], wepad[g, :, cols]) + be_s[g:g + 1, cols]
-            val, slp = gelu_both(u)
-            act[g, :, cols] = val.astype(bf16)
-            slope[g, :, cols] = slp
-        parts.append(dot(act[g], wspad[g]))
-    f = jnp.concatenate(join_windows(parts), axis=1)
-    h2 = a + f + shrink_bias
-    cen = h2 - jnp.mean(h2, axis=-1, keepdims=True)
-    rstd2 = lax.rsqrt(jnp.mean(cen * cen, axis=-1, keepdims=True) + epsilon)
-    xhat2 = cen * rstd2
-    result_ref[0] = (xhat2 * final_gain + final_bias).astype(bf16)
-
-    up = e_ref[0].astype(f32)
-    gvec_ref[4:5] += jnp.sum(up * xhat2, axis=0, keepdims=True)
-    gvec_ref[5:6] += jnp.sum(up, axis=0, keepdims=True)
-    dx = up * final_gain
-    dh2 = rstd2 * (dx - jnp.mean(dx, axis=-1, keepdims=True) - xhat2 * jnp.mean(dx * xhat2, axis=-1, keepdims=True))
-    gvec_ref[3:4] += jnp.sum(dh2, axis=0, keepdims=True)
-    df_low[...] = dh2.astype(bf16)
-    a_t = jnp.transpose(a_low)
-    df_t = jnp.transpose(df_low[...])
-    parts = []
-    for g in range(groups):
-        base, _ = window(g, per)
         rows = slice(per * g, per * g + per)
         gws_ref[g] += dot(df_t[rows], act[g])
-        acc = None
-        for n in range(hidden // 256):
-            cols = slice(256 * n, 256 * n + 256)
-            dg = dot(df_low[:, base:base + 256], wspad[g, cols, :], NT)
-            du = (dg * slope[g, :, cols]).astype(bf16)
-            gbe_ref[g:g + 1, cols] += jnp.sum(du.astype(f32), axis=0, keepdims=True)
-            gwe_ref[g, :, cols] += dot(a_t[rows], du)
-            da = dot(du, wepad[g, :, cols], NT)
-            acc = da if acc is None else acc + da
-        parts.append(acc)
-    da = dh2 + jnp.concatenate(join_windows(parts), axis=1)
-    gvec_ref[1:2] += jnp.sum(da * xhat1, axis=0, keepdims=True)
-    gvec_ref[2:3] += jnp.sum(da, axis=0, keepdims=True)
-    dx = da * mixed_gain
-    dh1 = rstd1 * (dx - jnp.mean(dx, axis=-1, keepdims=True) - xhat1 * jnp.mean(dx * xhat1, axis=-1, keepdims=True))
-    gvec_ref[0:1] += jnp.sum(dh1, axis=0, keepdims=True)
-    dh1_ref[0] = dh1
-    dy = dh1.astype(bf16)
-    gwo_ref[...] += dot(jnp.transpose(c_ref[0]), dy)
-    dc_ref[0] = dot(dy, wo_ref[...], NT).astype(bf16)
+        gwe_ref[g] += dot(a_t[rows], back[g])
+
+    for t in chunks:
+        da = dh2_s[t]
+        xhat = xhat1[t]
+        gvec_ref[1:2] += jnp.sum(da * xhat, axis=0, keepdims=True)
+        gvec_ref[2:3] += jnp.sum(da, axis=0, keepdims=True)
+        dx = da * mixed_gain
+        dh1 = keep[t.start] * (dx - jnp.mean(dx, axis=-1, keepdims=True) - xhat * jnp.mean(dx * xhat, axis=-1, keepdims=True))
+        gvec_ref[0:1] += jnp.sum(dh1, axis=0, keepdims=True)
+        dh1_ref[0, t] = dh1
+        dy = dh1.astype(bf16)
+        df_low[t] = dy
+        dc_ref[0, t] = (dot(dy, wo_ref[...], NT) * r_ref[0, t]).astype(bf16)
+    gwo_ref[...] += dot(jnp.transpose(c_ref[0]), df_low[...])
 
     @pl.when(step == pl.num_programs(0) - 1)
     def _():
@@ -303,7 +326,7 @@
     return pl.BlockSpec(memory_space=pltpu.VMEM)
 
 
-def feed(me, x, c, e, wo, shards, vectors):
+def feed(me, x, c, r, e, wo, shards, vectors):
     rows, length, width = x.shape
     groups = shards[0].shape[0]
     part = shards[0].shape[2] // 2
@@ -317,7 +340,7 @@
     return pl.pallas_call(
         feed_kernel,
         grid=(rows,),
-        in_specs=[pl.BlockSpec(memory_space=pltpu.SMEM), wide, wide, wide] + [whole()] * 11,
+        in_specs=[pl.BlockSpec(memory_space=pltpu.SMEM), wide, wide, wide, wide] + [whole()] * 11,
         out_specs=[wide, wide, wide] + [whole()] * 7,
         out_shape=[low, jax.ShapeDtypeStruct((rows, length, width), f32), low, half_e, half_e, flat_e, flat_w, flat_w,
                    jax.ShapeDtypeStruct((8, width), f32), jax.ShapeDtypeStruct((8, hidden), f32)],
@@ -327,6 +350,9 @@
             pltpu.VMEM((8, hidden), f32),
             pltpu.VMEM((groups, length, hidden), bf16),
             pltpu.VMEM((groups, length, hidden), f32),
+            pltpu.VMEM((groups, length, hidden), bf16),
+            pltpu.VMEM((length, width), f32),
+            pltpu.VMEM((length, width), f32),
             pltpu.VMEM((length, width), bf16),
             pltpu.VMEM((length, width), bf16),
             pltpu.VMEM((width, width), f32),
@@ -336,7 +362,7 @@
         compiler_params=pltpu.CompilerParams(vmem_limit_bytes=VMEM_LIMIT),
         cost_estimate=pl.CostEstimate(flops=int(4e10), bytes_accessed=int(5e7), transcendentals=0),
         name="feed",
-    )(me, x, c, e, wo, *shards, *vectors)
+    )(me, x, c, r, e, wo, *shards, *vectors)
 
 
 def attend_back_kernel(lanes_in, per, x_ref, q_ref, k_ref, v_ref, c_ref, dc_ref, p_ref, me_ref, vec_ref, gbe_ref,
@@ -357,25 +383,26 @@
         v2 = v_ref[0, :, lanes]
         dc2 = dc_ref[0, :, lanes]
         prod = dc2.astype(f32) * c_ref[0, :, lanes].astype(f32)
-        dq = dk = dv = None
+        q_t = jnp.transpose(q2)
+        dc_t = jnp.transpose(dc2)
+        dq = None
+        dk, dv = [], []
         for h in range(2):
             half = low if h == 0 else jnp.logical_not(low)
+            rows = slice(64 * h, 64 * h + 64)
             km = jnp.where(half, k2, bf16(0))
-            qm = jnp.where(half, q2, bf16(0))
-            dcm = jnp.where(half, dc2, bf16(0))
+            vm = jnp.where(half, v2, bf16(0))
             delta = jnp.sum(jnp.where(half, prod, 0.0), axis=-1, keepdims=True)
             pr = p_ref[0, 2 * pair + h]
-            dp = dot(dcm, v2, NT)
+            dp = dot(dc2, vm, NT)
             ds = (pr.astype(f32) * (dp - delta)).astype(bf16)
             a = dot(ds, km)
-            b = dot(ds, qm, TN)
-            c = dot(pr, dcm, TN)
             dq = a if dq is None else dq + a
-            dk = b if dk is None else dk + b
-            dv = c if dv is None else dv + c
+            dk.append(dot(q_t[rows], ds))
+            dv.append(dot(dc_t[rows], pr))
         dq = (dq * (HEAD ** -0.5)).astype(bf16)
-        dk = dk.astype(bf16)
-        dv = dv.astype(bf16)
+        dk = jnp.transpose(jnp.concatenate(dk, axis=0)).astype(bf16)
+        dv = jnp.transpose(jnp.concatenate(dv, axis=0)).astype(bf16)
         dqkv_ref[0, 0, :, lanes] = dq
         dqkv_ref[0, 1, :, lanes] = dk
         dqkv_ref[0, 2, :, lanes] = dv
@@ -672,9 +699,9 @@
     bias = jnp.pad(expand_bias[:, None], ((0, 0), (0, 15), (0, part)))
     shard = jnp.concatenate([jnp.concatenate([expand_weight, shrink_weight], axis=2), bias], axis=1)
     shards = [shard] + [swap(shard, bit) for bit in (1, 2, 3)]
-    q, k, v, c, p = attend(x, docs, query_weight, key_weight, value_weight, query_bias, value_bias)
+    q, k, v, c, r, p = attend(x, docs, query_weight, key_weight, value_weight, query_bias, value_bias)
     result, dh1, dc, near_e, far_e, send_e, keep_w, send_w, gvec, gbe = feed(
-        me, x, c, cot, out_weight, shards, (out_bias, mixed_gain, mixed_bias, shrink_bias, final_gain, final_bias)
+        me, x, c, r, cot, out_weight, shards, (out_bias, mixed_gain, mixed_bias, shrink_bias, final_gain, final_bias)
     )
 
     core_w = swap(send_w, 1)

time: 239 us -> 231 us (0.967)
  Pallas kernels: 153 us -> 144 us
    pallas_call x1, Pallas kernels: 31.3 us -> 27 us  [attend(): pl.pallas_call(attend_kernel, grid=(rows,), in_specs=[wide, row_spec((1,...]
    pallas_call x2, Pallas kernels: 41.3 us -> 37.9 us  [attend_back(): pl.pallas_call(lambda *refs: attend_back_kernel(lanes, per, *refs[:8], *p...]
  transfers between devices with their start and end apart: 19 -> 19, of which waited for: 4 -> 5; matrix products, arithmetic and copies ran while one was open for 0% -> 0% of each run, Pallas kernels for 40% -> 38%
where the time goes in v3:
time: 231 us
  Pallas kernels  144 us (62%)
  starting transfers between devices  34.1 us (15%)
  blocking collectives  18.2 us (8%)
  between operations  14.3 us (6%)
  waiting for transfers between devices  9.89 us (4%)
  local copies, waits for them, and re-layouts  8.34 us (4%)
    pallas_call x1, Pallas kernels, feed(): pl.pallas_call(feed_kernel, grid=(rows,), in_specs=[pl.BlockSpec(memory_s...  48.6 us
    pallas_call x2, Pallas kernels, attend_back(): pl.pallas_call(lambda *refs: attend_back_kernel(lanes, per, *refs[:8], *p...  37.9 us
    pallas_call x1, Pallas kernels, attend(): pl.pallas_call(attend_kernel, grid=(rows,), in_specs=[wide, row_spec((1,...  27 us
    all_to_all x1, blocking collectives, exchange(): return lax.all_to_all(x, axes, 0, 0, axis_index_groups=groups, tiled=True)  18.2 us
    all_to_all x3, starting transfers between devices, exchange(): return lax.all_to_all(x, axes, 0, 0, axis_index_groups=groups, tiled=True)  17.8 us
    pallas_call x7, Pallas kernels, call_sum(): pl.pallas_call(lambda *refs: kernel(*refs[:count], *refs[count + len(afte...  14.7 us
    ppermute x7, starting transfers between devices, on_device(): lax.ppermute(t, 'dp', [(d, d ^ bit) for d in range(dp)])  10.5 us
    pallas_call x1, Pallas kernels, input_grad(): pl.pallas_call(lambda *refs: input_grad_kernel(*refs[:count], *refs[count...  10.2 us
  transfers between devices with their start and end apart: 19, of which 5 were waited for; matrix products, arithmetic and copies ran while one was open for 0% of the time, Pallas kernels for 38%

profile of v3, /device:TPU:0, one launch (start us, length us, event | category | flops | bytes accessed | tf_op | source)
XLA Modules:
  0.0 230.6 jit_solution(7101121767352656747)
XLA Ops:
  7.2 0.7 copy.37
  7.9 1.3 fusion.1.w0_ref
  9.2 2.5 %collective-permute-start.2 = (bf16[4,208,384]{2,1,0:T(8,128)(2,1)S(1)}, bf16[4,208,384]{2,1,0:T(8,128)(2,1)S(1)}, u32[]{:S(2)}, u32[]{:S(2)}) collective-permute-start(bf16[4,208,384]{2,1,0:T(8,128)(2,1)S(1)} %fusion.1.w0_ref), channel_id=1, source_target_pairs={{0,3},{1,2},{2,1},{3,0},{4,7},{5,6},{6,5},{7,4},{8,11},{9,10},{10,... | collective-permute-start | bytes 1916936 | tf_op jit(solution)/shard_map/ppermute | solution.py:697
  11.7 0.6 collective-permute-start.1
  12.3 0.0 collective-permute-start
  12.4 27.0 %attend.1 = (bf16[4,512,768]{2,1,0:T(8,128)(2,1)}, bf16[4,512,768]{2,1,0:T(8,128)(2,1)}, bf16[4,512,768]{2,1,0:T(8,128)(2,1)}, bf16[4,512,768]{2,1,0:T(8,128)(2,...) custom-call(bf16[4,512,768]{2,1,0:T(8,128)(2,1)} %bitcast.26, s32[4,1,512]{2,1,0:T(1,128)} %docs_ref.1, ...), custom_call_target="tpu_custom_call" | custom-call | flops 20000000000 | bytes 50000000 | tf_op jit(solution)/shard_map/attend/pallas_call | solution.py:136
  39.4 0.0 collective-permute-done.2.w3_ref
  39.4 0.0 copy-start.17
  39.4 0.9 collective-permute-done.1.w2_ref
  40.3 0.0 collective-permute-done.w1_ref
  40.3 0.8 copy-done.18
  41.2 0.2 copy-done.19
  41.4 48.6 %feed.1 = (bf16[4,512,768]{2,1,0:T(8,128)(2,1)}, f32[4,512,768]{2,1,0:T(8,128)}, bf16[4,512,768]{2,1,0:T(8,128)(2,1)}, bf16[2304,128]{1,0:T(8,128)(2,1)}, bf16[2...) custom-call(s32[1]{0:T(128)} %bitcast.me_ref.refs_7_, ...), custom_call_target="tpu_custom_call" | custom-call | flops 40000000000 | bytes 50000000 | tf_op jit(solution)/shard_map/feed/pallas_call | solution.py:340
  90.0 0.1 collective-permute-start.3
  90.1 0.5 collective-permute-start.4
  90.6 3.4 %collective-permute-done.4.refs_1_ = bf16[2304,128]{1,0:T(8,128)(2,1)S(1)} collective-permute-done((bf16[2304,128]{1,0:T(8,128)(2,1)}, bf16[2304,128]{1,0:T(8,128)(2,1)S(1)}, u32[]{:S(2)}, u32[]{:S(2)}) %collective-permute-start.4) | collective-permute-done | bytes 589856 | tf_op jit(solution)/shard_map/ppermute | solution.py:697
  94.0 0.8 copy-done.6
  94.8 2.2 add_up.8.refs_11_
  97.0 7.6 %all-to-all-start = ((bf16[16,144,128]{2,1,0:T(8,128)(2,1)}), bf16[16,144,128]{2,1,0:T(8,128)(2,1)S(1)}, u32[]{:S(2)}, u32[]{:S(2)}) async-start(bf16[16,144,128]{2,1,0:T(8,128)(2,1)} %bitcast.19), calls=%async_computation | async-start | bytes 1179648 | tf_op jit(solution)/shard_map/all_to_all | solution.py:661
  104.6 0.0 all-gather.3.cloned.1.call-start
  104.7 0.0 collective-permute-done.3.refs_1_
  104.7 0.0 copy-start
  104.7 1.0 copy-done
  105.7 2.4 %add_up.7.refs_10_ = bf16[2304,128]{1,0:T(8,128)(2,1)} custom-call(bf16[2304,128]{1,0:T(8,128)(2,1)} %get-tuple-element.64.refs_0_, bf16[4608,128]{1,0:T(8,128)(2,1)} %copy-done), custom_call_target="tpu_custom_call" | custom-call | tf_op jit(solution)/shard_map/add_up/pallas_call | solution.py:461
  108.1 1.9 collective-permute-start.5
  110.0 18.8 %attend_back.2 = (bf16[4,3,512,384]{3,2,1,0:T(8,128)(2,1)}, bf16[1872,128]{1,0:T(8,128)(2,1)}) custom-call(bf16[4,512,768]{2,1,0:T(8,128)(2,1)} %bitcast.28, bf16[4,512,768]{2,1,0:T(8,128)(2,1)} %get-tuple-element.57.refs_1_, bf16[4,512,768]{2,1,0:T(8,128)(2,1)} %get-tuple-element.58.refs_2_, bf16[4,512,768]{2,1,0:T(8,128)(2,1)} %get-tuple-element.59.refs_3_, ...), custom_call_target="tpu_custom_call" | custom-call | flops 20000000000 | bytes 30000000 | tf_op jit(solution)/shard_map/attend_back/pallas_call | solution.py:524
  128.8 0.0 all-to-all-done.refs_0_
  128.8 0.0 copy-start.1
  128.8 0.8 copy-done.1
  129.6 1.8 add_up.10.refs_10_
  131.4 0.0 all-gather.3.cloned.1.call-update
  131.4 0.0 collective-permute-done.5.refs_2_
  131.4 0.0 copy-start.7
  131.4 0.8 copy-done.7
  132.2 2.6 %add_up.9.refs_9_ = bf16[2304,128]{1,0:T(8,128)(2,1)} custom-call(bf16[2304,128]{1,0:T(8,128)(2,1)} %get-tuple-element.70.refs_0_, bf16[4608,128]{1,0:T(8,128)(2,1)} %copy-done, bf16[2304,128]{1,0:T(8,128)(2,1)} %copy-done.7, bf16[1872,128]{1,0:T(8,128)(2,1)} %get-tuple-element.69.refs_3_.refs_1_.refs_8_), custom_call_target="tpu_custom_call" | custom-call | tf_op jit(solution)/shard_map/add_up/pallas_call | solution.py:461
  134.8 5.4 %all-to-all-start.1 = ((bf16[8,288,128]{2,1,0:T(8,128)(2,1)}), bf16[8,288,128]{2,1,0:T(8,128)(2,1)S(1)}, u32[]{:S(2)}, u32[]{:S(2)}) async-start(bf16[8,288,128]{2,1,0:T(8,128)(2,1)} %bitcast.20), calls=%async_computation.1 | async-start | bytes 1179648 | tf_op jit(solution)/shard_map/all_to_all | solution.py:661
  140.3 19.1 %attend_back.3 = (bf16[4,3,512,384]{3,2,1,0:T(8,128)(2,1)}, bf16[1920,128]{1,0:T(8,128)(2,1)}, bf16[1920,128]{1,0:T(8,128)(2,1)}) custom-call(bf16[4,512,768]{2,1,0:T(8,128)(2,1)} %bitcast.29, bf16[4,512,768]{2,1,0:T(8,128)(2,1)} %get-tuple-element.57.refs_1_, bf16[4,512,768]{2,1,0:T(8,128)(2,1)} %get-tuple-element.58.refs_2_, ...), custom_call_target="tpu_custom_call" | custom-call | flops 20000000000 | bytes 30000000 | tf_op jit(solution)/shard_map/attend_back/pallas_call | solution.py:524
  159.4 0.1 collective-permute-start.6
  159.5 0.0 copy-start.2
  159.5 0.8 copy-done.2
  160.3 1.8 add_up.11.refs_2_.refs_0_
  162.1 2.9 %collective-permute-start.7 = (bf16[288,128]{1,0:T(8,128)(2,1)}, bf16[288,128]{1,0:T(8,128)(2,1)S(1)}, u32[]{:S(2)}, u32[]{:S(2)}) collective-permute-start(bf16[288,128]{1,0:T(8,128)(2,1)} %add_up.11.refs_2_.refs_0_), channel_id=1, source_target_pairs={{0,16},{4,20},{8,24},{12,28},{16,0},{20,4},{24,8},{28,12},{1,17},{... | collective-permute-start | bytes 221192 | tf_op jit(solution)/shard_map/ppermute | solution.py:724
  165.0 1.5 collective-permute-start.8
  166.5 3.6 %collective-permute-done.7.refs_3_.refs_1_ = bf16[288,128]{1,0:T(8,128)(2,1)S(1)} collective-permute-done((bf16[288,128]{1,0:T(8,128)(2,1)}, bf16[288,128]{1,0:T(8,128)(2,1)S(1)}, u32[]{:S(2)}, u32[]{:S(2)}) %collective-permute-start.7) | collective-permute-done | bytes 73760 | tf_op jit(solution)/shard_map/ppermute | solution.py:724
  170.2 0.7 collective-permute-start.9
  170.8 1.5 collective-permute-start.10
  172.3 0.0 collective-permute-done.6.refs_1_
  172.3 0.8 copy-done.9
  173.1 2.1 add_up.12.refs_6_
  175.1 4.7 %all-to-all-start.2 = ((bf16[16,120,128]{2,1,0:T(8,128)(2,1)}), bf16[16,120,128]{2,1,0:T(8,128)(2,1)S(1)}, u32[]{:S(2)}, u32[]{:S(2)}) async-start(bf16[16,120,128]{2,1,0:T(8,128)(2,1)} %bitcast.23), calls=%async_computation.2 | async-start | bytes 983040 | tf_op jit(solution)/shard_map/all_to_all | solution.py:661
  179.9 1.9 collective-permute-start.11
  181.8 0.2 collective-permute-start.12
  182.0 0.0 collective-permute-done.9.refs_4_.refs_3_
  182.0 1.9 collective-permute-start.13
  183.9 10.2 %input_grad.1.refs_1_ = bf16[4,512,768]{2,1,0:T(8,128)(2,1)} custom-call(f32[4,512,768]{2,1,0:T(8,128)} %get-tuple-element.56.refs_0_, bf16[4,3,512,384]{3,2,1,0:T(8,128)(2,1)} %get-tuple-element.68.refs_1_, bf16[4,3,512,384]{3,2,1,0:T(8,128)(2,1)} %get-tuple-element.71.refs_1_.refs_2_, bf16[4,192,192]{2,1,0:T(8,128)(2,1)} %refs_3_.1, ...), custom_call_target="tpu_custom_call" | custom-call | flops 10000000000 | bytes 20000000 | tf_op jit(solution)/shard_map/input_grad/pallas_call | solution.py:571
  194.1 0.0 collective-permute-done.10.refs_5_.refs_4_
  194.2 0.7 all-to-all-done.2.refs_0_
  194.9 0.7 copy-done.4
  195.7 1.9 add_up.13
  197.6 18.2 %all_to_all.20 = bf16[16,120,128]{2,1,0:T(8,128)(2,1)S(1)} all-to-all(bf16[16,120,128]{2,1,0:T(8,128)(2,1)} %add_up.13), channel_id=1, replica_groups={{0,2,4,6,8,10,12,14,16,18,20,22,24,26,28,30},{1,3,5,7,9,11,13,15,17,19,..., dimensions={0} | all-to-all | bytes 983040 | tf_op jit(solution)/shard_map/all_to_all | solution.py:661
  215.7 0.7 pad_add_fusion.me_ref
  216.4 1.2 collective-permute-done.14.refs_10_
  217.6 0.8 copy-done.8
  218.4 5.3 %unpack.1 = (f32[4,192,192]{2,1,0:T(8,128)}, f32[4,192,192]{2,1,0:T(8,128)}, f32[768,768]{1,0:T(8,128)}, f32[4,192,192]{2,1,0:T(8,128)}, f32[4,192,192]{2,1,0:T(...) custom-call(s32[2]{0:T(128)} %pad_add_fusion.me_ref, ...), custom_call_target="tpu_custom_call" | custom-call | tf_op jit(solution)/shard_map/unpack/pallas_call | solution.py:647
  (32 shorter events, 0.1 us)
Async XLA Ops:
  9.2 30.1 %copy-start.5 = (bf16[4,208,384]{2,1,0:T(8,128)(2,1)}, bf16[4,208,384]{2,1,0:T(8,128)(2,1)S(1)}, u32[]{:S(2)}) copy-start(bf16[4,208,384]{2,1,0:T(8,128)(2,1)S(1)} %fusion.1.w0_ref) | copy-start | bytes 1916932
  9.2 30.1 %collective-permute-start.2 = (bf16[4,208,384]{2,1,0:T(8,128)(2,1)S(1)}, bf16[4,208,384]{2,1,0:T(8,128)(2,1)S(1)}, u32[]{:S(2)}, u32[]{:S(2)}) collective-permute-start(bf16[4,208,384]{2,1,0:T(8,128)(2,1)S(1)} %fusion.1.w0_ref), channel_id=1, source_target_pairs={{0,3},{1,2},{2,1},{3,0},{4,7},{5,6},{6,5},{7,4},{8,11},{9,10},{10,... | collective-permute-start | bytes 1916936 | tf_op jit(solution)/shard_map/ppermute | solution.py:697
  11.7 28.6 %collective-permute-start.1 = (bf16[4,208,384]{2,1,0:T(8,128)(2,1)S(1)}, bf16[4,208,384]{2,1,0:T(8,128)(2,1)S(1)}, u32[]{:S(2)}, u32[]{:S(2)}) collective-permute-start(bf16[4,208,384]{2,1,0:T(8,128)(2,1)S(1)} %fusion.1.w0_ref), channel_id=1, source_target_pairs={{0,2},{1,3},{2,0},{3,1},{4,6},{5,7},{6,4},{7,5},{8,10},{9,11},{10,... | collective-permute-start | bytes 1916936 | tf_op jit(solution)/shard_map/ppermute | solution.py:697
  12.3 28.0 %collective-permute-start = (bf16[4,208,384]{2,1,0:T(8,128)(2,1)S(1)}, bf16[4,208,384]{2,1,0:T(8,128)(2,1)S(1)}, u32[]{:S(2)}, u32[]{:S(2)}) collective-permute-start(bf16[4,208,384]{2,1,0:T(8,128)(2,1)S(1)} %fusion.1.w0_ref), channel_id=1, source_target_pairs={{0,1},{1,0},{2,3},{3,2},{4,5},{5,4},{6,7},{7,6},{8,9},{9,8},{10,11... | collective-permute-start | bytes 1916936 | tf_op jit(solution)/shard_map/ppermute | solution.py:697
  39.4 1.0 copy-start.17
  40.3 0.8 copy-start.18
  40.3 1.0 copy-start.19
  90.0 14.7 %collective-permute-start.3 = (bf16[4608,128]{1,0:T(8,128)(2,1)}, bf16[4608,128]{1,0:T(8,128)(2,1)S(1)}, u32[]{:S(2)}, u32[]{:S(2)}) collective-permute-start(bf16[4608,128]{1,0:T(8,128)(2,1)} %get-tuple-element.65), channel_id=1, source_target_pairs={{0,1},{1,0},{2,3},{3,2},{4,5},{5,4},{6,7},{7,6},{8,9},{9,8},{10,11... | collective-permute-start | bytes 3538952 | tf_op jit(solution)/shard_map/ppermute | solution.py:697
  90.1 3.9 %collective-permute-start.4 = (bf16[2304,128]{1,0:T(8,128)(2,1)}, bf16[2304,128]{1,0:T(8,128)(2,1)S(1)}, u32[]{:S(2)}, u32[]{:S(2)}) collective-permute-start(bf16[2304,128]{1,0:T(8,128)(2,1)} %get-tuple-element.67), channel_id=1, source_target_pairs={{0,1},{1,0},{2,3},{3,2},{4,5},{5,4},{6,7},{7,6},{8,9},{9,8},{10,11... | collective-permute-start | bytes 1769480 | tf_op jit(solution)/shard_map/ppermute | solution.py:697
  94.0 0.8 copy-start.6
  97.0 31.8 %all-to-all-start = ((bf16[16,144,128]{2,1,0:T(8,128)(2,1)}), bf16[16,144,128]{2,1,0:T(8,128)(2,1)S(1)}, u32[]{:S(2)}, u32[]{:S(2)}) async-start(bf16[16,144,128]{2,1,0:T(8,128)(2,1)} %bitcast.19), calls=%async_computation | async-start | bytes 1179648 | tf_op jit(solution)/shard_map/all_to_all | solution.py:661
  104.6 90.3 %all-gather.3.cloned.1.call-start = ((), (), s32[]{:S(2)}) async-start(), calls=%async_computation.4 | async-start | bytes 1216512 | tf_op jit(solution)/shard_map/all_gather | solution.py:718
  104.7 1.0 copy-start
  108.1 23.3 %collective-permute-start.5 = (bf16[2304,128]{1,0:T(8,128)(2,1)}, bf16[2304,128]{1,0:T(8,128)(2,1)S(1)}, u32[]{:S(2)}, u32[]{:S(2)}) collective-permute-start(bf16[2304,128]{1,0:T(8,128)(2,1)} %add_up.7.refs_10_), channel_id=1, source_target_pairs={{0,2},{1,3},{2,0},{3,1},{4,6},{5,7},{6,4},{7,5},{8,10},{9,11},{10,... | collective-permute-start | bytes 1769480 | tf_op jit(solution)/shard_map/ppermute | solution.py:697
  128.8 0.8 copy-start.1
  131.4 0.8 copy-start.7
  134.8 24.7 %all-to-all-start.1 = ((bf16[8,288,128]{2,1,0:T(8,128)(2,1)}), bf16[8,288,128]{2,1,0:T(8,128)(2,1)S(1)}, u32[]{:S(2)}, u32[]{:S(2)}) async-start(bf16[8,288,128]{2,1,0:T(8,128)(2,1)} %bitcast.20), calls=%async_computation.1 | async-start | bytes 1179648 | tf_op jit(solution)/shard_map/all_to_all | solution.py:661
  159.4 12.9 %collective-permute-start.6 = (bf16[1920,128]{1,0:T(8,128)(2,1)}, bf16[1920,128]{1,0:T(8,128)(2,1)S(1)}, u32[]{:S(2)}, u32[]{:S(2)}) collective-permute-start(bf16[1920,128]{1,0:T(8,128)(2,1)} %get-tuple-element.73), channel_id=1, source_target_pairs={{0,1},{1,0},{2,3},{3,2},{4,5},{5,4},{6,7},{7,6},{8,9},{9,8},{10,11... | collective-permute-start | bytes 1474568 | tf_op jit(solution)/shard_map/ppermute | solution.py:697
  159.5 0.8 copy-start.2
  162.1 8.0 %collective-permute-start.7 = (bf16[288,128]{1,0:T(8,128)(2,1)}, bf16[288,128]{1,0:T(8,128)(2,1)S(1)}, u32[]{:S(2)}, u32[]{:S(2)}) collective-permute-start(bf16[288,128]{1,0:T(8,128)(2,1)} %add_up.11.refs_2_.refs_0_), channel_id=1, source_target_pairs={{0,16},{4,20},{8,24},{12,28},{16,0},{20,4},{24,8},{28,12},{1,17},{... | collective-permute-start | bytes 221192 | tf_op jit(solution)/shard_map/ppermute | solution.py:724
  165.0 16.8 %collective-permute-start.8 = (bf16[288,128]{1,0:T(8,128)(2,1)}, bf16[288,128]{1,0:T(8,128)(2,1)S(1)}, u32[]{:S(2)}, u32[]{:S(2)}) collective-permute-start(bf16[288,128]{1,0:T(8,128)(2,1)} %add_up.11.refs_2_.refs_0_), channel_id=1, source_target_pairs={{0,8},{4,12},{8,0},{12,4},{16,24},{20,28},{24,16},{28,20},{1,9},{5... | collective-permute-start | bytes 221192 | tf_op jit(solution)/shard_map/ppermute | solution.py:724
  170.2 2.1 copy-start.10
  170.2 11.8 %collective-permute-start.9 = (bf16[288,128]{1,0:T(8,128)(2,1)S(1)}, bf16[288,128]{1,0:T(8,128)(2,1)S(1)}, u32[]{:S(2)}, u32[]{:S(2)}) collective-permute-start(bf16[288,128]{1,0:T(8,128)(2,1)S(1)} %collective-permute-done.7.refs_3_.refs_1_), channel_id=1, source_target_pairs={{0,8},{4,12},{8,0},{12,4},{16,24},{20,28},{24,16},{28,20},{1,9},{5... | collective-permute-start | bytes 221192 | tf_op jit(solution)/shard_map/ppermute | solution.py:724
  170.8 23.3 %collective-permute-start.10 = (bf16[288,128]{1,0:T(8,128)(2,1)}, bf16[288,128]{1,0:T(8,128)(2,1)S(1)}, u32[]{:S(2)}, u32[]{:S(2)}) collective-permute-start(bf16[288,128]{1,0:T(8,128)(2,1)} %add_up.11.refs_2_.refs_0_), channel_id=1, source_target_pairs={{0,4},{4,0},{8,12},{12,8},{16,20},{20,16},{24,28},{28,24},{1,5},{5... | collective-permute-start | bytes 221192 | tf_op jit(solution)/shard_map/ppermute | solution.py:724
  172.3 0.8 copy-start.9
  175.1 19.7 %all-to-all-start.2 = ((bf16[16,120,128]{2,1,0:T(8,128)(2,1)}), bf16[16,120,128]{2,1,0:T(8,128)(2,1)S(1)}, u32[]{:S(2)}, u32[]{:S(2)}) async-start(bf16[16,120,128]{2,1,0:T(8,128)(2,1)} %bitcast.23), calls=%async_computation.2 | async-start | bytes 983040 | tf_op jit(solution)/shard_map/all_to_all | solution.py:661
  179.9 14.2 %collective-permute-start.11 = (bf16[288,128]{1,0:T(8,128)(2,1)}, bf16[288,128]{1,0:T(8,128)(2,1)S(1)}, u32[]{:S(2)}, u32[]{:S(2)}) collective-permute-start(bf16[288,128]{1,0:T(8,128)(2,1)} %copy-done.10), channel_id=1, source_target_pairs={{0,4},{4,0},{8,12},{12,8},{16,20},{20,16},{24,28},{28,24},{1,5},{5... | collective-permute-start | bytes 221192 | tf_op jit(solution)/shard_map/ppermute | solution.py:724
  181.8 12.3 %copy-start.11 = (bf16[288,128]{1,0:T(8,128)(2,1)}, bf16[288,128]{1,0:T(8,128)(2,1)S(1)}, u32[]{:S(2)}) copy-start(bf16[288,128]{1,0:T(8,128)(2,1)S(1)} %collective-permute-done.8.refs_3_.refs_2_) | copy-start | bytes 221188
  181.8 12.3 %collective-permute-start.12 = (bf16[288,128]{1,0:T(8,128)(2,1)S(1)}, bf16[288,128]{1,0:T(8,128)(2,1)S(1)}, u32[]{:S(2)}, u32[]{:S(2)}) collective-permute-start(bf16[288,128]{1,0:T(8,128)(2,1)S(1)} %collective-permute-done.8.refs_3_.refs_2_), channel_id=1, source_target_pairs={{0,4},{4,0},{8,12},{12,8},{16,20},{20,16},{24,28},{28,24},{1,5},{5... | collective-permute-start | bytes 221192 | tf_op jit(solution)/shard_map/ppermute | solution.py:724
  182.0 12.1 %copy-start.12 = (bf16[288,128]{1,0:T(8,128)(2,1)}, bf16[288,128]{1,0:T(8,128)(2,1)S(1)}, u32[]{:S(2)}) copy-start(bf16[288,128]{1,0:T(8,128)(2,1)S(1)} %collective-permute-done.9.refs_4_.refs_3_) | copy-start | bytes 221188
  182.0 12.2 %collective-permute-start.13 = (bf16[288,128]{1,0:T(8,128)(2,1)S(1)}, bf16[288,128]{1,0:T(8,128)(2,1)S(1)}, u32[]{:S(2)}, u32[]{:S(2)}) collective-permute-start(bf16[288,128]{1,0:T(8,128)(2,1)S(1)} %collective-permute-done.9.refs_4_.refs_3_), channel_id=1, source_target_pairs={{0,4},{4,0},{8,12},{12,8},{16,20},{20,16},{24,28},{28,24},{1,5},{5... | collective-permute-start | bytes 221192 | tf_op jit(solution)/shard_map/ppermute | solution.py:724
  194.1 0.8 copy-start.13
  194.1 0.8 copy-start.15
  194.1 0.8 copy-start.14
  194.2 0.7 copy-start.16
  194.9 0.8 copy-start.4
  215.7 1.9 copy-start.3
  215.7 1.9 collective-permute-start.14
  217.6 0.8 copy-start.8
Sparse Core Ops, SparseCore 0:
  131.5 57.4 all-gather.2

commit v4 on v3

--- a/solution.py
+++ b/solution.py
@@ -16,6 +16,7 @@
 bf16 = jnp.bfloat16
 f32 = jnp.float32
 VMEM_LIMIT = 60 * 1024 * 1024
+SMALL_LIMIT = 30 * 1024 * 1024
 
 OUT_BIAS, MIXED_GAIN, MIXED_BIAS, SHRINK_BIAS, FINAL_GAIN, FINAL_BIAS, QUERY_BIAS, VALUE_BIAS = range(8)
 
@@ -463,7 +464,7 @@
         in_specs=[whole()] * count + [unused()] * len(after),
         out_specs=whole(),
         out_shape=jax.ShapeDtypeStruct(shape, bf16),
-        compiler_params=pltpu.CompilerParams(vmem_limit_bytes=VMEM_LIMIT),
+        compiler_params=pltpu.CompilerParams(vmem_limit_bytes=SMALL_LIMIT),
         name="add_up",
     )(*args, *after)
 
@@ -480,6 +481,22 @@
         refs[-1][...] = acc.astype(bf16)
 
     return call_sum(kernel, arrays, shape, after)
+
+
+def add_both(keep_w, core_w, far_e, core_e):
+    def kernel(kw_ref, cw_ref, fe_ref, ce_ref, w_ref, e_ref):
+        w_ref[...] = (kw_ref[...].astype(f32) + cw_ref[...].astype(f32)).astype(bf16)
+        half = fe_ref.shape[0]
+        e_ref[...] = (fe_ref[...].astype(f32) + ce_ref[half:].astype(f32)).astype(bf16)
+
+    return pl.pallas_call(
+        kernel,
+        in_specs=[whole()] * 4,
+        out_specs=[whole()] * 2,
+        out_shape=[jax.ShapeDtypeStruct(t.shape, bf16) for t in (keep_w, far_e)],
+        compiler_params=pltpu.CompilerParams(vmem_limit_bytes=SMALL_LIMIT),
+        name="add_up",
+    )(keep_w, core_w, far_e, core_e)
 
 
 def total(x, after=(), copies=0):
@@ -563,22 +580,30 @@
         dx_ref[0, :, lanes] = (col + dh1_ref[0, :, lanes]).astype(bf16)
 
 
-def input_grad(dh1, d0, d1, wq, wk, wv, after=()):
+def input_grad(dh1, d0, d1, wq, wk, wv, half, prev=None, after=()):
     rows, length, width = dh1.shape
-    wide = row_spec((length, width))
-    back = pl.BlockSpec((1, 3, length, width // 2), lambda r: (r, 0, 0, 0))
-    count = 6
+    count = rows // 2 if half == 0 else rows - rows // 2
+    first = half * (rows // 2)
+    wide = pl.BlockSpec((1, length, width), lambda r: (r + first, 0, 0))
+    back = pl.BlockSpec((1, 3, length, width // 2), lambda r: (r + first, 0, 0, 0))
+    args = [dh1, d0, d1, wq, wk, wv]
+    extra = list(after)
+    aliases = {}
+    if prev is not None:
+        aliases = {len(args) + len(extra): 0}
+        extra.append(prev)
     return pl.pallas_call(
-        lambda *refs: input_grad_kernel(*refs[:count], *refs[count + len(after):]),
-        grid=(rows,),
-        in_specs=[wide, back, back] + [full(wq.shape)] * 3 + [unused()] * len(after),
+        lambda *refs: input_grad_kernel(*refs[:len(args)], *refs[len(args) + len(extra):]),
+        grid=(count,),
+        in_specs=[wide, back, back] + [full(wq.shape)] * 3 + [unused()] * len(extra),
         out_specs=wide,
         out_shape=jax.ShapeDtypeStruct((rows, length, width), bf16),
+        input_output_aliases=aliases,
         scratch_shapes=[pltpu.VMEM((3, wq.shape[0], 256, 256), bf16)],
-        compiler_params=pltpu.CompilerParams(vmem_limit_bytes=VMEM_LIMIT),
-        cost_estimate=pl.CostEstimate(flops=int(1e10), bytes_accessed=int(2e7), transcendentals=0),
+        compiler_params=pltpu.CompilerParams(vmem_limit_bytes=SMALL_LIMIT),
+        cost_estimate=pl.CostEstimate(flops=int(5e9), bytes_accessed=int(1e7), transcendentals=0),
         name="input_grad",
-    )(dh1, d0, d1, wq, wk, wv, *after)
+    )(*args, *extra)
 
 
 def unpack_kernel(order, me_ref, *refs):
@@ -652,7 +677,7 @@
         scratch_shapes=[pltpu.VMEM((len(pieces) * pieces[0].shape[0], 128), f32),
                         pltpu.VMEM((w.shape[0] * w.shape[1], 128), f32),
                         pltpu.VMEM((2 * own.shape[0], 128), bf16)],
-        compiler_params=pltpu.CompilerParams(vmem_limit_bytes=VMEM_LIMIT),
+        compiler_params=pltpu.CompilerParams(vmem_limit_bytes=SMALL_LIMIT),
         name="unpack",
     )(place, *pieces, w, own, other)
 
@@ -706,14 +731,13 @@
 
     core_w = swap(send_w, 1)
     core_e = swap(send_e, 1)
-    sum_w = add((keep_w, core_w))
-    far = add((far_e, core_e), (None, 1))
+    sum_w, far = add_both(keep_w, core_w, far_e, core_e)
     got_w = exchange(sum_w.reshape(2 * dp, -1, 128), everyone, like)
     far_got = swap(far, 2)
     back = functools.partial(attend_back, x, q, k, v, c, dc, p, me=me, per=per)
     d0, flat0 = back(part=0, vec=gvec, gbe=gbe, after=(far, sum_w))
     piece_w = total(got_w, after=(flat0,))
-    sum_e = add((near_e, core_e, far_got), (None, 0, None), after=(flat0,))
+    sum_e = add((near_e, core_e, far_got), (None, 0, None), after=(piece_w,))
     got_e = exchange(sum_e.reshape(dp, -1, 128), "dp")
     all_w = lax.all_gather(piece_w, everyone)
     d1, keep_q, send_q = back(part=1, prev=flat0, devices=count, after=(sum_e, piece_w))
@@ -724,10 +748,12 @@
         pieces = pieces + [lax.ppermute(t, "dp", [(d, d ^ bit) for d in range(dp)]) for t in pieces]
         order = order + [n ^ bit for n in order]
         bit //= 2
-    sum_q = add((keep_q, swap(send_q, 1)), after=(piece_e, pieces[1]))
+    sum_q = add((keep_q, swap(send_q, 1)))
     got_q = exchange(sum_q.reshape(2 * dp, -1, 128), everyone, like)
-    dx = input_grad(dh1, d0, d1, query_weight, key_weight, value_weight, after=(sum_q,))
-    piece_q = total(got_q, after=(dx, all_w, *pieces[2:]), copies=2 * dp)
+    back_weights = (query_weight, key_weight, value_weight)
+    dx = input_grad(dh1, d0, d1, *back_weights, half=0, after=(sum_q, pieces[1]))
+    dx = input_grad(dh1, d0, d1, *back_weights, half=1, prev=dx, after=pieces[2:4])
+    piece_q = total(got_q, after=(dx, all_w, *pieces[4:]), copies=2 * dp)
     own_q = exchange(piece_q, everyone, like).reshape(-1, 128)
     other_q = swap(own_q, 1)
     place = jnp.stack([lax.axis_index("ffn"), lax.axis_index("dp")]).astype(jnp.int32)

time: 231 us -> 223 us (0.965)
  Pallas kernels: 144 us -> 128 us
  local copies, waits for them, and re-layouts: 8.34 us -> 18.1 us
    pallas_call x7 -> x5, Pallas kernels: 14.7 us -> 2.78 us  [call_sum(): pl.pallas_call(lambda *refs: kernel(*refs[:count], *refs[count + len(afte...]
    unnamed x40, local copies, waits for them, and re-layouts: 7.65 us -> 17.4 us
    ppermute x7, waiting for transfers between devices: 3.66 us -> 0.5 us  [on_device(): lax.ppermute(t, 'dp', [(d, d ^ bit) for d in range(dp)])]
    pallas_call x1 -> x3, Pallas kernels: 10.2 us -> 7.84 us  [the longest x2 6.83 us: input_grad(): pl.pallas_call(lambda *refs: input_grad_kernel(*refs[:len(args)], *refs[l...]
  transfers between devices with their start and end apart: 19 -> 19, of which waited for: 5 -> 5; matrix products, arithmetic and copies ran while one was open for 0% -> 0% of each run, Pallas kernels for 38% -> 34%
where the time goes in v4:
time: 223 us; the launch traced here: 222 us
  Pallas kernels  128 us (57%)
  starting transfers between devices  32.7 us (15%)
  blocking collectives  19.4 us (9%)
  local copies, waits for them, and re-layouts  18.1 us (8%)
  between operations  14.3 us (6%)
  waiting for transfers between devices  8.12 us (4%)
    pallas_call x1, Pallas kernels, feed(): pl.pallas_call(feed_kernel, grid=(rows,), in_specs=[pl.BlockSpec(memory_s...  48.6 us
    pallas_call x2, Pallas kernels, attend_back(): pl.pallas_call(lambda *refs: attend_back_kernel(lanes, per, *refs[:8], *p...  37.9 us
    pallas_call x1, Pallas kernels, attend(): pl.pallas_call(attend_kernel, grid=(rows,), in_specs=[wide, row_spec((1,...  27 us
    all_to_all x1, blocking collectives, exchange(): return lax.all_to_all(x, axes, 0, 0, axis_index_groups=groups, tiled=True)  19.4 us
    unnamed x40, local copies, waits for them, and re-layouts  17.4 us
    all_to_all x3, starting transfers between devices, exchange(): return lax.all_to_all(x, axes, 0, 0, axis_index_groups=groups, tiled=True)  16.7 us
    ppermute x7, starting transfers between devices, on_device(): lax.ppermute(t, 'dp', [(d, d ^ bit) for d in range(dp)])  10.2 us
    pallas_call x2, Pallas kernels, input_grad(): pl.pallas_call(lambda *refs: input_grad_kernel(*refs[:len(args)], *refs[l...  6.83 us
  transfers between devices with their start and end apart: 19, of which 5 were waited for; matrix products, arithmetic and copies ran while one was open for 0% of the time, Pallas kernels for 34%

profile of v4, /device:TPU:0, one launch (start us, length us, event | category | flops | bytes accessed | tf_op | source)
XLA Modules:
  0.0 222.0 jit_solution(4561892112707401997)
XLA Ops:
  7.2 0.7 copy.38
  7.9 1.3 fusion.1.w0_ref
  9.2 2.5 %collective-permute-start.2 = (bf16[4,208,384]{2,1,0:T(8,128)(2,1)S(1)}, bf16[4,208,384]{2,1,0:T(8,128)(2,1)S(1)}, u32[]{:S(2)}, u32[]{:S(2)}) collective-permute-start(bf16[4,208,384]{2,1,0:T(8,128)(2,1)S(1)} %fusion.1.w0_ref), channel_id=1, source_target_pairs={{0,3},{1,2},{2,1},{3,0},{4,7},{5,6},{6,5},{7,4},{8,11},{9,10},{10,... | collective-permute-start | bytes 1916936 | tf_op jit(solution)/shard_map/ppermute | solution.py:722
  11.7 0.6 collective-permute-start.1
  12.3 0.0 collective-permute-start
  12.4 27.0 %attend.1 = (bf16[4,512,768]{2,1,0:T(8,128)(2,1)}, bf16[4,512,768]{2,1,0:T(8,128)(2,1)}, bf16[4,512,768]{2,1,0:T(8,128)(2,1)}, bf16[4,512,768]{2,1,0:T(8,128)(2,...) custom-call(bf16[4,512,768]{2,1,0:T(8,128)(2,1)} %bitcast.23, s32[4,1,512]{2,1,0:T(1,128)} %docs_ref.1, ...), custom_call_target="tpu_custom_call" | custom-call | flops 20000000000 | bytes 50000000 | tf_op jit(solution)/shard_map/attend/pallas_call | solution.py:137
  39.4 0.0 collective-permute-done.2.w3_ref
  39.4 0.0 copy-start.17
  39.4 0.9 collective-permute-done.1.w2_ref
  40.3 0.0 collective-permute-done.w1_ref
  40.3 0.8 copy-done.18
  41.2 0.2 copy-done.19
  41.4 48.6 %feed.1 = (bf16[4,512,768]{2,1,0:T(8,128)(2,1)}, f32[4,512,768]{2,1,0:T(8,128)}, bf16[4,512,768]{2,1,0:T(8,128)(2,1)}, bf16[2304,128]{1,0:T(8,128)(2,1)}, bf16[2...) custom-call(s32[1]{0:T(128)} %bitcast.me_ref.refs_7_, ...), custom_call_target="tpu_custom_call" | custom-call | flops 40000000000 | bytes 50000000 | tf_op jit(solution)/shard_map/feed/pallas_call | solution.py:341
  90.0 0.1 collective-permute-start.4
  90.1 0.5 collective-permute-start.3
  90.6 3.4 %collective-permute-done.3.cw_ref = bf16[2304,128]{1,0:T(8,128)(2,1)S(1)} collective-permute-done((bf16[2304,128]{1,0:T(8,128)(2,1)}, bf16[2304,128]{1,0:T(8,128)(2,1)S(1)}, u32[]{:S(2)}, u32[]{:S(2)}) %collective-permute-start.3) | collective-permute-done | bytes 589856 | tf_op jit(solution)/shard_map/ppermute | solution.py:722
  93.9 0.0 collective-permute-done.4.ce_ref.refs_1_
  94.0 1.1 copy-done.11
  95.0 1.1 copy-done.12
  96.1 1.0 add_up.6
  97.1 7.6 %all-to-all-start = ((bf16[16,144,128]{2,1,0:T(8,128)(2,1)}), bf16[16,144,128]{2,1,0:T(8,128)(2,1)S(1)}, u32[]{:S(2)}, u32[]{:S(2)}) async-start(bf16[16,144,128]{2,1,0:T(8,128)(2,1)} %bitcast.6), calls=%async_computation | async-start | bytes 1179648 | tf_op jit(solution)/shard_map/all_to_all | solution.py:686
  104.7 0.0 all-gather.3.cloned.1.call-start
  104.8 2.0 collective-permute-start.5
  106.8 18.7 %attend_back.2 = (bf16[4,3,512,384]{3,2,1,0:T(8,128)(2,1)}, bf16[1872,128]{1,0:T(8,128)(2,1)}) custom-call(bf16[4,512,768]{2,1,0:T(8,128)(2,1)} %bitcast.25, bf16[4,512,768]{2,1,0:T(8,128)(2,1)} %get-tuple-element.59.refs_1_, bf16[4,512,768]{2,1,0:T(8,128)(2,1)} %get-tuple-element.60.refs_2_, bf16[4,512,768]{2,1,0:T(8,128)(2,1)} %get-tuple-element.61.refs_3_, ...), custom_call_target="tpu_custom_call" | custom-call | flops 20000000000 | bytes 30000000 | tf_op jit(solution)/shard_map/attend_back/pallas_call | solution.py:541
  125.5 0.0 all-to-all-done.refs_0_
  125.5 0.0 copy-start.14
  125.5 1.0 copy-done.14
  126.6 0.7 add_up.7.refs_3_.refs_10_
  127.3 0.0 all-gather.3.cloned.1.call-update
  127.3 0.0 collective-permute-done.5.refs_2_
  127.3 1.0 add_up.8.refs_9_
  128.3 5.4 %all-to-all-start.1 = ((bf16[8,288,128]{2,1,0:T(8,128)(2,1)}), bf16[8,288,128]{2,1,0:T(8,128)(2,1)S(1)}, u32[]{:S(2)}, u32[]{:S(2)}) async-start(bf16[8,288,128]{2,1,0:T(8,128)(2,1)} %bitcast.7), calls=%async_computation.1 | async-start | bytes 1179648 | tf_op jit(solution)/shard_map/all_to_all | solution.py:686
  133.8 19.2 %attend_back.3 = (bf16[4,3,512,384]{3,2,1,0:T(8,128)(2,1)}, bf16[1920,128]{1,0:T(8,128)(2,1)}, bf16[1920,128]{1,0:T(8,128)(2,1)}) custom-call(bf16[4,512,768]{2,1,0:T(8,128)(2,1)} %bitcast.26, bf16[4,512,768]{2,1,0:T(8,128)(2,1)} %get-tuple-element.59.refs_1_, bf16[4,512,768]{2,1,0:T(8,128)(2,1)} %get-tuple-element.60.refs_2_, ...), custom_call_target="tpu_custom_call" | custom-call | flops 20000000000 | bytes 30000000 | tf_op jit(solution)/shard_map/attend_back/pallas_call | solution.py:541
  153.0 0.1 collective-permute-start.9
  153.1 2.4 %copy-done = bf16[4,3,512,384]{3,2,1,0:T(8,128)(2,1)S(1)} copy-done((bf16[4,3,512,384]{3,2,1,0:T(8,128)(2,1)S(1)}, bf16[4,3,512,384]{3,2,1,0:T(8,128)(2,1)}, u32[]{:S(2)}) %copy-start) | copy-done | bytes 4718616
  155.4 0.1 add_up.9.refs_0_
  155.5 3.0 %collective-permute-start.7 = (bf16[288,128]{1,0:T(8,128)(2,1)S(1)}, bf16[288,128]{1,0:T(8,128)(2,1)S(1)}, u32[]{:S(2)}, u32[]{:S(2)}) collective-permute-start(bf16[288,128]{1,0:T(8,128)(2,1)S(1)} %add_up.9.refs_0_), channel_id=1, source_target_pairs={{0,16},{4,20},{8,24},{12,28},{16,0},{20,4},{24,8},{28,12},{1,17},{... | collective-permute-start | bytes 221192 | tf_op jit(solution)/shard_map/ppermute | solution.py:748
  158.5 1.4 collective-permute-start.6
  160.0 0.0 collective-permute-done.9.refs_1_
  160.0 0.9 add_up.10.refs_6_
  160.9 3.6 %all-to-all-start.2 = ((bf16[16,120,128]{2,1,0:T(8,128)(2,1)}), bf16[16,120,128]{2,1,0:T(8,128)(2,1)S(1)}, u32[]{:S(2)}, u32[]{:S(2)}) async-start(bf16[16,120,128]{2,1,0:T(8,128)(2,1)} %bitcast.12), calls=%async_computation.2 | async-start | bytes 983040 | tf_op jit(solution)/shard_map/all_to_all | solution.py:686
  164.4 1.8 collective-permute-start.10
  166.3 0.0 collective-permute-done.7.refs_7_.refs_1_
  166.3 0.3 collective-permute-start.11
  166.5 1.8 collective-permute-start.8
  168.3 1.5 collective-permute-start.12
  169.8 2.5 %copy-done.1 = bf16[4,3,512,384]{3,2,1,0:T(8,128)(2,1)S(1)} copy-done((bf16[4,3,512,384]{3,2,1,0:T(8,128)(2,1)S(1)}, bf16[4,3,512,384]{3,2,1,0:T(8,128)(2,1)}, u32[]{:S(2)}) %copy-start.1) | copy-done | bytes 4718616
  172.3 2.8 %copy-done.3 = f32[4,512,768]{2,1,0:T(8,128)S(1)} copy-done((f32[4,512,768]{2,1,0:T(8,128)S(1)}, f32[4,512,768]{2,1,0:T(8,128)}, u32[]{:S(2)}) %copy-start.3) | copy-done | bytes 6291480
  175.1 2.3 %copy-done.4 = bf16[4,3,512,384]{3,2,1,0:T(8,128)(2,1)S(1)} copy-done((bf16[4,3,512,384]{3,2,1,0:T(8,128)(2,1)S(1)}, bf16[4,3,512,384]{3,2,1,0:T(8,128)(2,1)}, u32[]{:S(2)}) %copy-start.4) | copy-done | bytes 4718616
  177.4 3.4 %input_grad.2.refs_8_ = bf16[4,512,768]{2,1,0:T(8,128)(2,1)} custom-call(f32[4,512,768]{2,1,0:T(8,128)S(1)} %copy-done.3, bf16[4,3,512,384]{3,2,1,0:T(8,128)(2,1)S(1)} %copy-done.4, bf16[4,3,512,384]{3,2,1,0:T(8,128)(2,1)S(1)} %copy-done.1, bf16[4,192,192]{2,1,0:T(8,128)(2,1)S(1)} %copy-done.7, bf16[4,192,192]{2,1,0:T(8,128)(2,1)S(1)} %copy-done.8, ...), custom_call_target="tpu_custom_call" | custom-call | flops 5000000000 | bytes 10000000 | tf_op jit(solution)/shard_map/input_grad/pallas_call | solution.py:595
  180.8 0.4 collective-permute-start.13
  181.3 3.4 %input_grad.3.refs_1_ = bf16[4,512,768]{2,1,0:T(8,128)(2,1)} custom-call(f32[4,512,768]{2,1,0:T(8,128)S(1)} %copy-done.3, bf16[4,3,512,384]{3,2,1,0:T(8,128)(2,1)S(1)} %copy-done.4, bf16[4,3,512,384]{3,2,1,0:T(8,128)(2,1)S(1)} %copy-done.1, bf16[4,192,192]{2,1,0:T(8,128)(2,1)S(1)} %copy-done.7, ...), custom_call_target="tpu_custom_call", output_to_operand_aliasing={{}: (8, {})} | custom-call | flops 5000000000 | bytes 10000000 | tf_op jit(solution)/shard_map/input_grad/pallas_call | solution.py:595
  184.7 0.0 collective-permute-done.10.refs_3_.refs_4_
  184.7 0.0 collective-permute-done.11.refs_4_.refs_5_
  184.7 0.0 collective-permute-done.12.refs_5_.refs_6_
  184.7 0.5 collective-permute-done.13.refs_6_.refs_7_
  185.2 1.5 all-gather.3.cloned.1.call-done
  186.7 1.9 copy-done.2
  188.6 1.3 copy-done.5
  189.8 0.1 add_up.11
  189.9 19.4 %all_to_all.20 = bf16[16,120,128]{2,1,0:T(8,128)(2,1)S(1)} all-to-all(bf16[16,120,128]{2,1,0:T(8,128)(2,1)S(1)} %add_up.11), channel_id=1, replica_groups={{0,2,4,6,8,10,12,14,16,18,20,22,24,26,28,30},{1,3,5,7,9,11,13,15,17,19,..., dimensions={0} | all-to-all | bytes 983040 | tf_op jit(solution)/shard_map/all_to_all | solution.py:686
  209.4 0.1 pad_add_fusion.me_ref
  209.4 1.8 collective-permute-done.14.refs_10_
  211.2 4.0 %unpack.1 = (f32[4,192,192]{2,1,0:T(8,128)}, f32[4,192,192]{2,1,0:T(8,128)}, f32[768,768]{1,0:T(8,128)}, f32[4,192,192]{2,1,0:T(8,128)}, f32[4,192,192]{2,1,0:T(...) custom-call(s32[2]{0:T(128)S(1)} %pad_add_fusion.me_ref, ...), custom_call_target="tpu_custom_call" | custom-call | tf_op jit(solution)/shard_map/unpack/pallas_call | solution.py:672
  (32 shorter events, 0.1 us)
Async XLA Ops:
  9.2 30.1 %copy-start.16 = (bf16[4,208,384]{2,1,0:T(8,128)(2,1)}, bf16[4,208,384]{2,1,0:T(8,128)(2,1)S(1)}, u32[]{:S(2)}) copy-start(bf16[4,208,384]{2,1,0:T(8,128)(2,1)S(1)} %fusion.1.w0_ref) | copy-start | bytes 1916932
  9.2 30.2 %collective-permute-start.2 = (bf16[4,208,384]{2,1,0:T(8,128)(2,1)S(1)}, bf16[4,208,384]{2,1,0:T(8,128)(2,1)S(1)}, u32[]{:S(2)}, u32[]{:S(2)}) collective-permute-start(bf16[4,208,384]{2,1,0:T(8,128)(2,1)S(1)} %fusion.1.w0_ref), channel_id=1, source_target_pairs={{0,3},{1,2},{2,1},{3,0},{4,7},{5,6},{6,5},{7,4},{8,11},{9,10},{10,... | collective-permute-start | bytes 1916936 | tf_op jit(solution)/shard_map/ppermute | solution.py:722
  11.7 28.6 %collective-permute-start.1 = (bf16[4,208,384]{2,1,0:T(8,128)(2,1)S(1)}, bf16[4,208,384]{2,1,0:T(8,128)(2,1)S(1)}, u32[]{:S(2)}, u32[]{:S(2)}) collective-permute-start(bf16[4,208,384]{2,1,0:T(8,128)(2,1)S(1)} %fusion.1.w0_ref), channel_id=1, source_target_pairs={{0,2},{1,3},{2,0},{3,1},{4,6},{5,7},{6,4},{7,5},{8,10},{9,11},{10,... | collective-permute-start | bytes 1916936 | tf_op jit(solution)/shard_map/ppermute | solution.py:722
  12.3 28.0 %collective-permute-start = (bf16[4,208,384]{2,1,0:T(8,128)(2,1)S(1)}, bf16[4,208,384]{2,1,0:T(8,128)(2,1)S(1)}, u32[]{:S(2)}, u32[]{:S(2)}) collective-permute-start(bf16[4,208,384]{2,1,0:T(8,128)(2,1)S(1)} %fusion.1.w0_ref), channel_id=1, source_target_pairs={{0,1},{1,0},{2,3},{3,2},{4,5},{5,4},{6,7},{7,6},{8,9},{9,8},{10,11... | collective-permute-start | bytes 1916936 | tf_op jit(solution)/shard_map/ppermute | solution.py:722
  39.4 0.9 copy-start.17
  40.3 0.8 copy-start.18
  40.3 1.0 copy-start.19
  90.0 4.0 %collective-permute-start.4 = (bf16[4608,128]{1,0:T(8,128)(2,1)}, bf16[4608,128]{1,0:T(8,128)(2,1)S(1)}, u32[]{:S(2)}, u32[]{:S(2)}) collective-permute-start(bf16[4608,128]{1,0:T(8,128)(2,1)} %get-tuple-element.69), channel_id=1, source_target_pairs={{0,1},{1,0},{2,3},{3,2},{4,5},{5,4},{6,7},{7,6},{8,9},{9,8},{10,11... | collective-permute-start | bytes 3538952 | tf_op jit(solution)/shard_map/ppermute | solution.py:722
  90.1 3.9 %collective-permute-start.3 = (bf16[2304,128]{1,0:T(8,128)(2,1)}, bf16[2304,128]{1,0:T(8,128)(2,1)S(1)}, u32[]{:S(2)}, u32[]{:S(2)}) collective-permute-start(bf16[2304,128]{1,0:T(8,128)(2,1)} %get-tuple-element.67), channel_id=1, source_target_pairs={{0,1},{1,0},{2,3},{3,2},{4,5},{5,4},{6,7},{7,6},{8,9},{9,8},{10,11... | collective-permute-start | bytes 1769480 | tf_op jit(solution)/shard_map/ppermute | solution.py:722
  94.0 1.1 copy-start.11
  95.0 1.1 copy-start.12
  97.1 9.7 %copy-start.15 = (bf16[2304,128]{1,0:T(8,128)(2,1)}, bf16[2304,128]{1,0:T(8,128)(2,1)S(1)}, u32[]{:S(2)}) copy-start(bf16[2304,128]{1,0:T(8,128)(2,1)S(1)} %get-tuple-element.70.refs_10_) | copy-start | bytes 1769476
  97.1 28.4 %all-to-all-start = ((bf16[16,144,128]{2,1,0:T(8,128)(2,1)}), bf16[16,144,128]{2,1,0:T(8,128)(2,1)S(1)}, u32[]{:S(2)}, u32[]{:S(2)}) async-start(bf16[16,144,128]{2,1,0:T(8,128)(2,1)} %bitcast.6), calls=%async_computation | async-start | bytes 1179648 | tf_op jit(solution)/shard_map/all_to_all | solution.py:686
  104.7 81.9 %all-gather.3.cloned.1.call-start = ((), (), s32[]{:S(2)}) async-start(), calls=%async_computation.4 | async-start | bytes 1216512 | tf_op jit(solution)/shard_map/all_gather | solution.py:742
  104.8 22.5 %collective-permute-start.5 = (bf16[2304,128]{1,0:T(8,128)(2,1)S(1)}, bf16[2304,128]{1,0:T(8,128)(2,1)S(1)}, u32[]{:S(2)}, u32[]{:S(2)}) collective-permute-start(bf16[2304,128]{1,0:T(8,128)(2,1)S(1)} %get-tuple-element.70.refs_10_), channel_id=1, source_target_pairs={{0,2},{1,3},{2,0},{3,1},{4,6},{5,7},{6,4},{7,5},{8,10},{9,11},{10,... | collective-permute-start | bytes 1769480 | tf_op jit(solution)/shard_map/ppermute | solution.py:722
  106.8 20.5 %copy-start.10 = (bf16[2304,128]{1,0:T(8,128)(2,1)S(1)}, bf16[2304,128]{1,0:T(8,128)(2,1)}, u32[]{:S(2)}) copy-start(bf16[2304,128]{1,0:T(8,128)(2,1)} %get-tuple-element.74.refs_0_) | copy-start | bytes 1769476
  125.5 1.0 copy-start.14
  128.3 24.7 %all-to-all-start.1 = ((bf16[8,288,128]{2,1,0:T(8,128)(2,1)}), bf16[8,288,128]{2,1,0:T(8,128)(2,1)S(1)}, u32[]{:S(2)}, u32[]{:S(2)}) async-start(bf16[8,288,128]{2,1,0:T(8,128)(2,1)} %bitcast.7), calls=%async_computation.1 | async-start | bytes 1179648 | tf_op jit(solution)/shard_map/all_to_all | solution.py:686
  153.0 7.0 %collective-permute-start.9 = (bf16[1920,128]{1,0:T(8,128)(2,1)}, bf16[1920,128]{1,0:T(8,128)(2,1)S(1)}, u32[]{:S(2)}, u32[]{:S(2)}) collective-permute-start(bf16[1920,128]{1,0:T(8,128)(2,1)} %get-tuple-element.77), channel_id=1, source_target_pairs={{0,1},{1,0},{2,3},{3,2},{4,5},{5,4},{6,7},{7,6},{8,9},{9,8},{10,11... | collective-permute-start | bytes 1474568 | tf_op jit(solution)/shard_map/ppermute | solution.py:722
  153.0 2.4 %copy-start = (bf16[4,3,512,384]{3,2,1,0:T(8,128)(2,1)S(1)}, bf16[4,3,512,384]{3,2,1,0:T(8,128)(2,1)}, u32[]{:S(2)}) copy-start(bf16[4,3,512,384]{3,2,1,0:T(8,128)(2,1)} %get-tuple-element.75.refs_1_.refs_2_) | copy-start | bytes 14155780
  155.4 4.6 %copy-start.13 = (bf16[1920,128]{1,0:T(8,128)(2,1)S(1)}, bf16[1920,128]{1,0:T(8,128)(2,1)}, u32[]{:S(2)}) copy-start(bf16[1920,128]{1,0:T(8,128)(2,1)} %get-tuple-element.76.refs_0_) | copy-start | bytes 1474564
  155.4 14.4 %copy-start.7 = (bf16[4,192,192]{2,1,0:T(8,128)(2,1)S(1)}, bf16[4,192,192]{2,1,0:T(8,128)(2,1)}, u32[]{:S(2)}) copy-start(bf16[4,192,192]{2,1,0:T(8,128)(2,1)} %refs_3_.3) | copy-start | bytes 884740
  155.4 14.4 %copy-start.8 = (bf16[4,192,192]{2,1,0:T(8,128)(2,1)S(1)}, bf16[4,192,192]{2,1,0:T(8,128)(2,1)}, u32[]{:S(2)}) copy-start(bf16[4,192,192]{2,1,0:T(8,128)(2,1)} %refs_4_.3) | copy-start | bytes 884740
  155.4 14.4 %copy-start.9 = (bf16[4,192,192]{2,1,0:T(8,128)(2,1)S(1)}, bf16[4,192,192]{2,1,0:T(8,128)(2,1)}, u32[]{:S(2)}) copy-start(bf16[4,192,192]{2,1,0:T(8,128)(2,1)} %refs_5_.3) | copy-start | bytes 884740
  155.5 10.7 %collective-permute-start.7 = (bf16[288,128]{1,0:T(8,128)(2,1)S(1)}, bf16[288,128]{1,0:T(8,128)(2,1)S(1)}, u32[]{:S(2)}, u32[]{:S(2)}) collective-permute-start(bf16[288,128]{1,0:T(8,128)(2,1)S(1)} %add_up.9.refs_0_), channel_id=1, source_target_pairs={{0,16},{4,20},{8,24},{12,28},{16,0},{20,4},{24,8},{28,12},{1,17},{... | collective-permute-start | bytes 221192 | tf_op jit(solution)/shard_map/ppermute | solution.py:748
  158.5 9.8 %collective-permute-start.6 = (bf16[288,128]{1,0:T(8,128)(2,1)S(1)}, bf16[288,128]{1,0:T(8,128)(2,1)S(1)}, u32[]{:S(2)}, u32[]{:S(2)}) collective-permute-start(bf16[288,128]{1,0:T(8,128)(2,1)S(1)} %add_up.9.refs_0_), channel_id=1, source_target_pairs={{0,8},{4,12},{8,0},{12,4},{16,24},{20,28},{24,16},{28,20},{1,9},{5... | collective-permute-start | bytes 221192 | tf_op jit(solution)/shard_map/ppermute | solution.py:748
  160.9 24.3 %all-to-all-start.2 = ((bf16[16,120,128]{2,1,0:T(8,128)(2,1)}), bf16[16,120,128]{2,1,0:T(8,128)(2,1)S(1)}, u32[]{:S(2)}, u32[]{:S(2)}) async-start(bf16[16,120,128]{2,1,0:T(8,128)(2,1)} %bitcast.12), calls=%async_computation.2 | async-start | bytes 983040 | tf_op jit(solution)/shard_map/all_to_all | solution.py:686
  164.4 20.3 %collective-permute-start.10 = (bf16[288,128]{1,0:T(8,128)(2,1)S(1)}, bf16[288,128]{1,0:T(8,128)(2,1)S(1)}, u32[]{:S(2)}, u32[]{:S(2)}) collective-permute-start(bf16[288,128]{1,0:T(8,128)(2,1)S(1)} %add_up.9.refs_0_), channel_id=1, source_target_pairs={{0,4},{4,0},{8,12},{12,8},{16,20},{20,16},{24,28},{28,24},{1,5},{5... | collective-permute-start | bytes 221192 | tf_op jit(solution)/shard_map/ppermute | solution.py:748
  166.3 18.4 %collective-permute-start.11 = (bf16[288,128]{1,0:T(8,128)(2,1)S(1)}, bf16[288,128]{1,0:T(8,128)(2,1)S(1)}, u32[]{:S(2)}, u32[]{:S(2)}) collective-permute-start(bf16[288,128]{1,0:T(8,128)(2,1)S(1)} %collective-permute-done.7.refs_7_.refs_1_), channel_id=1, source_target_pairs={{0,4},{4,0},{8,12},{12,8},{16,20},{20,16},{24,28},{28,24},{1,5},{5... | collective-permute-start | bytes 221192 | tf_op jit(solution)/shard_map/ppermute | solution.py:748
  166.5 14.3 %collective-permute-start.8 = (bf16[288,128]{1,0:T(8,128)(2,1)S(1)}, bf16[288,128]{1,0:T(8,128)(2,1)S(1)}, u32[]{:S(2)}, u32[]{:S(2)}) collective-permute-start(bf16[288,128]{1,0:T(8,128)(2,1)S(1)} %collective-permute-done.7.refs_7_.refs_1_), channel_id=1, source_target_pairs={{0,8},{4,12},{8,0},{12,4},{16,24},{20,28},{24,16},{28,20},{1,9},{5... | collective-permute-start | bytes 221192 | tf_op jit(solution)/shard_map/ppermute | solution.py:748
  168.3 16.4 %collective-permute-start.12 = (bf16[288,128]{1,0:T(8,128)(2,1)S(1)}, bf16[288,128]{1,0:T(8,128)(2,1)S(1)}, u32[]{:S(2)}, u32[]{:S(2)}) collective-permute-start(bf16[288,128]{1,0:T(8,128)(2,1)S(1)} %collective-permute-done.6.refs_6_.refs_2_), channel_id=1, source_target_pairs={{0,4},{4,0},{8,12},{12,8},{16,20},{20,16},{24,28},{28,24},{1,5},{5... | collective-permute-start | bytes 221192 | tf_op jit(solution)/shard_map/ppermute | solution.py:748
  169.8 2.5 %copy-start.1 = (bf16[4,3,512,384]{3,2,1,0:T(8,128)(2,1)S(1)}, bf16[4,3,512,384]{3,2,1,0:T(8,128)(2,1)}, u32[]{:S(2)}) copy-start(bf16[4,3,512,384]{3,2,1,0:T(8,128)(2,1)} %get-tuple-element.75.refs_1_.refs_2_) | copy-start | bytes 14155780
  172.3 2.8 %copy-start.3 = (f32[4,512,768]{2,1,0:T(8,128)S(1)}, f32[4,512,768]{2,1,0:T(8,128)}, u32[]{:S(2)}) copy-start(f32[4,512,768]{2,1,0:T(8,128)} %get-tuple-element.58.refs_0_) | copy-start | bytes 18874372
  175.1 2.3 %copy-start.4 = (bf16[4,3,512,384]{3,2,1,0:T(8,128)(2,1)S(1)}, bf16[4,3,512,384]{3,2,1,0:T(8,128)(2,1)}, u32[]{:S(2)}) copy-start(bf16[4,3,512,384]{3,2,1,0:T(8,128)(2,1)} %get-tuple-element.72.refs_1_) | copy-start | bytes 14155780
  180.8 4.4 %collective-permute-start.13 = (bf16[288,128]{1,0:T(8,128)(2,1)S(1)}, bf16[288,128]{1,0:T(8,128)(2,1)S(1)}, u32[]{:S(2)}, u32[]{:S(2)}) collective-permute-start(bf16[288,128]{1,0:T(8,128)(2,1)S(1)} %collective-permute-done.8.refs_7_.refs_3_), channel_id=1, source_target_pairs={{0,4},{4,0},{8,12},{12,8},{16,20},{20,16},{24,28},{28,24},{1,5},{5... | collective-permute-start | bytes 221192 | tf_op jit(solution)/shard_map/ppermute | solution.py:748
  186.7 1.9 copy-start.2
  188.6 1.3 copy-start.5
  189.8 21.4 %copy-start.6 = (bf16[4608,128]{1,0:T(8,128)(2,1)S(1)}, bf16[4608,128]{1,0:T(8,128)(2,1)}, u32[]{:S(2)}) copy-start(bf16[4608,128]{1,0:T(8,128)(2,1)} %all-gather.3.cloned.1.call-done) | copy-start | bytes 3538948
  209.4 1.9 collective-permute-start.14
Sparse Core Ops, SparseCore 0:
  127.4 59.2 all-gather.2

commit v5 on v4

--- a/solution.py
+++ b/solution.py
@@ -17,6 +17,7 @@
 f32 = jnp.float32
 VMEM_LIMIT = 60 * 1024 * 1024
 SMALL_LIMIT = 30 * 1024 * 1024
+GRAD_LIMIT = 30 * 1024 * 1024
 
 OUT_BIAS, MIXED_GAIN, MIXED_BIAS, SHRINK_BIAS, FINAL_GAIN, FINAL_BIAS, QUERY_BIAS, VALUE_BIAS = range(8)
 
@@ -367,8 +368,9 @@
 
 
 def attend_back_kernel(lanes_in, per, x_ref, q_ref, k_ref, v_ref, c_ref, dc_ref, p_ref, me_ref, vec_ref, gbe_ref,
-                       prev_ref, dqkv_ref, out_ref, send_ref, gacc, gvec_ref, flat_ref):
+                       prev_ref, dqkv_ref, out_ref, send_ref, token_ref, gacc, gvec_ref, flat_ref):
     step = pl.program_id(0)
+    token_ref[...] = jnp.zeros(token_ref.shape, f32)
     groups = lanes_in // per
 
     @pl.when(step == 0)
@@ -381,7 +383,8 @@
         lanes = slice(128 * pair, 128 * pair + 128)
         q2 = q_ref[0, :, lanes] * bf16(HEAD ** -0.5)
         k2 = k_ref[0, :, lanes]
-        v2 = v_ref[0, :, lanes]
+        v_t = jnp.transpose(v_ref[0, :, lanes])
+        zeros = jnp.zeros((HEAD, v_t.shape[1]), bf16)
         dc2 = dc_ref[0, :, lanes]
         prod = dc2.astype(f32) * c_ref[0, :, lanes].astype(f32)
         q_t = jnp.transpose(q2)
@@ -392,10 +395,10 @@
             half = low if h == 0 else jnp.logical_not(low)
             rows = slice(64 * h, 64 * h + 64)
             km = jnp.where(half, k2, bf16(0))
-            vm = jnp.where(half, v2, bf16(0))
+            vm = jnp.concatenate([v_t[:HEAD], zeros] if h == 0 else [zeros, v_t[HEAD:]], axis=0)
             delta = jnp.sum(jnp.where(half, prod, 0.0), axis=-1, keepdims=True)
             pr = p_ref[0, 2 * pair + h]
-            dp = dot(dc2, vm, NT)
+            dp = dot(dc2, vm)
             ds = (pr.astype(f32) * (dp - delta)).astype(bf16)
             a = dot(ds, km)
             dq = a if dq is None else dq + a
@@ -453,6 +456,9 @@
             send_ref[...] = flat_ref[pl.ds(pl.multiple_of((1 - core) * half, 16), half)]
 
 
+TOKEN = jax.ShapeDtypeStruct((8, 128), f32)
+
+
 def unused():
     return pl.BlockSpec(memory_space=pl.ANY)
 
@@ -542,8 +548,8 @@
         lambda *refs: attend_back_kernel(lanes, per, *refs[:8], *pick(refs[:len(args)] + refs[len(args) + len(after):])),
         grid=(rows,),
         in_specs=specs + [unused()] * len(after),
-        out_specs=[pl.BlockSpec((1, 3, length, lanes), lambda r: (r, 0, 0, 0))] + [whole()] * len(outs),
-        out_shape=[dqkv] + outs,
+        out_specs=[pl.BlockSpec((1, 3, length, lanes), lambda r: (r, 0, 0, 0))] + [whole()] * (len(outs) + 1),
+        out_shape=[dqkv] + outs + [TOKEN],
         scratch_shapes=[
             pltpu.VMEM((3, lanes // per, per, 256), f32),
             pltpu.VMEM((8, lanes), f32),
@@ -555,7 +561,8 @@
     )(*args, *after)
 
 
-def input_grad_kernel(dh1_ref, d0_ref, d1_ref, wq_ref, wk_ref, wv_ref, dx_ref, wpad):
+def input_grad_kernel(dh1_ref, d0_ref, d1_ref, wq_ref, wk_ref, wv_ref, dx_ref, token_ref, wpad):
+    token_ref[...] = jnp.zeros(token_ref.shape, f32)
     groups, per = wq_ref.shape[0], wq_ref.shape[1]
 
     @pl.when(pl.program_id(0) == 0)
@@ -596,11 +603,11 @@
         lambda *refs: input_grad_kernel(*refs[:len(args)], *refs[len(args) + len(extra):]),
         grid=(count,),
         in_specs=[wide, back, back] + [full(wq.shape)] * 3 + [unused()] * len(extra),
-        out_specs=wide,
-        out_shape=jax.ShapeDtypeStruct((rows, length, width), bf16),
+        out_specs=[wide, whole()],
+        out_shape=[jax.ShapeDtypeStruct((rows, length, width), bf16), TOKEN],
         input_output_aliases=aliases,
         scratch_shapes=[pltpu.VMEM((3, wq.shape[0], 256, 256), bf16)],
-        compiler_params=pltpu.CompilerParams(vmem_limit_bytes=SMALL_LIMIT),
+        compiler_params=pltpu.CompilerParams(vmem_limit_bytes=GRAD_LIMIT),
         cost_estimate=pl.CostEstimate(flops=int(5e9), bytes_accessed=int(1e7), transcendentals=0),
         name="input_grad",
     )(*args, *extra)
@@ -735,13 +742,13 @@
     got_w = exchange(sum_w.reshape(2 * dp, -1, 128), everyone, like)
     far_got = swap(far, 2)
     back = functools.partial(attend_back, x, q, k, v, c, dc, p, me=me, per=per)
-    d0, flat0 = back(part=0, vec=gvec, gbe=gbe, after=(far, sum_w))
-    piece_w = total(got_w, after=(flat0,))
+    d0, flat0, done_0 = back(part=0, vec=gvec, gbe=gbe, after=(far, sum_w))
+    piece_w = total(got_w, after=(done_0,))
     sum_e = add((near_e, core_e, far_got), (None, 0, None), after=(piece_w,))
     got_e = exchange(sum_e.reshape(dp, -1, 128), "dp")
     all_w = lax.all_gather(piece_w, everyone)
-    d1, keep_q, send_q = back(part=1, prev=flat0, devices=count, after=(sum_e, piece_w))
-    piece_e = total(got_e, after=(d1,))
+    d1, keep_q, send_q, done_1 = back(part=1, prev=flat0, devices=count, after=(sum_e, piece_w))
+    piece_e = total(got_e, after=(done_1,))
     order, pieces = [0], [piece_e]
     bit = dp // 2
     while bit:
@@ -751,9 +758,9 @@
     sum_q = add((keep_q, swap(send_q, 1)))
     got_q = exchange(sum_q.reshape(2 * dp, -1, 128), everyone, like)
     back_weights = (query_weight, key_weight, value_weight)
-    dx = input_grad(dh1, d0, d1, *back_weights, half=0, after=(sum_q, pieces[1]))
-    dx = input_grad(dh1, d0, d1, *back_weights, half=1, prev=dx, after=pieces[2:4])
-    piece_q = total(got_q, after=(dx, all_w, *pieces[4:]), copies=2 * dp)
+    dx, _ = input_grad(dh1, d0, d1, *back_weights, half=0, after=(sum_q, pieces[1]))
+    dx, done_2 = input_grad(dh1, d0, d1, *back_weights, half=1, prev=dx, after=pieces[2:4])
+    piece_q = total(got_q, after=(done_2, all_w[0, :8], *pieces[4:]), copies=2 * dp)
     own_q = exchange(piece_q, everyone, like).reshape(-1, 128)
     other_q = swap(own_q, 1)
     place = jnp.stack([lax.axis_index("ffn"), lax.axis_index("dp")]).astype(jnp.int32)

time: 223 us -> 221 us (level)
  local copies, waits for them, and re-layouts: 18.1 us -> 15.8 us
    unnamed x40 -> x36, local copies, waits for them, and re-layouts: 17.4 us -> 14.5 us
  transfers between devices with their start and end apart: 19 -> 19, of which waited for: 5 -> 4; matrix products, arithmetic and copies ran while one was open for 0% -> 0% of each run, Pallas kernels for 34% -> 34%
where the time goes in v5:
time: 221 us; the launch traced here: 220 us
  Pallas kernels  127 us (57%)
  starting transfers between devices  32.6 us (15%)
  blocking collectives  19.3 us (9%)
  local copies, waits for them, and re-layouts  15.8 us (7%)
  between operations  14.3 us (6%)
  waiting for transfers between devices  8.97 us (4%)
    pallas_call x1, Pallas kernels, feed(): pl.pallas_call(feed_kernel, grid=(rows,), in_specs=[pl.BlockSpec(memory_s...  48.6 us
    pallas_call x2, Pallas kernels, attend_back(): pl.pallas_call(lambda *refs: attend_back_kernel(lanes, per, *refs[:8], *p...  37.1 us
    pallas_call x1, Pallas kernels, attend(): pl.pallas_call(attend_kernel, grid=(rows,), in_specs=[wide, row_spec((1,...  27 us
    all_to_all x1, blocking collectives, exchange(): return lax.all_to_all(x, axes, 0, 0, axis_index_groups=groups, tiled=True)  19.3 us
    all_to_all x3, starting transfers between devices, exchange(): return lax.all_to_all(x, axes, 0, 0, axis_index_groups=groups, tiled=True)  16.7 us
    unnamed x36, local copies, waits for them, and re-layouts  14.5 us
    ppermute x7, starting transfers between devices, on_device(): lax.ppermute(t, 'dp', [(d, d ^ bit) for d in range(dp)])  10.1 us
    pallas_call x2, Pallas kernels, input_grad(): pl.pallas_call(lambda *refs: input_grad_kernel(*refs[:len(args)], *refs[l...  6.84 us
  transfers between devices with their start and end apart: 19, of which 4 were waited for; matrix products, arithmetic and copies ran while one was open for 0% of the time, Pallas kernels for 34%

profile of v5, /device:TPU:0, one launch (start us, length us, event | category | flops | bytes accessed | tf_op | source)
XLA Modules:
  0.0 219.7 jit_solution(17038298164081959619)
XLA Ops:
  7.2 0.7 copy.38
  7.9 1.3 fusion.1.w0_ref
  9.2 2.5 %collective-permute-start.2 = (bf16[4,208,384]{2,1,0:T(8,128)(2,1)S(1)}, bf16[4,208,384]{2,1,0:T(8,128)(2,1)S(1)}, u32[]{:S(2)}, u32[]{:S(2)}) collective-permute-start(bf16[4,208,384]{2,1,0:T(8,128)(2,1)S(1)} %fusion.1.w0_ref), channel_id=1, source_target_pairs={{0,3},{1,2},{2,1},{3,0},{4,7},{5,6},{6,5},{7,4},{8,11},{9,10},{10,... | collective-permute-start | bytes 1916936 | tf_op jit(solution)/shard_map/ppermute | solution.py:729
  11.7 0.6 collective-permute-start.1
  12.3 0.0 collective-permute-start
  12.4 27.0 %attend.1 = (bf16[4,512,768]{2,1,0:T(8,128)(2,1)}, bf16[4,512,768]{2,1,0:T(8,128)(2,1)}, bf16[4,512,768]{2,1,0:T(8,128)(2,1)}, bf16[4,512,768]{2,1,0:T(8,128)(2,...) custom-call(bf16[4,512,768]{2,1,0:T(8,128)(2,1)} %bitcast.25, s32[4,1,512]{2,1,0:T(1,128)} %docs_ref.1, ...), custom_call_target="tpu_custom_call" | custom-call | flops 20000000000 | bytes 50000000 | tf_op jit(solution)/shard_map/attend/pallas_call | solution.py:138
  39.4 0.0 collective-permute-done.2.w3_ref
  39.4 0.0 copy-start.15
  39.4 0.9 collective-permute-done.1.w2_ref
  40.3 0.8 copy-done.16
  41.2 0.2 copy-done.17
  41.4 48.6 %feed.1 = (bf16[4,512,768]{2,1,0:T(8,128)(2,1)}, f32[4,512,768]{2,1,0:T(8,128)}, bf16[4,512,768]{2,1,0:T(8,128)(2,1)}, bf16[2304,128]{1,0:T(8,128)(2,1)}, bf16[2...) custom-call(s32[1]{0:T(128)} %bitcast.me_ref.refs_7_, ...), custom_call_target="tpu_custom_call" | custom-call | flops 40000000000 | bytes 50000000 | tf_op jit(solution)/shard_map/feed/pallas_call | solution.py:342
  90.0 0.1 collective-permute-start.4
  90.1 0.5 collective-permute-start.3
  90.6 3.4 %collective-permute-done.3.cw_ref = bf16[2304,128]{1,0:T(8,128)(2,1)S(1)} collective-permute-done((bf16[2304,128]{1,0:T(8,128)(2,1)}, bf16[2304,128]{1,0:T(8,128)(2,1)S(1)}, u32[]{:S(2)}, u32[]{:S(2)}) %collective-permute-start.3) | collective-permute-done | bytes 589856 | tf_op jit(solution)/shard_map/ppermute | solution.py:729
  94.0 1.1 copy-done.5
  95.0 1.1 copy-done.6
  96.1 1.0 add_up.6
  97.1 7.6 %all-to-all-start = ((bf16[16,144,128]{2,1,0:T(8,128)(2,1)}), bf16[16,144,128]{2,1,0:T(8,128)(2,1)S(1)}, u32[]{:S(2)}, u32[]{:S(2)}) async-start(bf16[16,144,128]{2,1,0:T(8,128)(2,1)} %bitcast.6), calls=%async_computation | async-start | bytes 1179648 | tf_op jit(solution)/shard_map/all_to_all | solution.py:693
  104.7 0.0 all-gather.3.cloned.1.call-start
  104.8 2.0 collective-permute-start.5
  106.8 18.3 %attend_back.2 = (bf16[4,3,512,384]{3,2,1,0:T(8,128)(2,1)}, bf16[1872,128]{1,0:T(8,128)(2,1)}, f32[8,128]{1,0:T(8,128)}) custom-call(bf16[4,512,768]{2,1,0:T(8,128)(2,1)} %bitcast.27, bf16[4,512,768]{2,1,0:T(8,128)(2,1)} %get-tuple-element.64.refs_1_, bf16[4,512,768]{2,1,0:T(8,128)(2,1)} %get-tuple-element.65.refs_2_, ...), custom_call_target="tpu_custom_call" | custom-call | flops 20000000000 | bytes 30000000 | tf_op jit(solution)/shard_map/attend_back/pallas_call | solution.py:547
  125.1 0.0 all-to-all-done.refs_0_
  125.1 0.0 copy-start.12
  125.1 0.7 copy-done.12
  125.8 0.7 add_up.7.refs_3_.refs_10_
  126.5 0.0 all-gather.3.cloned.1.call-update
  126.5 0.0 collective-permute-done.5.refs_2_
  126.6 1.0 add_up.8.refs_9_
  127.6 5.4 %all-to-all-start.1 = ((bf16[8,288,128]{2,1,0:T(8,128)(2,1)}), bf16[8,288,128]{2,1,0:T(8,128)(2,1)S(1)}, u32[]{:S(2)}, u32[]{:S(2)}) async-start(bf16[8,288,128]{2,1,0:T(8,128)(2,1)} %bitcast.7), calls=%async_computation.1 | async-start | bytes 1179648 | tf_op jit(solution)/shard_map/all_to_all | solution.py:693
  133.0 0.0 copy-start.9
  133.0 0.0 copy-start.10
  133.1 18.8 %attend_back.3 = (bf16[4,3,512,384]{3,2,1,0:T(8,128)(2,1)}, bf16[1920,128]{1,0:T(8,128)(2,1)}, bf16[1920,128]{1,0:T(8,128)(2,1)}, f32[8,128]{1,0:T(8,128)}) custom-call(bf16[4,512,768]{2,1,0:T(8,128)(2,1)} %bitcast.28, bf16[4,512,768]{2,1,0:T(8,128)(2,1)} %get-tuple-element.64.refs_1_, bf16[4,512,768]{2,1,0:T(8,128)(2,1)} %get-tuple-element.65.refs_2_, ...), custom_call_target="tpu_custom_call" | custom-call | flops 20000000000 | bytes 30000000 | tf_op jit(solution)/shard_map/attend_back/pallas_call | solution.py:547
  151.9 0.1 collective-permute-start.9
  151.9 0.0 all-to-all-done.1.refs_0_
  152.0 0.0 copy-start.11
  152.0 0.7 copy-done.11
  152.7 0.1 add_up.9.refs_0_
  152.7 3.0 %collective-permute-start.7 = (bf16[288,128]{1,0:T(8,128)(2,1)S(1)}, bf16[288,128]{1,0:T(8,128)(2,1)S(1)}, u32[]{:S(2)}, u32[]{:S(2)}) collective-permute-start(bf16[288,128]{1,0:T(8,128)(2,1)S(1)} %add_up.9.refs_0_), channel_id=1, source_target_pairs={{0,16},{4,20},{8,24},{12,28},{16,0},{20,4},{24,8},{28,12},{1,17},{... | collective-permute-start | bytes 221192 | tf_op jit(solution)/shard_map/ppermute | solution.py:755
  155.7 1.5 collective-permute-start.6
  157.2 0.0 collective-permute-done.9.refs_1_
  157.2 1.0 copy-done.7
  158.2 0.9 add_up.10.refs_6_
  159.1 3.6 %all-to-all-start.2 = ((bf16[16,120,128]{2,1,0:T(8,128)(2,1)}), bf16[16,120,128]{2,1,0:T(8,128)(2,1)S(1)}, u32[]{:S(2)}, u32[]{:S(2)}) async-start(bf16[16,120,128]{2,1,0:T(8,128)(2,1)} %bitcast.12), calls=%async_computation.2 | async-start | bytes 983040 | tf_op jit(solution)/shard_map/all_to_all | solution.py:693
  162.7 1.8 collective-permute-start.10
  164.5 0.0 collective-permute-done.7.refs_7_.refs_1_
  164.5 0.3 collective-permute-start.11
  164.8 1.8 collective-permute-start.8
  166.5 0.0 collective-permute-done.6.refs_6_.refs_2_
  166.5 1.5 collective-permute-start.12
  168.0 2.9 %copy-done = f32[4,512,768]{2,1,0:T(8,128)S(1)} copy-done((f32[4,512,768]{2,1,0:T(8,128)S(1)}, f32[4,512,768]{2,1,0:T(8,128)}, u32[]{:S(2)}) %copy-start) | copy-done | bytes 6291480
  171.0 2.3 %copy-done.1 = bf16[4,3,512,384]{3,2,1,0:T(8,128)(2,1)S(1)} copy-done((bf16[4,3,512,384]{3,2,1,0:T(8,128)(2,1)S(1)}, bf16[4,3,512,384]{3,2,1,0:T(8,128)(2,1)}, u32[]{:S(2)}) %copy-start.1) | copy-done | bytes 4718616
  173.3 2.3 %copy-done.2 = bf16[4,3,512,384]{3,2,1,0:T(8,128)(2,1)S(1)} copy-done((bf16[4,3,512,384]{3,2,1,0:T(8,128)(2,1)S(1)}, bf16[4,3,512,384]{3,2,1,0:T(8,128)(2,1)}, u32[]{:S(2)}) %copy-start.2) | copy-done | bytes 4718616
  175.7 3.4 %input_grad.2 = (bf16[4,512,768]{2,1,0:T(8,128)(2,1)}, f32[8,128]{1,0:T(8,128)}) custom-call(f32[4,512,768]{2,1,0:T(8,128)S(1)} %copy-done, bf16[4,3,512,384]{3,2,1,0:T(8,128)(2,1)S(1)} %copy-done.1, bf16[4,3,512,384]{3,2,1,0:T(8,128)(2,1)S(1)} %copy-done.2, bf16[4,192,192]{2,1,0:T(8,128)(2,1)S(1)} %copy-done.8, bf16[4,192,192]{2,1,0:T(8,128)(2,1)S(1)} %copy-done.9, ...), custom_call_target="tpu_custom_call" | custom-call | flops 5000000000 | bytes 10000000 | tf_op jit(solution)/shard_map/input_grad/pallas_call | solution.py:602
  179.1 0.4 collective-permute-start.13
  179.5 3.4 %input_grad.3 = (bf16[4,512,768]{2,1,0:T(8,128)(2,1)}, f32[8,128]{1,0:T(8,128)S(1)}) custom-call(f32[4,512,768]{2,1,0:T(8,128)S(1)} %copy-done, bf16[4,3,512,384]{3,2,1,0:T(8,128)(2,1)S(1)} %copy-done.1, bf16[4,3,512,384]{3,2,1,0:T(8,128)(2,1)S(1)} %copy-done.2, bf16[4,192,192]{2,1,0:T(8,128)(2,1)S(1)} %copy-done.8, ...), custom_call_target="tpu_custom_call", output_to_operand_aliasing={{0}: (8, {})} | custom-call | flops 5000000000 | bytes 10000000 | tf_op jit(solution)/shard_map/input_grad/pallas_call | solution.py:602
  182.9 2.8 %all-gather.3.cloned.1.call-done = bf16[4608,128]{1,0:T(8,128)(2,1)} async-done(((bf16[144,128]{1,0:T(8,128)(2,1)}), bf16[4608,128]{1,0:T(8,128)(2,1)}) %all-gather.3.cloned.1.call-update) | async-done | bytes 1179664 | tf_op jit(solution)/shard_map/all_gather | solution.py:749
  185.7 0.7 slice_bitcast_fusion.refs_2_
  186.4 0.1 add_up.11
  186.5 19.3 %all_to_all.20 = bf16[16,120,128]{2,1,0:T(8,128)(2,1)S(1)} all-to-all(bf16[16,120,128]{2,1,0:T(8,128)(2,1)S(1)} %add_up.11), channel_id=1, replica_groups={{0,2,4,6,8,10,12,14,16,18,20,22,24,26,28,30},{1,3,5,7,9,11,13,15,17,19,..., dimensions={0} | all-to-all | bytes 983040 | tf_op jit(solution)/shard_map/all_to_all | solution.py:693
  205.8 0.1 pad_add_fusion.me_ref
  205.8 1.8 collective-permute-done.14.refs_10_
  207.6 1.3 copy-done.3
  208.9 4.0 %unpack.1 = (f32[4,192,192]{2,1,0:T(8,128)}, f32[4,192,192]{2,1,0:T(8,128)}, f32[768,768]{1,0:T(8,128)}, f32[4,192,192]{2,1,0:T(8,128)}, f32[4,192,192]{2,1,0:T(...) custom-call(s32[2]{0:T(128)S(1)} %pad_add_fusion.me_ref, ...), custom_call_target="tpu_custom_call" | custom-call | tf_op jit(solution)/shard_map/unpack/pallas_call | solution.py:679
  (29 shorter events, 0.1 us)
Async XLA Ops:
  9.2 30.1 %copy-start.14 = (bf16[4,208,384]{2,1,0:T(8,128)(2,1)}, bf16[4,208,384]{2,1,0:T(8,128)(2,1)S(1)}, u32[]{:S(2)}) copy-start(bf16[4,208,384]{2,1,0:T(8,128)(2,1)S(1)} %fusion.1.w0_ref) | copy-start | bytes 1916932
  9.2 30.2 %collective-permute-start.2 = (bf16[4,208,384]{2,1,0:T(8,128)(2,1)S(1)}, bf16[4,208,384]{2,1,0:T(8,128)(2,1)S(1)}, u32[]{:S(2)}, u32[]{:S(2)}) collective-permute-start(bf16[4,208,384]{2,1,0:T(8,128)(2,1)S(1)} %fusion.1.w0_ref), channel_id=1, source_target_pairs={{0,3},{1,2},{2,1},{3,0},{4,7},{5,6},{6,5},{7,4},{8,11},{9,10},{10,... | collective-permute-start | bytes 1916936 | tf_op jit(solution)/shard_map/ppermute | solution.py:729
  11.7 28.6 %collective-permute-start.1 = (bf16[4,208,384]{2,1,0:T(8,128)(2,1)S(1)}, bf16[4,208,384]{2,1,0:T(8,128)(2,1)S(1)}, u32[]{:S(2)}, u32[]{:S(2)}) collective-permute-start(bf16[4,208,384]{2,1,0:T(8,128)(2,1)S(1)} %fusion.1.w0_ref), channel_id=1, source_target_pairs={{0,2},{1,3},{2,0},{3,1},{4,6},{5,7},{6,4},{7,5},{8,10},{9,11},{10,... | collective-permute-start | bytes 1916936 | tf_op jit(solution)/shard_map/ppermute | solution.py:729
  12.3 28.0 %collective-permute-start = (bf16[4,208,384]{2,1,0:T(8,128)(2,1)S(1)}, bf16[4,208,384]{2,1,0:T(8,128)(2,1)S(1)}, u32[]{:S(2)}, u32[]{:S(2)}) collective-permute-start(bf16[4,208,384]{2,1,0:T(8,128)(2,1)S(1)} %fusion.1.w0_ref), channel_id=1, source_target_pairs={{0,1},{1,0},{2,3},{3,2},{4,5},{5,4},{6,7},{7,6},{8,9},{9,8},{10,11... | collective-permute-start | bytes 1916936 | tf_op jit(solution)/shard_map/ppermute | solution.py:729
  39.4 0.9 copy-start.15
  40.3 0.8 copy-start.16
  40.3 1.0 copy-start.17
  90.0 4.0 %collective-permute-start.4 = (bf16[4608,128]{1,0:T(8,128)(2,1)}, bf16[4608,128]{1,0:T(8,128)(2,1)S(1)}, u32[]{:S(2)}, u32[]{:S(2)}) collective-permute-start(bf16[4608,128]{1,0:T(8,128)(2,1)} %get-tuple-element.74), channel_id=1, source_target_pairs={{0,1},{1,0},{2,3},{3,2},{4,5},{5,4},{6,7},{7,6},{8,9},{9,8},{10,11... | collective-permute-start | bytes 3538952 | tf_op jit(solution)/shard_map/ppermute | solution.py:729
  90.1 3.9 %collective-permute-start.3 = (bf16[2304,128]{1,0:T(8,128)(2,1)}, bf16[2304,128]{1,0:T(8,128)(2,1)S(1)}, u32[]{:S(2)}, u32[]{:S(2)}) collective-permute-start(bf16[2304,128]{1,0:T(8,128)(2,1)} %get-tuple-element.72), channel_id=1, source_target_pairs={{0,1},{1,0},{2,3},{3,2},{4,5},{5,4},{6,7},{7,6},{8,9},{9,8},{10,11... | collective-permute-start | bytes 1769480 | tf_op jit(solution)/shard_map/ppermute | solution.py:729
  94.0 1.1 copy-start.5
  95.0 1.1 copy-start.6
  97.1 9.7 %copy-start.13 = (bf16[2304,128]{1,0:T(8,128)(2,1)}, bf16[2304,128]{1,0:T(8,128)(2,1)S(1)}, u32[]{:S(2)}) copy-start(bf16[2304,128]{1,0:T(8,128)(2,1)S(1)} %get-tuple-element.75.refs_10_) | copy-start | bytes 1769476
  97.1 28.0 %all-to-all-start = ((bf16[16,144,128]{2,1,0:T(8,128)(2,1)}), bf16[16,144,128]{2,1,0:T(8,128)(2,1)S(1)}, u32[]{:S(2)}, u32[]{:S(2)}) async-start(bf16[16,144,128]{2,1,0:T(8,128)(2,1)} %bitcast.6), calls=%async_computation | async-start | bytes 1179648 | tf_op jit(solution)/shard_map/all_to_all | solution.py:693
  104.7 80.9 %all-gather.3.cloned.1.call-start = ((), (), s32[]{:S(2)}) async-start(), calls=%async_computation.4 | async-start | bytes 1216512 | tf_op jit(solution)/shard_map/all_gather | solution.py:749
  104.8 21.7 %collective-permute-start.5 = (bf16[2304,128]{1,0:T(8,128)(2,1)S(1)}, bf16[2304,128]{1,0:T(8,128)(2,1)S(1)}, u32[]{:S(2)}, u32[]{:S(2)}) collective-permute-start(bf16[2304,128]{1,0:T(8,128)(2,1)S(1)} %get-tuple-element.75.refs_10_), channel_id=1, source_target_pairs={{0,2},{1,3},{2,0},{3,1},{4,6},{5,7},{6,4},{7,5},{8,10},{9,11},{10,... | collective-permute-start | bytes 1769480 | tf_op jit(solution)/shard_map/ppermute | solution.py:729
  106.8 19.8 %copy-start.4 = (bf16[2304,128]{1,0:T(8,128)(2,1)S(1)}, bf16[2304,128]{1,0:T(8,128)(2,1)}, u32[]{:S(2)}) copy-start(bf16[2304,128]{1,0:T(8,128)(2,1)} %get-tuple-element.79.refs_0_) | copy-start | bytes 1769476
  125.1 0.7 copy-start.12
  127.6 24.4 %all-to-all-start.1 = ((bf16[8,288,128]{2,1,0:T(8,128)(2,1)}), bf16[8,288,128]{2,1,0:T(8,128)(2,1)S(1)}, u32[]{:S(2)}, u32[]{:S(2)}) async-start(bf16[8,288,128]{2,1,0:T(8,128)(2,1)} %bitcast.7), calls=%async_computation.1 | async-start | bytes 1179648 | tf_op jit(solution)/shard_map/all_to_all | solution.py:693
  133.0 35.0 %copy-start.8 = (bf16[4,192,192]{2,1,0:T(8,128)(2,1)S(1)}, bf16[4,192,192]{2,1,0:T(8,128)(2,1)}, u32[]{:S(2)}) copy-start(bf16[4,192,192]{2,1,0:T(8,128)(2,1)} %refs_3_.3) | copy-start | bytes 884740
  133.0 35.0 %copy-start.9 = (bf16[4,192,192]{2,1,0:T(8,128)(2,1)S(1)}, bf16[4,192,192]{2,1,0:T(8,128)(2,1)}, u32[]{:S(2)}) copy-start(bf16[4,192,192]{2,1,0:T(8,128)(2,1)} %refs_4_.3) | copy-start | bytes 884740
  133.0 35.0 %copy-start.10 = (bf16[4,192,192]{2,1,0:T(8,128)(2,1)S(1)}, bf16[4,192,192]{2,1,0:T(8,128)(2,1)}, u32[]{:S(2)}) copy-start(bf16[4,192,192]{2,1,0:T(8,128)(2,1)} %refs_5_.3) | copy-start | bytes 884740
  151.9 5.3 %collective-permute-start.9 = (bf16[1920,128]{1,0:T(8,128)(2,1)}, bf16[1920,128]{1,0:T(8,128)(2,1)S(1)}, u32[]{:S(2)}, u32[]{:S(2)}) collective-permute-start(bf16[1920,128]{1,0:T(8,128)(2,1)} %get-tuple-element.84), channel_id=1, source_target_pairs={{0,1},{1,0},{2,3},{3,2},{4,5},{5,4},{6,7},{7,6},{8,9},{9,8},{10,11... | collective-permute-start | bytes 1474568 | tf_op jit(solution)/shard_map/ppermute | solution.py:729
  152.0 0.7 copy-start.11
  152.7 11.8 %collective-permute-start.7 = (bf16[288,128]{1,0:T(8,128)(2,1)S(1)}, bf16[288,128]{1,0:T(8,128)(2,1)S(1)}, u32[]{:S(2)}, u32[]{:S(2)}) collective-permute-start(bf16[288,128]{1,0:T(8,128)(2,1)S(1)} %add_up.9.refs_0_), channel_id=1, source_target_pairs={{0,16},{4,20},{8,24},{12,28},{16,0},{20,4},{24,8},{28,12},{1,17},{... | collective-permute-start | bytes 221192 | tf_op jit(solution)/shard_map/ppermute | solution.py:755
  155.7 10.8 %collective-permute-start.6 = (bf16[288,128]{1,0:T(8,128)(2,1)S(1)}, bf16[288,128]{1,0:T(8,128)(2,1)S(1)}, u32[]{:S(2)}, u32[]{:S(2)}) collective-permute-start(bf16[288,128]{1,0:T(8,128)(2,1)S(1)} %add_up.9.refs_0_), channel_id=1, source_target_pairs={{0,8},{4,12},{8,0},{12,4},{16,24},{20,28},{24,16},{28,20},{1,9},{5... | collective-permute-start | bytes 221192 | tf_op jit(solution)/shard_map/ppermute | solution.py:755
  157.2 1.0 copy-start.7
  159.1 27.3 %all-to-all-start.2 = ((bf16[16,120,128]{2,1,0:T(8,128)(2,1)}), bf16[16,120,128]{2,1,0:T(8,128)(2,1)S(1)}, u32[]{:S(2)}, u32[]{:S(2)}) async-start(bf16[16,120,128]{2,1,0:T(8,128)(2,1)} %bitcast.12), calls=%async_computation.2 | async-start | bytes 983040 | tf_op jit(solution)/shard_map/all_to_all | solution.py:693
  162.7 23.7 %collective-permute-start.10 = (bf16[288,128]{1,0:T(8,128)(2,1)S(1)}, bf16[288,128]{1,0:T(8,128)(2,1)S(1)}, u32[]{:S(2)}, u32[]{:S(2)}) collective-permute-start(bf16[288,128]{1,0:T(8,128)(2,1)S(1)} %add_up.9.refs_0_), channel_id=1, source_target_pairs={{0,4},{4,0},{8,12},{12,8},{16,20},{20,16},{24,28},{28,24},{1,5},{5... | collective-permute-start | bytes 221192 | tf_op jit(solution)/shard_map/ppermute | solution.py:755
  164.5 21.9 %collective-permute-start.11 = (bf16[288,128]{1,0:T(8,128)(2,1)S(1)}, bf16[288,128]{1,0:T(8,128)(2,1)S(1)}, u32[]{:S(2)}, u32[]{:S(2)}) collective-permute-start(bf16[288,128]{1,0:T(8,128)(2,1)S(1)} %collective-permute-done.7.refs_7_.refs_1_), channel_id=1, source_target_pairs={{0,4},{4,0},{8,12},{12,8},{16,20},{20,16},{24,28},{28,24},{1,5},{5... | collective-permute-start | bytes 221192 | tf_op jit(solution)/shard_map/ppermute | solution.py:755
  164.8 14.3 %collective-permute-start.8 = (bf16[288,128]{1,0:T(8,128)(2,1)S(1)}, bf16[288,128]{1,0:T(8,128)(2,1)S(1)}, u32[]{:S(2)}, u32[]{:S(2)}) collective-permute-start(bf16[288,128]{1,0:T(8,128)(2,1)S(1)} %collective-permute-done.7.refs_7_.refs_1_), channel_id=1, source_target_pairs={{0,8},{4,12},{8,0},{12,4},{16,24},{20,28},{24,16},{28,20},{1,9},{5... | collective-permute-start | bytes 221192 | tf_op jit(solution)/shard_map/ppermute | solution.py:755
  166.5 19.8 %collective-permute-start.12 = (bf16[288,128]{1,0:T(8,128)(2,1)S(1)}, bf16[288,128]{1,0:T(8,128)(2,1)S(1)}, u32[]{:S(2)}, u32[]{:S(2)}) collective-permute-start(bf16[288,128]{1,0:T(8,128)(2,1)S(1)} %collective-permute-done.6.refs_6_.refs_2_), channel_id=1, source_target_pairs={{0,4},{4,0},{8,12},{12,8},{16,20},{20,16},{24,28},{28,24},{1,5},{5... | collective-permute-start | bytes 221192 | tf_op jit(solution)/shard_map/ppermute | solution.py:755
  168.0 2.9 %copy-start = (f32[4,512,768]{2,1,0:T(8,128)S(1)}, f32[4,512,768]{2,1,0:T(8,128)}, u32[]{:S(2)}) copy-start(f32[4,512,768]{2,1,0:T(8,128)} %get-tuple-element.63.refs_0_) | copy-start | bytes 18874372
  171.0 2.3 %copy-start.1 = (bf16[4,3,512,384]{3,2,1,0:T(8,128)(2,1)S(1)}, bf16[4,3,512,384]{3,2,1,0:T(8,128)(2,1)}, u32[]{:S(2)}) copy-start(bf16[4,3,512,384]{3,2,1,0:T(8,128)(2,1)} %get-tuple-element.77.refs_1_) | copy-start | bytes 14155780
  173.3 2.3 %copy-start.2 = (bf16[4,3,512,384]{3,2,1,0:T(8,128)(2,1)S(1)}, bf16[4,3,512,384]{3,2,1,0:T(8,128)(2,1)}, u32[]{:S(2)}) copy-start(bf16[4,3,512,384]{3,2,1,0:T(8,128)(2,1)} %get-tuple-element.81.refs_2_) | copy-start | bytes 14155780
  179.1 7.3 %collective-permute-start.13 = (bf16[288,128]{1,0:T(8,128)(2,1)S(1)}, bf16[288,128]{1,0:T(8,128)(2,1)S(1)}, u32[]{:S(2)}, u32[]{:S(2)}) collective-permute-start(bf16[288,128]{1,0:T(8,128)(2,1)S(1)} %collective-permute-done.8.refs_7_.refs_3_), channel_id=1, source_target_pairs={{0,4},{4,0},{8,12},{12,8},{16,20},{20,16},{24,28},{28,24},{1,5},{5... | collective-permute-start | bytes 221192 | tf_op jit(solution)/shard_map/ppermute | solution.py:755
  205.8 1.9 collective-permute-start.14
  207.6 1.3 copy-start.3
Sparse Core Ops, SparseCore 0:
  126.7 58.9 all-gather.2

commit v6 on v5

--- a/solution.py
+++ b/solution.py
@@ -748,14 +748,14 @@
     got_e = exchange(sum_e.reshape(dp, -1, 128), "dp")
     all_w = lax.all_gather(piece_w, everyone)
     d1, keep_q, send_q, done_1 = back(part=1, prev=flat0, devices=count, after=(sum_e, piece_w))
-    piece_e = total(got_e, after=(done_1,))
+    sum_q = add((keep_q, swap(send_q, 1)))
+    piece_e = total(got_e, after=(done_1, sum_q))
     order, pieces = [0], [piece_e]
     bit = dp // 2
     while bit:
         pieces = pieces + [lax.ppermute(t, "dp", [(d, d ^ bit) for d in range(dp)]) for t in pieces]
         order = order + [n ^ bit for n in order]
         bit //= 2
-    sum_q = add((keep_q, swap(send_q, 1)))
     got_q = exchange(sum_q.reshape(2 * dp, -1, 128), everyone, like)
     back_weights = (query_weight, key_weight, value_weight)
     dx, _ = input_grad(dh1, d0, d1, *back_weights, half=0, after=(sum_q, pieces[1]))

time: 221 us -> 221 us (level)
  transfers between devices with their start and end apart: 19 -> 19, of which waited for: 4 -> 5; matrix products, arithmetic and copies ran while one was open for 0% -> 0% of each run, Pallas kernels for 34% -> 33%
where the time goes in v6:
time: 221 us; the launch traced here: 220 us
  Pallas kernels  127 us (57%)
  starting transfers between devices  32.9 us (15%)
  blocking collectives  19.4 us (9%)
  local copies, waits for them, and re-layouts  15.7 us (7%)
  between operations  14.3 us (6%)
  waiting for transfers between devices  8.91 us (4%)
    pallas_call x1, Pallas kernels, feed(): pl.pallas_call(feed_kernel, grid=(rows,), in_specs=[pl.BlockSpec(memory_s...  48.6 us
    pallas_call x2, Pallas kernels, attend_back(): pl.pallas_call(lambda *refs: attend_back_kernel(lanes, per, *refs[:8], *p...  37.1 us
    pallas_call x1, Pallas kernels, attend(): pl.pallas_call(attend_kernel, grid=(rows,), in_specs=[wide, row_spec((1,...  27 us
    all_to_all x1, blocking collectives, exchange(): return lax.all_to_all(x, axes, 0, 0, axis_index_groups=groups, tiled=True)  19.4 us
    all_to_all x3, starting transfers between devices, exchange(): return lax.all_to_all(x, axes, 0, 0, axis_index_groups=groups, tiled=True)  16.7 us
    unnamed x36, local copies, waits for them, and re-layouts  14.3 us
    ppermute x7, starting transfers between devices, on_device(): lax.ppermute(t, 'dp', [(d, d ^ bit) for d in range(dp)])  10.5 us
    ppermute x8, waiting for transfers between devices, swap(): return lax.ppermute(array, 'ffn', [(f, f ^ bit) for f in range(4)])  8.18 us
  transfers between devices with their start and end apart: 19, of which 5 were waited for; matrix products, arithmetic and copies ran while one was open for 0% of the time, Pallas kernels for 33%

profile of v6, /device:TPU:0, one launch (start us, length us, event | category | flops | bytes accessed | tf_op | source)
XLA Modules:
  0.0 219.9 jit_solution(11926184919798090787)
XLA Ops:
  7.2 0.7 copy.38
  7.9 1.3 fusion.1.w0_ref
  9.2 2.5 %collective-permute-start.2 = (bf16[4,208,384]{2,1,0:T(8,128)(2,1)S(1)}, bf16[4,208,384]{2,1,0:T(8,128)(2,1)S(1)}, u32[]{:S(2)}, u32[]{:S(2)}) collective-permute-start(bf16[4,208,384]{2,1,0:T(8,128)(2,1)S(1)} %fusion.1.w0_ref), channel_id=1, source_target_pairs={{0,3},{1,2},{2,1},{3,0},{4,7},{5,6},{6,5},{7,4},{8,11},{9,10},{10,... | collective-permute-start | bytes 1916936 | tf_op jit(solution)/shard_map/ppermute | solution.py:729
  11.7 0.6 collective-permute-start.1
  12.3 0.0 collective-permute-start
  12.4 27.0 %attend.1 = (bf16[4,512,768]{2,1,0:T(8,128)(2,1)}, bf16[4,512,768]{2,1,0:T(8,128)(2,1)}, bf16[4,512,768]{2,1,0:T(8,128)(2,1)}, bf16[4,512,768]{2,1,0:T(8,128)(2,...) custom-call(bf16[4,512,768]{2,1,0:T(8,128)(2,1)} %bitcast.25, s32[4,1,512]{2,1,0:T(1,128)} %docs_ref.1, ...), custom_call_target="tpu_custom_call" | custom-call | flops 20000000000 | bytes 50000000 | tf_op jit(solution)/shard_map/attend/pallas_call | solution.py:138
  39.4 0.0 copy-start.15
  39.4 0.9 collective-permute-done.1.w2_ref
  40.3 0.0 collective-permute-done.w1_ref
  40.3 0.8 copy-done.16
  41.2 0.2 copy-done.17
  41.4 48.6 %feed.1 = (bf16[4,512,768]{2,1,0:T(8,128)(2,1)}, f32[4,512,768]{2,1,0:T(8,128)}, bf16[4,512,768]{2,1,0:T(8,128)(2,1)}, bf16[2304,128]{1,0:T(8,128)(2,1)}, bf16[2...) custom-call(s32[1]{0:T(128)} %bitcast.me_ref.refs_7_, ...), custom_call_target="tpu_custom_call" | custom-call | flops 40000000000 | bytes 50000000 | tf_op jit(solution)/shard_map/feed/pallas_call | solution.py:342
  90.0 0.1 collective-permute-start.4
  90.1 0.5 collective-permute-start.3
  90.6 3.4 %collective-permute-done.3.cw_ref = bf16[2304,128]{1,0:T(8,128)(2,1)S(1)} collective-permute-done((bf16[2304,128]{1,0:T(8,128)(2,1)}, bf16[2304,128]{1,0:T(8,128)(2,1)S(1)}, u32[]{:S(2)}, u32[]{:S(2)}) %collective-permute-start.3) | collective-permute-done | bytes 589856 | tf_op jit(solution)/shard_map/ppermute | solution.py:729
  93.9 0.0 collective-permute-done.4.ce_ref.refs_1_
  94.0 1.1 copy-done.5
  95.0 1.1 copy-done.6
  96.1 1.0 add_up.6
  97.1 7.6 %all-to-all-start = ((bf16[16,144,128]{2,1,0:T(8,128)(2,1)}), bf16[16,144,128]{2,1,0:T(8,128)(2,1)S(1)}, u32[]{:S(2)}, u32[]{:S(2)}) async-start(bf16[16,144,128]{2,1,0:T(8,128)(2,1)} %bitcast.6), calls=%async_computation | async-start | bytes 1179648 | tf_op jit(solution)/shard_map/all_to_all | solution.py:693
  104.7 0.0 all-gather.3.cloned.1.call-start
  104.8 2.0 collective-permute-start.5
  106.8 18.3 %attend_back.2 = (bf16[4,3,512,384]{3,2,1,0:T(8,128)(2,1)}, bf16[1872,128]{1,0:T(8,128)(2,1)}, f32[8,128]{1,0:T(8,128)}) custom-call(bf16[4,512,768]{2,1,0:T(8,128)(2,1)} %bitcast.27, bf16[4,512,768]{2,1,0:T(8,128)(2,1)} %get-tuple-element.64.refs_1_, bf16[4,512,768]{2,1,0:T(8,128)(2,1)} %get-tuple-element.65.refs_2_, ...), custom_call_target="tpu_custom_call" | custom-call | flops 20000000000 | bytes 30000000 | tf_op jit(solution)/shard_map/attend_back/pallas_call | solution.py:547
  125.1 0.0 copy-start.12
  125.1 0.7 copy-done.12
  125.8 0.7 add_up.7.refs_3_.refs_10_
  126.5 0.0 all-gather.3.cloned.1.call-update
  126.6 1.0 add_up.8.refs_9_
  127.6 5.4 %all-to-all-start.1 = ((bf16[8,288,128]{2,1,0:T(8,128)(2,1)}), bf16[8,288,128]{2,1,0:T(8,128)(2,1)S(1)}, u32[]{:S(2)}, u32[]{:S(2)}) async-start(bf16[8,288,128]{2,1,0:T(8,128)(2,1)} %bitcast.7), calls=%async_computation.1 | async-start | bytes 1179648 | tf_op jit(solution)/shard_map/all_to_all | solution.py:693
  133.0 0.0 copy-start.9
  133.0 0.0 copy-start.10
  133.1 18.8 %attend_back.3 = (bf16[4,3,512,384]{3,2,1,0:T(8,128)(2,1)}, bf16[1920,128]{1,0:T(8,128)(2,1)}, bf16[1920,128]{1,0:T(8,128)(2,1)}, f32[8,128]{1,0:T(8,128)}) custom-call(bf16[4,512,768]{2,1,0:T(8,128)(2,1)} %bitcast.28, bf16[4,512,768]{2,1,0:T(8,128)(2,1)} %get-tuple-element.64.refs_1_, bf16[4,512,768]{2,1,0:T(8,128)(2,1)} %get-tuple-element.65.refs_2_, ...), custom_call_target="tpu_custom_call" | custom-call | flops 20000000000 | bytes 30000000 | tf_op jit(solution)/shard_map/attend_back/pallas_call | solution.py:547
  151.9 0.1 collective-permute-start.6
  151.9 2.1 collective-permute-done.6.refs_1_
  154.0 1.0 copy-done.7
  155.0 0.9 add_up.9.refs_2_.refs_6_
  155.9 0.0 all-to-all-done.1.refs_0_
  155.9 0.7 copy-done.11
  156.6 0.1 add_up.10.refs_0_
  156.7 3.0 %collective-permute-start.8 = (bf16[288,128]{1,0:T(8,128)(2,1)S(1)}, bf16[288,128]{1,0:T(8,128)(2,1)S(1)}, u32[]{:S(2)}, u32[]{:S(2)}) collective-permute-start(bf16[288,128]{1,0:T(8,128)(2,1)S(1)} %add_up.10.refs_0_), channel_id=1, source_target_pairs={{0,16},{4,20},{8,24},{12,28},{16,0},{20,4},{24,8},{28,12},{1,17},{... | collective-permute-start | bytes 221192 | tf_op jit(solution)/shard_map/ppermute | solution.py:756
  159.7 1.5 collective-permute-start.7
  161.1 3.6 %all-to-all-start.2 = ((bf16[16,120,128]{2,1,0:T(8,128)(2,1)}), bf16[16,120,128]{2,1,0:T(8,128)(2,1)S(1)}, u32[]{:S(2)}, u32[]{:S(2)}) async-start(bf16[16,120,128]{2,1,0:T(8,128)(2,1)} %bitcast.12), calls=%async_computation.2 | async-start | bytes 983040 | tf_op jit(solution)/shard_map/all_to_all | solution.py:693
  164.7 1.8 collective-permute-start.10
  166.5 0.0 collective-permute-done.8.refs_7_.refs_1_
  166.5 0.3 collective-permute-start.11
  166.8 1.8 collective-permute-start.9
  168.6 0.0 collective-permute-done.7.refs_6_.refs_2_
  168.6 1.5 collective-permute-start.12
  170.1 2.8 %copy-done = f32[4,512,768]{2,1,0:T(8,128)S(1)} copy-done((f32[4,512,768]{2,1,0:T(8,128)S(1)}, f32[4,512,768]{2,1,0:T(8,128)}, u32[]{:S(2)}) %copy-start) | copy-done | bytes 6291480
  172.9 2.3 %copy-done.1 = bf16[4,3,512,384]{3,2,1,0:T(8,128)(2,1)S(1)} copy-done((bf16[4,3,512,384]{3,2,1,0:T(8,128)(2,1)S(1)}, bf16[4,3,512,384]{3,2,1,0:T(8,128)(2,1)}, u32[]{:S(2)}) %copy-start.1) | copy-done | bytes 4718616
  175.2 2.3 %copy-done.2 = bf16[4,3,512,384]{3,2,1,0:T(8,128)(2,1)S(1)} copy-done((bf16[4,3,512,384]{3,2,1,0:T(8,128)(2,1)S(1)}, bf16[4,3,512,384]{3,2,1,0:T(8,128)(2,1)}, u32[]{:S(2)}) %copy-start.2) | copy-done | bytes 4718616
  177.5 3.4 %input_grad.2 = (bf16[4,512,768]{2,1,0:T(8,128)(2,1)}, f32[8,128]{1,0:T(8,128)}) custom-call(f32[4,512,768]{2,1,0:T(8,128)S(1)} %copy-done, bf16[4,3,512,384]{3,2,1,0:T(8,128)(2,1)S(1)} %copy-done.1, bf16[4,3,512,384]{3,2,1,0:T(8,128)(2,1)S(1)} %copy-done.2, bf16[4,192,192]{2,1,0:T(8,128)(2,1)S(1)} %copy-done.8, bf16[4,192,192]{2,1,0:T(8,128)(2,1)S(1)} %copy-done.9, ...), custom_call_target="tpu_custom_call" | custom-call | flops 5000000000 | bytes 10000000 | tf_op jit(solution)/shard_map/input_grad/pallas_call | solution.py:602
  181.0 0.0 collective-permute-done.9.refs_7_.refs_3_
  181.0 0.7 collective-permute-start.13
  181.7 3.4 %input_grad.3 = (bf16[4,512,768]{2,1,0:T(8,128)(2,1)}, f32[8,128]{1,0:T(8,128)S(1)}) custom-call(f32[4,512,768]{2,1,0:T(8,128)S(1)} %copy-done, bf16[4,3,512,384]{3,2,1,0:T(8,128)(2,1)S(1)} %copy-done.1, bf16[4,3,512,384]{3,2,1,0:T(8,128)(2,1)S(1)} %copy-done.2, bf16[4,192,192]{2,1,0:T(8,128)(2,1)S(1)} %copy-done.8, ...), custom_call_target="tpu_custom_call", output_to_operand_aliasing={{0}: (8, {})} | custom-call | flops 5000000000 | bytes 10000000 | tf_op jit(solution)/shard_map/input_grad/pallas_call | solution.py:602
  185.1 0.7 all-gather.3.cloned.1.call-done
  185.8 0.7 slice_bitcast_fusion.refs_2_
  186.4 0.0 collective-permute-done.10.refs_3_.refs_4_
  186.5 0.1 add_up.11
  186.6 19.4 %all_to_all.20 = bf16[16,120,128]{2,1,0:T(8,128)(2,1)S(1)} all-to-all(bf16[16,120,128]{2,1,0:T(8,128)(2,1)S(1)} %add_up.11), channel_id=1, replica_groups={{0,2,4,6,8,10,12,14,16,18,20,22,24,26,28,30},{1,3,5,7,9,11,13,15,17,19,..., dimensions={0} | all-to-all | bytes 983040 | tf_op jit(solution)/shard_map/all_to_all | solution.py:693
  205.9 0.1 pad_add_fusion.me_ref
  206.0 1.8 collective-permute-done.14.refs_10_
  207.8 1.3 copy-done.3
  209.1 4.0 %unpack.1 = (f32[4,192,192]{2,1,0:T(8,128)}, f32[4,192,192]{2,1,0:T(8,128)}, f32[768,768]{1,0:T(8,128)}, f32[4,192,192]{2,1,0:T(8,128)}, f32[4,192,192]{2,1,0:T(...) custom-call(s32[2]{0:T(128)S(1)} %pad_add_fusion.me_ref, ...), custom_call_target="tpu_custom_call" | custom-call | tf_op jit(solution)/shard_map/unpack/pallas_call | solution.py:679
  (29 shorter events, 0.1 us)
Async XLA Ops:
  9.2 30.1 %copy-start.14 = (bf16[4,208,384]{2,1,0:T(8,128)(2,1)}, bf16[4,208,384]{2,1,0:T(8,128)(2,1)S(1)}, u32[]{:S(2)}) copy-start(bf16[4,208,384]{2,1,0:T(8,128)(2,1)S(1)} %fusion.1.w0_ref) | copy-start | bytes 1916932
  9.2 30.2 %collective-permute-start.2 = (bf16[4,208,384]{2,1,0:T(8,128)(2,1)S(1)}, bf16[4,208,384]{2,1,0:T(8,128)(2,1)S(1)}, u32[]{:S(2)}, u32[]{:S(2)}) collective-permute-start(bf16[4,208,384]{2,1,0:T(8,128)(2,1)S(1)} %fusion.1.w0_ref), channel_id=1, source_target_pairs={{0,3},{1,2},{2,1},{3,0},{4,7},{5,6},{6,5},{7,4},{8,11},{9,10},{10,... | collective-permute-start | bytes 1916936 | tf_op jit(solution)/shard_map/ppermute | solution.py:729
  11.7 28.6 %collective-permute-start.1 = (bf16[4,208,384]{2,1,0:T(8,128)(2,1)S(1)}, bf16[4,208,384]{2,1,0:T(8,128)(2,1)S(1)}, u32[]{:S(2)}, u32[]{:S(2)}) collective-permute-start(bf16[4,208,384]{2,1,0:T(8,128)(2,1)S(1)} %fusion.1.w0_ref), channel_id=1, source_target_pairs={{0,2},{1,3},{2,0},{3,1},{4,6},{5,7},{6,4},{7,5},{8,10},{9,11},{10,... | collective-permute-start | bytes 1916936 | tf_op jit(solution)/shard_map/ppermute | solution.py:729
  12.3 28.0 %collective-permute-start = (bf16[4,208,384]{2,1,0:T(8,128)(2,1)S(1)}, bf16[4,208,384]{2,1,0:T(8,128)(2,1)S(1)}, u32[]{:S(2)}, u32[]{:S(2)}) collective-permute-start(bf16[4,208,384]{2,1,0:T(8,128)(2,1)S(1)} %fusion.1.w0_ref), channel_id=1, source_target_pairs={{0,1},{1,0},{2,3},{3,2},{4,5},{5,4},{6,7},{7,6},{8,9},{9,8},{10,11... | collective-permute-start | bytes 1916936 | tf_op jit(solution)/shard_map/ppermute | solution.py:729
  39.4 0.9 copy-start.15
  40.3 0.8 copy-start.16
  40.3 1.0 copy-start.17
  90.0 4.0 %collective-permute-start.4 = (bf16[4608,128]{1,0:T(8,128)(2,1)}, bf16[4608,128]{1,0:T(8,128)(2,1)S(1)}, u32[]{:S(2)}, u32[]{:S(2)}) collective-permute-start(bf16[4608,128]{1,0:T(8,128)(2,1)} %get-tuple-element.74), channel_id=1, source_target_pairs={{0,1},{1,0},{2,3},{3,2},{4,5},{5,4},{6,7},{7,6},{8,9},{9,8},{10,11... | collective-permute-start | bytes 3538952 | tf_op jit(solution)/shard_map/ppermute | solution.py:729
  90.1 3.9 %collective-permute-start.3 = (bf16[2304,128]{1,0:T(8,128)(2,1)}, bf16[2304,128]{1,0:T(8,128)(2,1)S(1)}, u32[]{:S(2)}, u32[]{:S(2)}) collective-permute-start(bf16[2304,128]{1,0:T(8,128)(2,1)} %get-tuple-element.72), channel_id=1, source_target_pairs={{0,1},{1,0},{2,3},{3,2},{4,5},{5,4},{6,7},{7,6},{8,9},{9,8},{10,11... | collective-permute-start | bytes 1769480 | tf_op jit(solution)/shard_map/ppermute | solution.py:729
  94.0 1.1 copy-start.5
  95.0 1.1 copy-start.6
  97.1 9.7 %copy-start.13 = (bf16[2304,128]{1,0:T(8,128)(2,1)}, bf16[2304,128]{1,0:T(8,128)(2,1)S(1)}, u32[]{:S(2)}) copy-start(bf16[2304,128]{1,0:T(8,128)(2,1)S(1)} %get-tuple-element.75.refs_10_) | copy-start | bytes 1769476
  97.1 28.0 %all-to-all-start = ((bf16[16,144,128]{2,1,0:T(8,128)(2,1)}), bf16[16,144,128]{2,1,0:T(8,128)(2,1)S(1)}, u32[]{:S(2)}, u32[]{:S(2)}) async-start(bf16[16,144,128]{2,1,0:T(8,128)(2,1)} %bitcast.6), calls=%async_computation | async-start | bytes 1179648 | tf_op jit(solution)/shard_map/all_to_all | solution.py:693
  104.7 81.0 %all-gather.3.cloned.1.call-start = ((), (), s32[]{:S(2)}) async-start(), calls=%async_computation.4 | async-start | bytes 1216512 | tf_op jit(solution)/shard_map/all_gather | solution.py:749
  104.8 21.7 %collective-permute-start.5 = (bf16[2304,128]{1,0:T(8,128)(2,1)S(1)}, bf16[2304,128]{1,0:T(8,128)(2,1)S(1)}, u32[]{:S(2)}, u32[]{:S(2)}) collective-permute-start(bf16[2304,128]{1,0:T(8,128)(2,1)S(1)} %get-tuple-element.75.refs_10_), channel_id=1, source_target_pairs={{0,2},{1,3},{2,0},{3,1},{4,6},{5,7},{6,4},{7,5},{8,10},{9,11},{10,... | collective-permute-start | bytes 1769480 | tf_op jit(solution)/shard_map/ppermute | solution.py:729
  106.8 19.8 %copy-start.4 = (bf16[2304,128]{1,0:T(8,128)(2,1)S(1)}, bf16[2304,128]{1,0:T(8,128)(2,1)}, u32[]{:S(2)}) copy-start(bf16[2304,128]{1,0:T(8,128)(2,1)} %get-tuple-element.79.refs_0_) | copy-start | bytes 1769476
  125.1 0.7 copy-start.12
  127.6 28.4 %all-to-all-start.1 = ((bf16[8,288,128]{2,1,0:T(8,128)(2,1)}), bf16[8,288,128]{2,1,0:T(8,128)(2,1)S(1)}, u32[]{:S(2)}, u32[]{:S(2)}) async-start(bf16[8,288,128]{2,1,0:T(8,128)(2,1)} %bitcast.7), calls=%async_computation.1 | async-start | bytes 1179648 | tf_op jit(solution)/shard_map/all_to_all | solution.py:693
  133.0 37.0 %copy-start.8 = (bf16[4,192,192]{2,1,0:T(8,128)(2,1)S(1)}, bf16[4,192,192]{2,1,0:T(8,128)(2,1)}, u32[]{:S(2)}) copy-start(bf16[4,192,192]{2,1,0:T(8,128)(2,1)} %refs_3_.3) | copy-start | bytes 884740
  133.0 37.0 %copy-start.9 = (bf16[4,192,192]{2,1,0:T(8,128)(2,1)S(1)}, bf16[4,192,192]{2,1,0:T(8,128)(2,1)}, u32[]{:S(2)}) copy-start(bf16[4,192,192]{2,1,0:T(8,128)(2,1)} %refs_4_.3) | copy-start | bytes 884740
  133.0 37.0 %copy-start.10 = (bf16[4,192,192]{2,1,0:T(8,128)(2,1)S(1)}, bf16[4,192,192]{2,1,0:T(8,128)(2,1)}, u32[]{:S(2)}) copy-start(bf16[4,192,192]{2,1,0:T(8,128)(2,1)} %refs_5_.3) | copy-start | bytes 884740
  151.9 2.1 collective-permute-start.6
  154.0 1.0 copy-start.7
  155.9 0.7 copy-start.11
  156.7 9.8 %collective-permute-start.8 = (bf16[288,128]{1,0:T(8,128)(2,1)S(1)}, bf16[288,128]{1,0:T(8,128)(2,1)S(1)}, u32[]{:S(2)}, u32[]{:S(2)}) collective-permute-start(bf16[288,128]{1,0:T(8,128)(2,1)S(1)} %add_up.10.refs_0_), channel_id=1, source_target_pairs={{0,16},{4,20},{8,24},{12,28},{16,0},{20,4},{24,8},{28,12},{1,17},{... | collective-permute-start | bytes 221192 | tf_op jit(solution)/shard_map/ppermute | solution.py:756
  159.7 8.9 %collective-permute-start.7 = (bf16[288,128]{1,0:T(8,128)(2,1)S(1)}, bf16[288,128]{1,0:T(8,128)(2,1)S(1)}, u32[]{:S(2)}, u32[]{:S(2)}) collective-permute-start(bf16[288,128]{1,0:T(8,128)(2,1)S(1)} %add_up.10.refs_0_), channel_id=1, source_target_pairs={{0,8},{4,12},{8,0},{12,4},{16,24},{20,28},{24,16},{28,20},{1,9},{5... | collective-permute-start | bytes 221192 | tf_op jit(solution)/shard_map/ppermute | solution.py:756
  161.1 25.3 %all-to-all-start.2 = ((bf16[16,120,128]{2,1,0:T(8,128)(2,1)}), bf16[16,120,128]{2,1,0:T(8,128)(2,1)S(1)}, u32[]{:S(2)}, u32[]{:S(2)}) async-start(bf16[16,120,128]{2,1,0:T(8,128)(2,1)} %bitcast.12), calls=%async_computation.2 | async-start | bytes 983040 | tf_op jit(solution)/shard_map/all_to_all | solution.py:693
  164.7 21.7 %collective-permute-start.10 = (bf16[288,128]{1,0:T(8,128)(2,1)S(1)}, bf16[288,128]{1,0:T(8,128)(2,1)S(1)}, u32[]{:S(2)}, u32[]{:S(2)}) collective-permute-start(bf16[288,128]{1,0:T(8,128)(2,1)S(1)} %add_up.10.refs_0_), channel_id=1, source_target_pairs={{0,4},{4,0},{8,12},{12,8},{16,20},{20,16},{24,28},{28,24},{1,5},{5... | collective-permute-start | bytes 221192 | tf_op jit(solution)/shard_map/ppermute | solution.py:756
  166.5 19.9 %collective-permute-start.11 = (bf16[288,128]{1,0:T(8,128)(2,1)S(1)}, bf16[288,128]{1,0:T(8,128)(2,1)S(1)}, u32[]{:S(2)}, u32[]{:S(2)}) collective-permute-start(bf16[288,128]{1,0:T(8,128)(2,1)S(1)} %collective-permute-done.8.refs_7_.refs_1_), channel_id=1, source_target_pairs={{0,4},{4,0},{8,12},{12,8},{16,20},{20,16},{24,28},{28,24},{1,5},{5... | collective-permute-start | bytes 221192 | tf_op jit(solution)/shard_map/ppermute | solution.py:756
  166.8 14.2 %collective-permute-start.9 = (bf16[288,128]{1,0:T(8,128)(2,1)S(1)}, bf16[288,128]{1,0:T(8,128)(2,1)S(1)}, u32[]{:S(2)}, u32[]{:S(2)}) collective-permute-start(bf16[288,128]{1,0:T(8,128)(2,1)S(1)} %collective-permute-done.8.refs_7_.refs_1_), channel_id=1, source_target_pairs={{0,8},{4,12},{8,0},{12,4},{16,24},{20,28},{24,16},{28,20},{1,9},{5... | collective-permute-start | bytes 221192 | tf_op jit(solution)/shard_map/ppermute | solution.py:756
  168.6 17.9 %collective-permute-start.12 = (bf16[288,128]{1,0:T(8,128)(2,1)S(1)}, bf16[288,128]{1,0:T(8,128)(2,1)S(1)}, u32[]{:S(2)}, u32[]{:S(2)}) collective-permute-start(bf16[288,128]{1,0:T(8,128)(2,1)S(1)} %collective-permute-done.7.refs_6_.refs_2_), channel_id=1, source_target_pairs={{0,4},{4,0},{8,12},{12,8},{16,20},{20,16},{24,28},{28,24},{1,5},{5... | collective-permute-start | bytes 221192 | tf_op jit(solution)/shard_map/ppermute | solution.py:756
  170.1 2.8 %copy-start = (f32[4,512,768]{2,1,0:T(8,128)S(1)}, f32[4,512,768]{2,1,0:T(8,128)}, u32[]{:S(2)}) copy-start(f32[4,512,768]{2,1,0:T(8,128)} %get-tuple-element.63.refs_0_) | copy-start | bytes 18874372
  172.9 2.3 %copy-start.1 = (bf16[4,3,512,384]{3,2,1,0:T(8,128)(2,1)S(1)}, bf16[4,3,512,384]{3,2,1,0:T(8,128)(2,1)}, u32[]{:S(2)}) copy-start(bf16[4,3,512,384]{3,2,1,0:T(8,128)(2,1)} %get-tuple-element.77.refs_1_) | copy-start | bytes 14155780
  175.2 2.3 %copy-start.2 = (bf16[4,3,512,384]{3,2,1,0:T(8,128)(2,1)S(1)}, bf16[4,3,512,384]{3,2,1,0:T(8,128)(2,1)}, u32[]{:S(2)}) copy-start(bf16[4,3,512,384]{3,2,1,0:T(8,128)(2,1)} %get-tuple-element.81.refs_2_) | copy-start | bytes 14155780
  181.0 5.5 %collective-permute-start.13 = (bf16[288,128]{1,0:T(8,128)(2,1)S(1)}, bf16[288,128]{1,0:T(8,128)(2,1)S(1)}, u32[]{:S(2)}, u32[]{:S(2)}) collective-permute-start(bf16[288,128]{1,0:T(8,128)(2,1)S(1)} %collective-permute-done.9.refs_7_.refs_3_), channel_id=1, source_target_pairs={{0,4},{4,0},{8,12},{12,8},{16,20},{20,16},{24,28},{28,24},{1,5},{5... | collective-permute-start | bytes 221192 | tf_op jit(solution)/shard_map/ppermute | solution.py:756
  205.9 1.9 collective-permute-start.14
  207.8 1.3 copy-start.3
Sparse Core Ops, SparseCore 0:
  126.7 59.0 all-gather.2
